TPU v7x, 32 devices: a whole 2x2x4 slice. The times are simulated.
32 devices in a mesh: shape: 8 (over z, y), oct: 4 (over x, core).
Axes of the slice: x: 2, y: 2, z: 4, core: 2. Of those that a mesh axis runs over, the one named last changes fastest.
Arguments:
- point_inputs: bfloat16 [131072, 256], P(('shape', 'oct')), may hold values from -6 to 6
- shape_ids: int32 [131072], P(('shape', 'oct')), may hold values from 0 to 15, as said below
- octants: int32 [131072, 1], P(('shape', 'oct')), may hold values from 0 to 3; in each aligned block of 4096 rows (0 to 4095, 4096 to 8191, ...) at most 2048 rows name the same one
- categories: int32 [16], replicated, may hold values from 0 to 4, as said below
- codes: bfloat16 [16, 256], P('shape'), may hold values from -6 to 6
- direction: float32 [512, 512], replicated, may hold values from -0.25 to 0.25
- gain: float32 [512], replicated, may hold values from 0.5 to 1.5
- bias: float32 [512], replicated, may hold values from -3 to 3
- cotangent: bfloat16 [262144, 512], P(('shape', 'oct')), may hold values from -6 to 6
- prev_mean: float32 [5, 256], replicated, may hold values from -5 to 5
- prev_var: float32 [5, 256], replicated, may hold values from 0.5 to 2
- momentum: float32 [5], replicated, may hold values from 0.2 to 0.8
Outputs:
- layer_out: bfloat16 [262144, 512], P(('shape', 'oct'))
- input_grad: bfloat16 [131072, 256], P(('shape', 'oct'))
- code_grad: float32 [16, 256], P('shape')
- direction_grad: float32 [512, 512], replicated
- gain_grad: float32 [512], replicated
- bias_grad: float32 [512], replicated
- running_mean: float32 [5, 256], replicated
- running_var: float32 [5, 256], replicated
Inputs may be any that keep to these rules, and one draw needn't show every extreme that they name: `shape_ids`: the points on the devices of index s along shape belong to shapes s * 2 to (s + 1) * 2 - 1, and every shape has points on every device of its index. `octants`: in the rows of one device no octant is named by more than 2048 points. `categories`: every category holds at least one shape.
All inputs are finite; a program needn't handle non-finite values.
Results may differ from a plain program's by a relative error of at most 0.0059.
Values may be sent and summed in bfloat16 or wider, within the bound.
No kernel may reach another device: no remote copies, remote signals or barrier semaphores. Data moves between devices by JAX's collectives and lax.ppermute only.
A program may use at most 128 MiB of HBM per device.

v0:
```python
import jax
import jax.numpy as jnp
from jax import lax
from jax.sharding import PartitionSpec as P

HID = 253
CATS = 5


norm_eps = 1e-06


def forward_rows(point_rows, local_ids, w_point, code_proj, bias):
    shape_count = code_proj.shape[0]
    select = (local_ids[:, None] == jnp.arange(shape_count, dtype=jnp.int32)[None, :]).astype(
        jnp.float32
    )
    pre_act = jnp.dot(point_rows, w_point, preferred_element_type=jnp.float32)
    pre_act = pre_act + jnp.dot(select, code_proj, precision=lax.Precision.HIGHEST) + bias[None, :]
    valid = (local_ids >= 0)[:, None]
    outputs = jnp.where(valid, jax.nn.softplus(pre_act), 0.0).astype(jnp.bfloat16)
    return (pre_act, outputs)


def backward_rows(point_rows, local_ids, pre_act, upstream, codes, w_point, w_code):
    shape_count = codes.shape[0]
    valid = (local_ids >= 0)[:, None]
    grad_pre = jnp.where(valid, upstream.astype(jnp.float32) * jax.nn.sigmoid(pre_act), 0.0).astype(
        jnp.bfloat16
    )
    grad_bias = jnp.sum(grad_pre.astype(jnp.float32), axis=0)
    grad_point_w = jnp.einsum("rp,ro->po", point_rows, grad_pre, preferred_element_type=jnp.float32)
    select = (local_ids[:, None] == jnp.arange(shape_count, dtype=jnp.int32)[None, :]).astype(
        jnp.bfloat16
    )
    per_shape = jnp.einsum("rs,ro->so", select, grad_pre, preferred_element_type=jnp.float32)
    grad_code_w = jnp.dot(codes.astype(jnp.float32).T, per_shape, precision=lax.Precision.HIGHEST)
    code_part = jnp.dot(per_shape, w_code.astype(jnp.float32).T, precision=lax.Precision.HIGHEST)
    grad_rows = jnp.einsum(
        "ro,po->rp", grad_pre, w_point, preferred_element_type=jnp.float32
    ).astype(jnp.bfloat16)
    hidden_width = HID
    grad_weight = jnp.concatenate(
        [grad_point_w[:hidden_width], grad_code_w, grad_point_w[hidden_width:]], axis=0
    )
    return (grad_weight, grad_bias, code_part, grad_rows)


def norm_backward(grad_weight, direction, gain, norms):
    dots = jnp.sum(grad_weight * direction, axis=0)
    gain_grad = dots / norms
    direction_grad = (gain / norms)[None, :] * (
        grad_weight - direction * (dots / (norms * norms))[None, :]
    )
    return (direction_grad, gain_grad)


def body(
    point_inputs,
    shape_ids,
    octants,
    categories,
    codes,
    direction,
    gain,
    bias,
    cotangent,
    prev_mean,
    prev_var,
    momentum,
):
    point_count = point_inputs.shape[0]
    point_width = point_inputs.shape[1]
    oct_count = lax.axis_size("oct")
    capacity = 2 * point_count // oct_count
    shape_count = codes.shape[0]
    hidden_width = HID
    code_width = codes.shape[1]
    base = lax.axis_index("shape") * shape_count
    local_ids = shape_ids - base
    octant_col = octants[:, 0]
    onehot = (octant_col[:, None] == jnp.arange(oct_count, dtype=jnp.int32)[None, :]).astype(
        jnp.int32
    )
    ranks = jnp.sum((jnp.cumsum(onehot, axis=0) - onehot) * onehot, axis=1)
    slots = octant_col * capacity + ranks
    norms = jnp.sqrt(jnp.sum(direction * direction, axis=0) + norm_eps)
    weight = (direction * (gain / norms)[None, :]).astype(jnp.bfloat16)
    w_point = jnp.concatenate([weight[:hidden_width], weight[hidden_width + code_width :]], axis=0)
    w_code = weight[hidden_width : hidden_width + code_width]
    code_proj = jnp.dot(codes, w_code, preferred_element_type=jnp.float32)
    counts = jnp.sum(
        (local_ids[:, None] == jnp.arange(shape_count, dtype=jnp.int32)[None, :]).astype(
            jnp.float32
        ),
        axis=0,
    )
    my_cats = lax.dynamic_slice_in_dim(categories, base, shape_count)
    cat_select = (my_cats[:, None] == jnp.arange(CATS, dtype=jnp.int32)[None, :]).astype(
        jnp.float32
    )
    codes_f = codes.astype(jnp.float32)
    code_sums = jnp.sum(cat_select[:, :, None] * (counts[:, None] * codes_f)[:, None, :], axis=0)
    code_squares = jnp.sum(
        cat_select[:, :, None] * (counts[:, None] * codes_f * codes_f)[:, None, :], axis=0
    )
    cat_counts = jnp.sum(cat_select * counts[:, None], axis=0)
    send_rows = (
        jnp.zeros((oct_count * capacity, point_width), jnp.bfloat16).at[slots].set(point_inputs)
    )
    send_ids = jnp.full((oct_count * capacity,), -1, jnp.int32).at[slots].set(local_ids)
    recv_rows, recv_ids = (
        lax.all_to_all(
            send_rows.reshape(oct_count, capacity, point_width),
            "oct",
            split_axis=0,
            concat_axis=0,
            tiled=True,
        ),
        lax.all_to_all(
            send_ids.reshape(oct_count, capacity), "oct", split_axis=0, concat_axis=0, tiled=True
        ),
    )
    bucket_rows = recv_rows.reshape(oct_count * capacity, point_width)
    bucket_ids = recv_ids.reshape(oct_count * capacity)
    pre_act, layer_out = forward_rows(bucket_rows, bucket_ids, w_point, code_proj, bias)
    grad_weight, grad_bias, code_part, grad_rows = backward_rows(
        bucket_rows, bucket_ids, pre_act, cotangent, codes, w_point, w_code
    )
    returned = lax.all_to_all(
        grad_rows.reshape(oct_count, capacity, point_width),
        "oct",
        split_axis=0,
        concat_axis=0,
        tiled=True,
    )
    input_grad = returned.reshape(oct_count * capacity, point_width)[slots]
    code_grad = lax.psum(code_part, "oct")
    grad_weight, grad_bias, code_sums, code_squares, cat_counts = lax.psum(
        (grad_weight, grad_bias, code_sums, code_squares, cat_counts), ("shape", "oct")
    )
    direction_grad, gain_grad = norm_backward(grad_weight, direction, gain, norms)
    batch_mean = code_sums / cat_counts[:, None]
    batch_var = code_squares / cat_counts[:, None] - batch_mean * batch_mean
    rate = momentum[:, None]
    running_mean = (1.0 - rate) * prev_mean + rate * batch_mean
    running_var = (1.0 - rate) * prev_var + rate * batch_var
    return (
        layer_out,
        input_grad,
        code_grad,
        direction_grad,
        gain_grad,
        grad_bias,
        running_mean,
        running_var,
    )


def solution(mesh):
    in_specs = (
        P(("shape", "oct"), None),
        P(("shape", "oct")),
        P(("shape", "oct"), None),
        P(),
        P("shape", None),
        P(),
        P(),
        P(),
        P(("shape", "oct"), None),
        P(),
        P(),
        P(),
    )
    out_specs = (
        P(("shape", "oct"), None),
        P(("shape", "oct"), None),
        P("shape", None),
        P(),
        P(),
        P(),
        P(),
        P(),
    )
    return jax.shard_map(body, mesh=mesh, in_specs=in_specs, out_specs=out_specs, check_vma=False)
```

profile of v0, /device:TPU:0, one launch (start us, length us, event | category | flops | bytes accessed | tf_op | source)
XLA Modules:
  0.0 321.8 jit_solution(11269139200141950825)
XLA Ops:
  7.2 0.8 fusion.13
  8.0 1.1 reduce-window.6
  9.2 0.2 slice_reduce_fusion
  9.4 0.2 reduce-window.9
  9.6 0.1 add_bitcast_fusion
  9.7 0.8 fusion.11
  10.5 0.7 compare_select_fusion.1
  11.3 0.7 broadcast_subtract_fusion
  12.0 16.1 %scatter_custom_fusion = s32[8192]{0:T(1024)} fusion(s32[4096]{0:T(1024)S(1)} %bitcast.50, s32[4096]{0:T(1024)S(1)} %broadcast_subtract_fusion, s32[]{:T(128)} %constant.12.clone.1), kind=kCustom, calls=%fused_computation.41 | custom fusion | bytes 32772 | tf_op jit(solution)/shard_map/scatter | solution.py:111
  28.1 4.2 %all-to-all-start = ((s32[4,1,2048]{2,1,0:T(1,128)}), s32[4,1,2048]{2,1,0:T(1,128)S(1)}, u32[]{:S(2)}, u32[]{:S(2)}) async-start(s32[4,1,2048]{2,1,0:T(1,128)} %bitcast.5), calls=%async_computation | async-start | bytes 65536 | tf_op jit(solution)/shard_map/all_to_all | solution.py:120
  32.3 20.9 %scatter_custom_fusion.1 = bf16[8192,256]{1,0:T(8,128)(2,1)} fusion(s32[4096]{0:T(1024)S(1)} %bitcast.51, bf16[4096,256]{1,0:T(8,128)(2,1)} %param.12, bf16[]{:T(256)} %constant.9.clone.1), kind=kCustom, calls=%fused_computation.10 | custom fusion | bytes 4194816 | tf_op jit(solution)/shard_map/scatter | solution.py:109
  53.2 0.0 all-to-all-done
  53.2 5.0 %all-to-all-start.1 = ((bf16[4,2048,256]{2,1,0:T(8,128)(2,1)}), bf16[4,2048,256]{2,1,0:T(8,128)(2,1)}, u32[]{:S(2)}, u32[]{:S(2)}) async-start(bf16[4,2048,256]{2,1,0:T(8,128)(2,1)} %bitcast.42), calls=%async_computation.1 | async-start | bytes 8388608 | tf_op jit(solution)/shard_map/all_to_all | solution.py:113
  58.3 0.0 copy-done.2
  58.3 0.1 multiply_reduce_fusion.1
  58.4 0.1 multiply_convert_fusion
  58.6 0.1 dynamic_slice.3
  58.7 0.1 fusion.21
  58.8 0.1 copy.20
  58.9 0.1 fusion.14
  59.0 0.1 convert_multiply_fusion.1
  59.1 0.2 fusion.6
  59.3 47.2 %all-to-all-done.1 = bf16[4,2048,256]{2,1,0:T(8,128)(2,1)} async-done(((bf16[4,2048,256]{2,1,0:T(8,128)(2,1)}), bf16[4,2048,256]{2,1,0:T(8,128)(2,1)}, u32[]{:S(2)}, u32[]{:S(2)}) %all-to-all-start.1) | async-done | bytes 4194336 | tf_op jit(solution)/shard_map/all_to_all | solution.py:113
  106.5 4.5 %fusion.8 = f32[8192,512]{1,0:T(8,128)S(1)} fusion(bf16[8192,256]{1,0:T(8,128)(2,1)} %bitcast.8, bf16[3,512]{1,0:T(4,128)(2,1)S(1)} %slice.32, bf16[253,512]{1,0:T(8,128)(2,1)S(1)} %slice.31), kind=kOutput, calls=%fused_computation.23 | convolution fusion | flops 2148007936 | bytes 21233664 | tf_op jit(solution)/shard_map/dot_general | solution.py:18
  111.1 26.1 %convert_reduce_fusion = (f32[512]{0:T(512)S(1)}, bf16[8192,512]{1,0:T(8,128)(2,1)S(1)}, bf16[8192,512]{1,0:T(8,128)(2,1)}) fusion(bf16[8192,512]{1,0:T(8,128)(2,1)} %param.20, pred[8192]{0:T(1024)(128)(4,1)S(1)} %broadcast_compare_fusion, f32[512]{0:T(512)S(1)} %copy-done.8, f32[8192,512]{1,0:T(8,128)S(1)} %fusion.8, f32[512,2]{0,1:T(2,128)S(1)} %fusion.6, ...), kind=kOutput, calls=%fused_computation.6 | convolution fusion | flops 180370944 | bytes 41992192 | tf_op jit(solution)/shard_map/dot_general | solution.py:19
  137.2 3.2 %copy-done = bf16[8192,512]{1,0:T(8,128)(2,1)} copy-done((bf16[8192,512]{1,0:T(8,128)(2,1)}, bf16[8192,512]{1,0:T(8,128)(2,1)S(1)}, u32[]{:S(2)}) %copy-start) | copy-done | bytes 8388632
  140.4 4.3 %convolution_convert_fusion = bf16[8192,256]{1,0:T(8,128)(2,1)} fusion(bf16[8192,512]{1,0:T(8,128)(2,1)S(1)} %get-tuple-element.15, bf16[3,512]{1,0:T(4,128)(2,1)S(1)} %slice.32, bf16[253,512]{1,0:T(8,128)(2,1)S(1)} %slice.31), kind=kOutput, calls=%fused_computation.9 | convolution fusion | flops 2150105088 | bytes 12845056 | tf_op jit(solution)/shard_map/ro,po->rp/dot_general | solution.py:39
  144.7 4.9 %all-to-all-start.2 = ((bf16[4,2048,256]{2,1,0:T(8,128)(2,1)}), bf16[4,2048,256]{2,1,0:T(8,128)(2,1)}, u32[]{:S(2)}, u32[]{:S(2)}) async-start(bf16[4,2048,256]{2,1,0:T(8,128)(2,1)} %bitcast.43), calls=%async_computation.2 | async-start | bytes 8388608 | tf_op jit(solution)/shard_map/all_to_all | solution.py:130
  149.7 0.0 all-reduce.3.cloned.1.call-start
  149.7 0.1 select_reduce_fusion
  149.8 7.1 %fusion.24 = f32[256,512]{1,0:T(8,128)S(1)} fusion(bf16[8192,256]{1,0:T(8,128)(2,1)} %bitcast.8, bf16[8192,512]{1,0:T(8,128)(2,1)} %copy-done), kind=kOutput, calls=%fused_computation.62 | convolution fusion | flops 2147483648 | bytes 13107200 | tf_op jit(solution)/shard_map/rp,ro->po/dot_general | solution.py:32
  157.0 0.0 copy-start.3
  157.0 0.0 copy-start.4
  157.0 1.2 fusion.12
  158.2 0.4 convolution_bitcast_fusion
  158.6 1.1 pad_maximum_fusion
  159.7 0.0 all-reduce.3.cloned.1.call-update
  159.7 0.1 multiply_reduce_fusion.2
  159.8 76.1 %all-reduce = (f32[512]{0:T(512)}, f32[5,256]{1,0:T(8,128)S(1)}, f32[5]{0:T(128)S(1)}, f32[5,256]{1,0:T(8,128)S(1)}) all-reduce(f32[512]{0:T(512)S(1)} %get-tuple-element.14, f32[5,256]{1,0:T(8,128)S(1)} %get-tuple-element.9, f32[5]{0:T(128)S(1)} %select_reduce_fusion, ...), channel_id=1, replica_groups=mesh['shape'=8,'oct'=4] {'shape','oct'}, use_global_device_ids=true, to_apply=%region_10.11 | all-reduce | flops 3077 | bytes 24616 | tf_op jit(solution)/shard_map/psum | solution.py:139
  235.9 0.3 fusion.4
  236.2 6.6 %psum.42 = f32[2,256]{1,0:T(2,128)} all-reduce(f32[2,256]{1,0:T(2,128)S(1)} %fusion.4), channel_id=1, replica_groups=mesh['shape'=8,'oct'=4] {'oct'}, use_global_device_ids=true, to_apply=%region_6.7 | all-reduce | flops 512 | bytes 4096 | tf_op jit(solution)/shard_map/psum | solution.py:138
  242.9 0.7 multiply_add_fusion
  243.5 48.4 %all-reduce.3.cloned.1.call-done = f32[512,512]{1,0:T(8,128)} async-done(((f32[512,512]{1,0:T(8,128)}), f32[512,512]{1,0:T(8,128)}) %all-reduce.3.cloned.1.call-update) | async-done | bytes 1048592 | tf_op jit(solution)/shard_map/psum | solution.py:139
  291.9 1.4 multiply_reduce_fusion
  293.3 0.6 fusion.19
  293.9 2.4 subtract_multiply_fusion
  296.3 0.0 all-to-all-done.2
  296.3 18.7 %gather_fusion = bf16[4096,256]{1,0:T(8,128)(2,1)} fusion(bf16[8192,256]{1,0:T(8,128)(2,1)} %bitcast.10, s32[4096]{0:T(1024)S(1)} %broadcast_clamp_fusion), kind=kCustom, calls=%fused_computation | custom fusion | bytes 4210688 | tf_op jit(solution)/shard_map/gather | solution.py:137
  (23 shorter events, 0.1 us)
Async XLA Ops:
  7.2 51.1 %copy-start.2 = (f32[512,512]{1,0:T(8,128)S(1)}, f32[512,512]{1,0:T(8,128)}, u32[]{:S(2)}) copy-start(f32[512,512]{1,0:T(8,128)} %param.17) | copy-start | bytes 3145732
  7.2 51.2 %copy-start.6 = (f32[512]{0:T(512)S(1)}, f32[512]{0:T(512)}, u32[]{:S(2)}) copy-start(f32[512]{0:T(512)} %param.18) | copy-start | bytes 6148
  7.2 51.4 %copy-start.9 = (s32[16]{0:T(128)S(1)}, s32[16]{0:T(128)}, u32[]{:S(2)}) copy-start(s32[16]{0:T(128)} %param.15) | copy-start | bytes 196
  7.2 51.8 %copy-start.7 = (f32[5]{0:T(128)S(1)}, f32[5]{0:T(128)}, u32[]{:S(2)}) copy-start(f32[5]{0:T(128)} %param.23) | copy-start | bytes 64
  7.2 51.8 %copy-start.5 = (bf16[2,256]{1,0:T(2,128)(2,1)S(1)}, bf16[2,256]{1,0:T(2,128)(2,1)}, u32[]{:S(2)}) copy-start(bf16[2,256]{1,0:T(2,128)(2,1)} %param.16) | copy-start | bytes 3076
  28.1 25.1 %all-to-all-start = ((s32[4,1,2048]{2,1,0:T(1,128)}), s32[4,1,2048]{2,1,0:T(1,128)S(1)}, u32[]{:S(2)}, u32[]{:S(2)}) async-start(s32[4,1,2048]{2,1,0:T(1,128)} %bitcast.5), calls=%async_computation | async-start | bytes 65536 | tf_op jit(solution)/shard_map/all_to_all | solution.py:120
  53.2 53.3 %all-to-all-start.1 = ((bf16[4,2048,256]{2,1,0:T(8,128)(2,1)}), bf16[4,2048,256]{2,1,0:T(8,128)(2,1)}, u32[]{:S(2)}, u32[]{:S(2)}) async-start(bf16[4,2048,256]{2,1,0:T(8,128)(2,1)} %bitcast.42), calls=%async_computation.1 | async-start | bytes 8388608 | tf_op jit(solution)/shard_map/all_to_all | solution.py:113
  106.5 4.5 %copy-start.8 = (f32[512]{0:T(512)S(1)}, f32[512]{0:T(512)}, u32[]{:S(2)}) copy-start(f32[512]{0:T(512)} %param.19) | copy-start | bytes 6148
  137.2 3.2 %copy-start = (bf16[8192,512]{1,0:T(8,128)(2,1)}, bf16[8192,512]{1,0:T(8,128)(2,1)S(1)}, u32[]{:S(2)}) copy-start(bf16[8192,512]{1,0:T(8,128)(2,1)S(1)} %get-tuple-element.15) | copy-start | bytes 25165828
  144.7 151.6 %all-to-all-start.2 = ((bf16[4,2048,256]{2,1,0:T(8,128)(2,1)}), bf16[4,2048,256]{2,1,0:T(8,128)(2,1)}, u32[]{:S(2)}, u32[]{:S(2)}) async-start(bf16[4,2048,256]{2,1,0:T(8,128)(2,1)} %bitcast.43), calls=%async_computation.2 | async-start | bytes 8388608 | tf_op jit(solution)/shard_map/all_to_all | solution.py:130
  149.7 142.3 %all-reduce.3.cloned.1.call-start = ((), (), s32[]{:S(2)}) async-start(), calls=%async_computation.3 | async-start | bytes 2097152 | tf_op jit(solution)/shard_map/psum | solution.py:139
  149.8 7.2 %copy-start.1 = (bf16[8192,512]{1,0:T(8,128)(2,1)S(1)}, bf16[8192,512]{1,0:T(8,128)(2,1)}, u32[]{:S(2)}) copy-start(bf16[8192,512]{1,0:T(8,128)(2,1)} %copy-done) | copy-start | bytes 25165828
  157.0 85.9 %copy-start.3 = (f32[5,256]{1,0:T(8,128)S(1)}, f32[5,256]{1,0:T(8,128)}, u32[]{:S(2)}) copy-start(f32[5,256]{1,0:T(8,128)} %param.22) | copy-start | bytes 15364
  157.0 85.9 %copy-start.4 = (f32[5,256]{1,0:T(8,128)S(1)}, f32[5,256]{1,0:T(8,128)}, u32[]{:S(2)}) copy-start(f32[5,256]{1,0:T(8,128)} %param.21) | copy-start | bytes 15364
Sparse Core Ops, SparseCore 0:
  159.8 132.0 all-reduce.2
where the time goes:
time: 323 us; the launch traced here: 322 us
  waiting for transfers between devices  95.6 us (30%)
  blocking collectives  82.7 us (26%)
  local copies, waits for them, and re-layouts  59.4 us (18%)
  matrix products  44.2 us (14%)
  between operations  14.3 us (4%)
  starting transfers between devices  14.2 us (4%)
  other arithmetic  11.4 us (4%)
    psum x1, blocking collectives, body(): lax.psum((grad_weight, grad_bias, code_sums, code_squares, cat_counts), (...  76.1 us
    psum x1, waiting for transfers between devices, body(): lax.psum((grad_weight, grad_bias, code_sums, code_squares, cat_counts), (...  48.4 us
    all_to_all x1, waiting for transfers between devices, body(): lax.all_to_all(send_rows.reshape(oct_count, capacity, point_width), 'oct'...  47.2 us
    dot_general x1, matrix products, forward_rows(): jnp.dot(select, code_proj, precision=lax.Precision.HIGHEST)  26.1 us
    scatter x1, local copies, waits for them, and re-layouts, body(): jnp.zeros((oct_count * capacity, point_width), jnp.bfloat16).at[slots]  20.9 us
    gather x1, local copies, waits for them, and re-layouts, body(): input_grad = returned.reshape(oct_count * capacity, point_width)[slots]  18.7 us
    scatter x1, local copies, waits for them, and re-layouts, body(): jnp.full((oct_count * capacity,), -1, jnp.int32).at[slots].set(local_ids)  16.1 us
    dot_general x1, matrix products, backward_rows(): jnp.einsum('rp,ro->po', point_rows, grad_pre, preferred_element_type=jnp....  7.13 us
  transfers between devices with their start and end apart: 4, of which 2 were waited for; matrix products, arithmetic and copies ran while one was open for 12% of the time, Pallas kernels for 0%

commit v1 on v0

v1 whole, which is shorter than its diff:
```python
import functools

import jax
import jax.numpy as jnp
from jax import lax
from jax.experimental import pallas as pl
from jax.experimental.pallas import tpu as pltpu
from jax.sharding import PartitionSpec as P

HID = 253
CATS = 5
BLOCK = 256
TILE = 256
CHUNK = 2
WIN = BLOCK + 16
LEAD = 4
USUAL = 7
STEPS = 11
FAR = 1 << 20

norm_eps = 1e-06
CHEAP = pl.CostEstimate(flops=1, bytes_accessed=1, transcendentals=0)


def cost(us):
    return pl.CostEstimate(flops=us * 10**9, bytes_accessed=1, transcendentals=0)


f32, bf16, i32 = jnp.float32, jnp.bfloat16, jnp.int32


def params(mib):
    return pltpu.CompilerParams(vmem_limit_bytes=mib * 1024 * 1024)


def keep(x):
    return pltpu.with_memory_space_constraint(x, pltpu.VMEM)


def stay(x):
    return pltpu.with_memory_space_constraint(x, pltpu.HBM)


def specs(text):
    kinds = {"v": pltpu.VMEM, "s": pltpu.SMEM, "a": pl.ANY}
    return [pl.BlockSpec(memory_space=kinds[c]) for c in text]


def iota(shape, dim):
    return lax.broadcasted_iota(i32, shape, dim)


def ceil_to(n, step):
    return -(-n // step) * step


def plan(labels, groups, span):
    rows = labels.shape[0]
    count = len(groups)
    mask = jnp.concatenate([(labels >= g * span) & (labels < (g + 1) * span) for g in groups], axis=0)
    one = jnp.where(mask, 1.0, 0.0)
    m = one.astype(bf16)
    total = count * rows
    upper = jnp.where(iota((BLOCK, BLOCK), 0) <= iota((BLOCK, BLOCK), 1), 1.0, 0.0).astype(bf16)
    cum = jnp.dot(m, upper, preferred_element_type=f32)
    a, b = iota((total, total), 0), iota((total, total), 1)
    lower = jnp.where((a // rows == b // rows) & (b < a), 1.0, 0.0).astype(bf16)
    tot = jnp.sum(one, axis=1, keepdims=True)
    base = jnp.dot(lower, jnp.broadcast_to(tot, (total, 128)).astype(bf16), preferred_element_type=f32)[:, :1]
    lo, hi = base.astype(i32), (base + tot).astype(i32)
    pos = jnp.where(mask, lo + cum.astype(i32) - 1, -FAR)
    tot_row = lax.dot_general(jnp.ones((8, BLOCK), bf16), m, (((1,), (1,)), ((), ())), preferred_element_type=f32)
    base_row = lax.dot_general(tot_row.astype(bf16), lower, (((1,), (1,)), ((), ())), preferred_element_type=f32)
    return pos, lo, hi, base_row.astype(i32), (base_row + tot_row).astype(i32)


def sorted_rows(pos, lo, hi, rows, first, count):
    row, at = None, 0
    for n in range(first, first + count):
        s = slice(n * rows, (n + 1) * rows)
        start = lo[s] // 16 * 16
        r = pos[s] + (at - start)
        row = r if row is None else jnp.maximum(row, r)
        at = at + (hi[s] + 15) // 16 * 16 - start
    return row


def squeeze(pos, labels, group, span):
    rows, lanes = pos.shape
    at = iota((rows, lanes), 0) * lanes + iota((rows, lanes), 1)
    v = jnp.where(pos >= 0, (at - pos) * 16 + (labels - group * span + 1), 0)
    for bit in range((rows * lanes).bit_length() - 1):
        step = 1 << bit
        go = jnp.where(((v >> (4 + bit)) & 1) == 1, v, 0)
        if step < lanes:
            moved = pltpu.roll(go, lanes - step, 1)
            moved = jnp.where(iota((rows, lanes), 1) < lanes - step, moved, pltpu.roll(moved, rows - 1, 0))
        else:
            moved = pltpu.roll(go, rows - step // lanes, 0)
        v = v - go + moved
    return v & 15


def tiles_of(bounds, group, blocks, row=1):
    return (bounds[row, (group + 1) * blocks - 1] + TILE - 1) // TILE


def spans(bounds, groups, blocks, b):
    at, result = 0, []
    for g in groups:
        lo, hi = bounds[0, g * blocks + b], bounds[1, g * blocks + b]
        first = pl.multiple_of(lo // 16 * 16, 16)
        result.append((first, pl.multiple_of(at, 16) if result else 0, lo - first))
        at = at + ((hi + 15) // 16 * 16 - first)
    return result


def window_rows(count, step):
    return ceil_to(BLOCK + 30 * count, step)


def sort_rows(bounds, row_ref, x_ref, groups, blocks, moved, put):
    rows = window_rows(len(groups), 64)
    for b in range(blocks):
        hot = jnp.where(iota((rows, BLOCK), 0) == row_ref[b : b + 1, :], 1.0, 0.0).astype(bf16)
        out = jnp.dot(hot, x_ref[b * BLOCK : (b + 1) * BLOCK, :], preferred_element_type=f32).astype(bf16)
        moved[b, :rows, :] = out
        moved[b, rows:, :] = jnp.zeros((moved.shape[1] - rows, out.shape[1]), bf16)
    for n in range(len(groups)):
        for b in range(blocks):
            first, at, over = spans(bounds, groups, blocks, b)[n]
            dst, start = put(n, first)
            old = dst[pl.ds(start, 16), :]
            new = moved[b, pl.ds(at, 16), :]
            dst[pl.ds(start, 16), :] = jnp.where(iota((16, 1), 0) < over, old, new)
            rest = pl.ds(pl.multiple_of(start + 16, 16), BLOCK)
            dst[rest, :] = moved[b, pl.ds(pl.multiple_of(at + 16, 16), BLOCK), :]


def unsort_rows(bounds, row_ref, groups, blocks, pick, moved, emit):
    rows = window_rows(len(groups), 128)
    tail = BLOCK + 16
    for b in range(blocks):
        moved[b, tail:, :] = jnp.zeros((moved.shape[1] - tail, moved.shape[2]), bf16)
        for n, (first, at, _) in enumerate(spans(bounds, groups, blocks, b)):
            moved[b, pl.ds(at, WIN), :] = pick(n, first, WIN)
    for b in range(blocks):
        hot = jnp.where(iota((rows, BLOCK), 0) == row_ref[b : b + 1, :], 1.0, 0.0).astype(bf16)
        emit(b, jnp.dot(jnp.transpose(hot), moved[b, :rows, :], preferred_element_type=f32))


def layer_tile(x, named, ct, wp_ref, wpt_ref, cb_ref, gw_ref, span):
    rows = x.shape[0]
    col = jnp.transpose(jnp.broadcast_to(named.astype(f32), (8, rows)))[:, :1]
    pre = jnp.dot(x, wp_ref[...], preferred_element_type=f32)
    add = cb_ref[0:1, :]
    for s in range(1, span):
        add = jnp.where(col == s + 1.0, cb_ref[s : s + 1, :], add)
    pre = pre + add
    valid = col > 0.0
    e = jnp.exp(-jnp.abs(pre))
    u = 1.0 + e
    r = 1.0 / u
    soft = jnp.maximum(pre, 0.0) + jnp.where(e < 2.0**-9, e - (0.5 * e) * e, jnp.log(u))
    sig = jnp.where(pre >= 0.0, r, e * r)
    lo = jnp.where(valid, soft, 0.0).astype(bf16)
    gp = jnp.where(valid, ct.astype(f32) * sig, 0.0).astype(bf16)
    gx = jnp.dot(gp, wpt_ref[...], preferred_element_type=f32).astype(bf16)
    sel = jnp.where(jnp.broadcast_to(named, (16, rows)) == iota((16, rows), 0) + 1, 1.0, 0.0).astype(bf16)
    left = jnp.concatenate([jnp.transpose(x), sel], axis=0)
    gw_ref[...] += jnp.dot(left, gp, preferred_element_type=f32)
    return lo, gx


def pack_kernel(oct_count, shape_axis, oct_axis, span, cap, octants_hbm, ids_hbm, x_hbm, *refs):
    far = oct_count // 2 - 1
    octants_ref, ids_ref, x_ref, in_sem = refs[-4:]
    refs = refs[:-4]
    fetches = [
        pltpu.make_async_copy(a, b, in_sem.at[i])
        for i, (a, b) in enumerate(zip((octants_hbm, ids_hbm, x_hbm), (octants_ref, ids_ref, x_ref)))
    ]
    for f in fetches:
        f.start()
    heads, refs = refs[: far * LEAD], refs[far * LEAD :]
    queues, rows_far, refs = refs[:far], refs[far : 2 * far], refs[2 * far :]
    row_near, bounds_ref, names_ref, info_ref, moved, bounds_v, bounds, sem = refs
    blocks = row_near.shape[0]
    me = lax.axis_index(oct_axis)
    first_shape = lax.axis_index(shape_axis) * span

    def wide(ref):
        return jnp.concatenate([ref[pl.ds(h, blocks, 2), :] for h in range(2)], axis=1)

    for f in fetches[:2]:
        f.wait()
    ids = wide(ids_ref) - first_shape
    labels = (wide(octants_ref) ^ me) * span + ids
    pos, lo, hi, first_row, last_row = plan(labels, range(oct_count), span)
    n = oct_count * blocks
    bounds_v[...] = jnp.zeros(bounds_v.shape, i32)
    bounds_v[0:1, :n] = first_row[:1]
    bounds_v[1:2, :n] = last_row[:1]
    bounds_ref[...] = bounds_v[...]
    copy = pltpu.make_async_copy(bounds_v, bounds, sem)
    copy.start()
    row_near[...] = sorted_rows(pos, lo, hi, blocks, 0, 2)
    for k in range(far):
        rows_far[k][...] = sorted_rows(pos, lo, hi, blocks, 2 + 2 * k, 2)
    tiles = cap // TILE
    names_ref[...] = jnp.zeros(names_ref.shape, i32)
    for g in range(2):
        names_ref[g * 8 : g * 8 + tiles, :] = squeeze(pos[g * blocks : (g + 1) * blocks], labels, g, span)[:tiles]

    info_ref[...] = jnp.zeros(info_ref.shape, f32)
    for s in range(span):
        number = jnp.sum(jnp.sum(jnp.where(ids == s, 1.0, 0.0), axis=1, keepdims=True), axis=0, keepdims=True)
        info_ref[s : s + 1, :] = jnp.broadcast_to(number, (1, 128))

    for k in range(far):
        queues[k][...] = jnp.zeros(queues[k].shape, bf16)
    copy.wait()
    fetches[2].wait()
    rows = CHUNK * TILE
    for k in range(far):
        groups = [2 + 2 * k, 3 + 2 * k]
        cut = tiles_of(bounds, groups[0], blocks) * TILE
        sort_rows(bounds, rows_far[k], x_ref, groups, blocks, moved,
                  lambda n, first: (queues[k], pl.multiple_of(first + n * cut, 16)))
        for j in range(LEAD):
            heads[k * LEAD + j][:rows, :] = queues[k][j * rows : (j + 1) * rows, :]
        heads[k * LEAD][rows:, :] = labels.astype(f32).astype(bf16)


def pack(octants, ids, points, oct_count, span, cap):
    count, width = points.shape
    blocks = count // BLOCK
    far = oct_count // 2 - 1
    rows = CHUNK * TILE
    shape = jax.ShapeDtypeStruct
    heads = [pltpu.VMEM((rows + (blocks if j == 0 else 0), width), bf16) for j in range(LEAD)] * far
    outs = heads + [pltpu.VMEM((4 * cap, width), bf16)] * far
    outs += [shape((blocks, BLOCK), i32)] * (far + 1)
    outs += [shape((8, 128), i32), shape((16, BLOCK), i32), shape((8, 128), f32)]
    out = pl.pallas_call(
        functools.partial(pack_kernel, oct_count, "shape", "oct", span, cap),
        in_specs=specs("aaa"),
        out_specs=specs("v" * len(outs)),
        out_shape=outs,
        scratch_shapes=[
            pltpu.VMEM((blocks, window_rows(2, 64) + WIN, width), bf16),
            pltpu.VMEM((8, 128), i32),
            pltpu.SMEM((8, 128), i32),
            pltpu.SemaphoreType.DMA,
            pltpu.VMEM((count // 128, 128), i32),
            pltpu.VMEM((count // 128, 128), i32),
            pltpu.VMEM(points.shape, bf16),
            pltpu.SemaphoreType.DMA((3,)),
        ],
        compiler_params=params(16),
        cost_estimate=CHEAP,
        name="pack",
    )(stay(octants.reshape(-1, 128)), stay(ids.reshape(-1, 128)), stay(points))
    heads, queues, rows_far, out = out[: far * LEAD], out[far * LEAD : far * LEAD + far], out[far * LEAD + far : far * LEAD + 2 * far], out[far * LEAD + 2 * far :]
    return heads, queues, rows_far, out


def set_weights(hid, direction_ref, gain_ref, bias_ref, codes_ref, wp_ref, wpt_ref, w_ref, cb_ref, norm_ref):
    direction = direction_ref[...]
    norms = jnp.sqrt(jnp.sum(direction * direction, axis=0, keepdims=True) + norm_eps)
    weight = (direction * (gain_ref[...] / norms)).astype(bf16)
    norm_ref[...] = norms
    w_ref[...] = weight
    width = wp_ref.shape[0]
    wf = weight.astype(f32)
    last = jnp.where(iota((8, 1), 0) + (width - 8) < hid, wf[width - 8 : width, :], wf[-8:, :])
    wp = jnp.concatenate([wf[: width - 8, :], last], axis=0)
    wp_ref[...] = wp.astype(bf16)
    wpt_ref[...] = wp.T.astype(bf16)
    span, code_width = codes_ref.shape
    w_code = wf[hid : hid + code_width, :].astype(bf16)
    codes = jnp.concatenate([codes_ref[...].astype(f32), jnp.zeros((8 - span, code_width), f32)], axis=0).astype(bf16)
    cb_ref[...] = jnp.dot(codes, w_code, preferred_element_type=f32) + bias_ref[...]


def prepare_kernel(oct_count, oct_axis, cap, bounds, row_ref, x_ref, codes_v, direction_hbm, gain_hbm, bias_hbm,
                   lo_hbm, lon_hbm, lof_hbm, gw_ref, buf, wp_ref, wpt_ref, w_ref, cb_ref, norm_ref,
                   moved, zero, direction_v, gain_v, bias_v, zero_sem, in_sem):
    blocks = row_ref.shape[0]
    tiles = cap // TILE
    source = lax.axis_index(oct_axis)
    cut = [tiles_of(bounds, r, blocks) for r in range(2)]
    fetches = [
        pltpu.make_async_copy(a, b, in_sem.at[i])
        for i, (a, b) in enumerate(((direction_hbm, direction_v), (gain_hbm, gain_v), (bias_hbm, bias_v)))
    ]
    for f in fetches:
        f.start()

    def clear(go):
        for t in range(tiles):
            for k in range(oct_count // 2):
                @pl.when(t >= (cut[0] if k == 0 else 0))
                def _():
                    at = (source ^ (2 * k)) * cap + t * TILE
                    go(pltpu.make_async_copy(zero, lo_hbm.at[pl.ds(pl.multiple_of(at, TILE), TILE), :], zero_sem))

            @pl.when(t >= cut[1])
            def _():
                go(pltpu.make_async_copy(zero, lon_hbm.at[pl.ds(t * TILE, TILE), :], zero_sem))

        for t in range(lof_hbm.shape[0] // TILE):
            go(pltpu.make_async_copy(zero, lof_hbm.at[pl.ds(t * TILE, TILE), :], zero_sem))

    zero[...] = jnp.zeros(zero.shape, bf16)
    clear(lambda c: c.start())
    gw_ref[...] = jnp.zeros(gw_ref.shape, f32)
    buf[...] = jnp.zeros(buf.shape, bf16)
    sort_rows(bounds, row_ref, x_ref, [0, 1], blocks, moved, lambda n, first: (buf.at[n], first))
    for f in fetches:
        f.wait()
    set_weights(HID, direction_v, gain_v, bias_v, codes_v, wp_ref, wpt_ref, w_ref, cb_ref, norm_ref)
    clear(lambda c: c.wait())


def prepare(bounds, row, points, direction, gain, bias, codes, oct_count, cap):
    width = points.shape[1]
    ins, outs = direction.shape
    blocks = row.shape[0]
    return pl.pallas_call(
        functools.partial(prepare_kernel, oct_count, "oct", cap),
        in_specs=specs("svvvaaa"),
        out_specs=specs("aaavvvvvvv"),
        out_shape=[
            pltpu.HBM((oct_count * cap, outs), bf16),
            pltpu.HBM((cap, outs), bf16),
            pltpu.HBM(((oct_count // 2 - 1) * cap, outs), bf16),
            pltpu.VMEM((width + 16, outs), f32),
            pltpu.VMEM((2, cap + WIN, width), bf16),
            pltpu.VMEM((width, outs), bf16),
            pltpu.VMEM((outs, width), bf16),
            pltpu.VMEM((ins, outs), bf16),
            pltpu.VMEM((8, outs), f32),
            pltpu.VMEM((1, outs), f32),
        ],
        scratch_shapes=[
            pltpu.VMEM((blocks, window_rows(2, 64) + WIN, width), bf16),
            pltpu.VMEM((TILE, outs), bf16),
            pltpu.VMEM((ins, outs), f32),
            pltpu.VMEM((1, outs), f32),
            pltpu.VMEM((1, outs), f32),
            pltpu.SemaphoreType.DMA,
            pltpu.SemaphoreType.DMA((3,)),
        ],
        compiler_params=params(14),
        cost_estimate=cost(4),
        name="prepare",
    )(bounds, row, keep(points), codes, stay(direction), stay(gain[None, :]), stay(bias[None, :]))


def local_kernel(oct_axis, blocks, span, cap, bounds, names_ref, ct_hbm, ctx_ref, wp_ref, wpt_ref, cb_ref, lo_in, lon_in, gw_in, buf_in,
                 lo_hbm, lon_hbm, gw_ref, buf, ct_v, lo_v, ct_sem, lo_sem):
    source = lax.axis_index(oct_axis)
    cut = [tiles_of(bounds, r, blocks) for r in range(2)]
    count = cut[0] + cut[1]

    def split(i):
        second = (i >= cut[0]).astype(i32)
        return second, i - second * cut[0]

    def fetch(i, go):
        second, t = split(i)
        rows = pl.ds(pl.multiple_of(source * cap + t * TILE, TILE), TILE)

        @pl.when(second == 0)
        def _():
            go(pltpu.make_async_copy(ct_hbm.at[rows, :], ct_v.at[i % 2], ct_sem.at[i % 2]))

        @pl.when(second == 1)
        def _():
            go(pltpu.make_async_copy(ctx_ref.at[rows, :], ct_v.at[i % 2], ct_sem.at[i % 2]))

    def store(i, go):
        second, t = split(i)

        @pl.when(second == 0)
        def _():
            rows = pl.ds(pl.multiple_of(source * cap + t * TILE, TILE), TILE)
            go(pltpu.make_async_copy(lo_v.at[i % 2], lo_hbm.at[rows, :], lo_sem.at[i % 2]))

        @pl.when(second == 1)
        def _():
            go(pltpu.make_async_copy(lo_v.at[i % 2], lon_hbm.at[pl.ds(pl.multiple_of(t * TILE, TILE), TILE), :], lo_sem.at[i % 2]))

    @pl.when(count > 0)
    def _():
        fetch(0, lambda c: c.start())

    def step(i, carry):
        second, t = split(i)

        @pl.when(i + 1 < count)
        def _():
            fetch(i + 1, lambda c: c.start())

        fetch(i, lambda c: c.wait())

        @pl.when(i >= 2)
        def _():
            store(i - 2, lambda c: c.wait())

        rows = pl.ds(pl.multiple_of(t * TILE, TILE), TILE)
        named = names_ref[pl.ds(second * 8 + t, 1), :]
        lo, gx = layer_tile(buf[second, rows, :], named, ct_v[i % 2], wp_ref, wpt_ref, cb_ref, gw_ref, span)
        lo_v[i % 2] = lo
        buf[second, rows, :] = gx
        store(i, lambda c: c.start())
        return carry

    lax.fori_loop(0, count, step, 0)
    for back in (2, 1):
        @pl.when(count >= back)
        def _():
            store(count - back, lambda c: c.wait())


def local(bounds, names, cotangent, ctx, weights, lo, lon, gw, buf, blocks, span, cap):
    outs = lo.shape[1]
    return pl.pallas_call(
        functools.partial(local_kernel, "oct", blocks, span, cap),
        in_specs=specs("svavvvvaavv"),
        out_specs=specs("aavv"),
        out_shape=[pltpu.HBM(lo.shape, bf16), pltpu.HBM(lon.shape, bf16), pltpu.VMEM(gw.shape, f32), pltpu.VMEM(buf.shape, bf16)],
        input_output_aliases={7: 0, 8: 1, 9: 2, 10: 3},
        scratch_shapes=[
            pltpu.VMEM((2, TILE, outs), bf16),
            pltpu.VMEM((2, TILE, outs), bf16),
            pltpu.SemaphoreType.DMA((2,)),
            pltpu.SemaphoreType.DMA((2,)),
        ],
        compiler_params=params(8),
        cost_estimate=cost(8),
        name="local",
    )(bounds, names, stay(cotangent), keep(ctx), *[keep(w) for w in weights], stay(lo), stay(lon), keep(gw), keep(buf))


def unlocal_kernel(bounds, row_ref, gbuf, part_ref, moved):
    blocks = row_ref.shape[0]

    def emit(b, rows):
        part_ref[b * BLOCK : (b + 1) * BLOCK, :] = rows.astype(bf16)

    unsort_rows(bounds, row_ref, [0, 1], blocks, lambda n, first, rows: gbuf[n, pl.ds(first, rows), :], moved, emit)


def unlocal(bounds, row, gbuf):
    blocks, width = row.shape[0], gbuf.shape[2]
    return pl.pallas_call(
        unlocal_kernel,
        in_specs=specs("svv"),
        out_specs=specs("v")[0],
        out_shape=pltpu.VMEM((blocks * BLOCK, width), bf16),
        scratch_shapes=[pltpu.VMEM((blocks, window_rows(2, 128) + WIN, width), bf16)],
        compiler_params=params(16),
        cost_estimate=CHEAP,
        name="unlocal",
    )(bounds, row, keep(gbuf))


def names_kernel(kx, span, cap, labels_ref, names_ref, count_ref, back_ref):
    labels = labels_ref[...].astype(f32).astype(i32)
    blocks = labels.shape[0]
    groups = [2 * kx, 2 * kx + 1]
    pos, _, _, _, last = plan(labels, groups, span)
    tiles = cap // TILE
    names_ref[...] = jnp.zeros(names_ref.shape, i32)
    for n, g in enumerate(groups):
        names_ref[n * 8 : n * 8 + tiles, :] = squeeze(pos[n * blocks : (n + 1) * blocks], labels, g, span)[:tiles]
    count_ref[...] = jnp.zeros(count_ref.shape, i32)
    count_ref[0:1, : 2 * blocks] = last[:1]
    back_ref[...] = jnp.zeros(back_ref.shape, bf16)


def make_names(labels, kx, span, cap):
    return pl.pallas_call(
        functools.partial(names_kernel, kx, span, cap),
        in_specs=specs("v"),
        out_specs=specs("vvv"),
        out_shape=[
            jax.ShapeDtypeStruct((16, BLOCK), i32),
            jax.ShapeDtypeStruct((8, 128), i32),
            pltpu.VMEM((2 * cap + CHUNK * TILE, labels.shape[1]), bf16),
        ],
        compiler_params=params(8),
        cost_estimate=CHEAP,
        name="names",
    )(labels)


def chunks(tiles):
    return (tiles + CHUNK - 1) // CHUNK


def lead_of(tiles):
    return jnp.maximum(chunks(tiles), LEAD)


def take_back(step_no, theirs, blocks, x_ref, back, limit=None):
    rows = CHUNK * TILE
    limit = limit or back.shape[0] // rows - 1
    n = step_no - lead_of(tiles_of(theirs, 0, blocks, 0) + tiles_of(theirs, 1, blocks, 0))

    @pl.when((n >= 0) & (n < limit))
    def _():
        back[pl.ds(pl.multiple_of(n * rows, rows), rows), :] = x_ref[:rows, :]


def far_kernel(chunk, first, last, loop, kx, oct_axis, blocks, span, cap, mine, theirs, *refs):
    if loop:
        turn, refs = refs[0], refs[1:]
    names_ref, x_ref, ct_hbm, ctx_hbm, wp_ref, wpt_ref, cb_ref, queue_in, lo_in, lof_in, gw_in, back_in, refs = *refs[:12], refs[12:]
    if not first:
        ct_v, lo_old, refs = *refs[:2], refs[2:]
    queue, lo_hbm, lof_hbm, gw_ref, back, payload, refs = *refs[:6], refs[6:]
    if not last:
        ct_new, refs = refs[0], refs[1:]
    lo_v, refs = refs[0], refs[1:]
    if first:
        ct_v, refs = refs[0], refs[1:]
    ct_sem, new_sem, lo_sem = refs
    source = lax.axis_index(oct_axis) ^ (2 * kx)
    cut = [tiles_of(theirs, r, blocks, 0) for r in range(2)]
    lead = lead_of(tiles_of(mine, 2 * kx, blocks) + tiles_of(mine, 2 * kx + 1, blocks))
    count = cut[0] + cut[1]
    rows = CHUNK * TILE
    if loop:
        count = jnp.where(turn[0] == 0, count, 0)

    def split(c, i):
        t = c * CHUNK + i
        second = (t >= cut[0]).astype(i32)
        return t, second, t - second * cut[0]

    def ct_copy(c, i, dst, sem, go):
        t, second, slot = split(c, i)
        at = pl.ds(pl.multiple_of(source * cap + slot * TILE, TILE), TILE)
        to = dst.at[pl.ds(i * TILE, TILE), :]

        @pl.when((t < count) & (second == 0))
        def _():
            go(pltpu.make_async_copy(ct_hbm.at[at, :], to, sem.at[i]))

        @pl.when((t < count) & (second == 1))
        def _():
            go(pltpu.make_async_copy(ctx_hbm.at[at, :], to, sem.at[i]))

    def lo_copy(c, i, src, go):
        t, second, slot = split(c, i)
        of = src.at[pl.ds(i * TILE, TILE), :]

        @pl.when((t < count) & (second == 0))
        def _():
            at = pl.ds(pl.multiple_of(source * cap + slot * TILE, TILE), TILE)
            go(pltpu.make_async_copy(of, lo_hbm.at[at, :], lo_sem.at[i]))

        @pl.when((t < count) & (second == 1))
        def _():
            at = pl.ds(pl.multiple_of((kx - 1) * cap + slot * TILE, TILE), TILE)
            go(pltpu.make_async_copy(of, lof_hbm.at[at, :], lo_sem.at[i]))

    start, wait = lambda c: c.start(), lambda c: c.wait()
    for i in range(CHUNK):
        if first:
            ct_copy(chunk, i, ct_v, ct_sem, start)
        else:
            lo_copy(chunk - 1, i, lo_old, start)
        if not last:
            ct_copy(chunk + 1, i, ct_new, new_sem, start)
    if not loop:
        take_back(chunk, theirs, blocks, x_ref, back)
    for i in range(CHUNK):
        t, second, slot = split(chunk, i)
        at = slice(i * TILE, (i + 1) * TILE)

        @pl.when(t < count)
        def _():
            if first:
                ct_copy(chunk, i, ct_v, ct_sem, wait)
            named = names_ref[pl.ds(second * 8 + slot, 1), :]
            lo, gx = layer_tile(x_ref[at, :], named, ct_v[at, :], wp_ref, wpt_ref, cb_ref, gw_ref, span)
            lo_v[at, :] = lo
            queue[pl.ds(pl.multiple_of((lead + chunk) * rows + i * TILE, TILE), TILE), :] = gx

    if loop:
        payload[...] = queue[pl.ds(pl.multiple_of((turn[0] + STEPS - 1) * rows, rows), rows), :]
        for i in range(CHUNK):
            lo_copy(chunk, i, lo_v, start)
        for i in range(CHUNK):
            lo_copy(chunk, i, lo_v, wait)
    else:
        payload[...] = queue[(chunk + LEAD) * rows : (chunk + LEAD + 1) * rows, :]
    for i in range(CHUNK):
        if not first:
            lo_copy(chunk - 1, i, lo_old, wait)
        if not last:
            ct_copy(chunk + 1, i, ct_new, new_sem, wait)


def far_step(chunk, kx, mine, theirs, names, x, cotangent, ctx, weights, state, ahead, blocks, span, cap, last, turn=None):
    wp, wpt, cb = weights
    queue, lo, lof, gw, back = state
    width, outs = wp.shape
    rows = CHUNK * TILE
    loop, first = turn is not None, ahead is None
    shapes = [pltpu.VMEM(queue.shape, bf16), pltpu.HBM(lo.shape, bf16), pltpu.HBM(lof.shape, bf16), pltpu.VMEM(gw.shape, f32),
              pltpu.VMEM(back.shape, bf16), pltpu.VMEM((rows, width), bf16)]
    shapes += [pltpu.VMEM((rows, outs), bf16)] * ((not last) + (not loop))
    base = 2 + loop
    args = [mine, theirs] + ([turn] if loop else []) + [names, keep(x), stay(cotangent), keep(ctx), keep(wp), keep(wpt), keep(cb), keep(queue), stay(lo),
            stay(lof), keep(gw), keep(back)] + [keep(a) for a in (ahead or ())]
    out = pl.pallas_call(
        functools.partial(far_kernel, chunk, first, last, loop, kx, "oct", blocks, span, cap),
        in_specs=specs("ss" + "s" * loop + "vvavvvvvaavv" + "vv" * (not first)),
        out_specs=specs("vaavvv" + "v" * (len(shapes) - 6)),
        out_shape=shapes,
        input_output_aliases={base + 7 + i: i for i in range(5)},
        scratch_shapes=([pltpu.VMEM((rows, outs), bf16)] * (first + loop))
        + [pltpu.SemaphoreType.DMA((CHUNK,)), pltpu.SemaphoreType.DMA((CHUNK,)), pltpu.SemaphoreType.DMA((CHUNK,))],
        compiler_params=params(12),
        cost_estimate=CHEAP,
        name="far",
    )(*args)
    return tuple(out[:5]), out[5], (None if loop else (None if last else out[6], out[6 + (not last)]))


def flush_kernel(chunk, kx, oct_axis, blocks, cap, theirs, lo_old, lo_in, lof_in, lo_hbm, lof_hbm, sem):
    source = lax.axis_index(oct_axis) ^ (2 * kx)
    cut = [tiles_of(theirs, r, blocks, 0) for r in range(2)]
    for go in (lambda c: c.start(), lambda c: c.wait()):
        for i in range(CHUNK):
            t = chunk * CHUNK + i
            second = (t >= cut[0]).astype(i32)
            slot = t - second * cut[0]
            of = lo_old.at[pl.ds(i * TILE, TILE), :]

            @pl.when((t < cut[0] + cut[1]) & (second == 0))
            def _():
                at = pl.ds(pl.multiple_of(source * cap + slot * TILE, TILE), TILE)
                go(pltpu.make_async_copy(of, lo_hbm.at[at, :], sem.at[i]))

            @pl.when((t < cut[0] + cut[1]) & (second == 1))
            def _():
                at = pl.ds(pl.multiple_of((kx - 1) * cap + slot * TILE, TILE), TILE)
                go(pltpu.make_async_copy(of, lof_hbm.at[at, :], sem.at[i]))


def flush(chunk, kx, theirs, lo_old, lo, lof, blocks, cap):
    return pl.pallas_call(
        functools.partial(flush_kernel, chunk, kx, "oct", blocks, cap),
        in_specs=specs("svaa"),
        out_specs=specs("aa"),
        out_shape=[pltpu.HBM(lo.shape, bf16), pltpu.HBM(lof.shape, bf16)],
        input_output_aliases={2: 0, 3: 1},
        scratch_shapes=[pltpu.SemaphoreType.DMA((CHUNK,))],
        compiler_params=params(4),
        cost_estimate=CHEAP,
        name="flush",
    )(theirs, keep(lo_old), stay(lo), stay(lof))


def return_kernel(blocks, turn, theirs, x_ref, back_in, back):
    take_back(turn[0] + STEPS - 1, theirs, blocks, x_ref, back)


def return_step(turn, theirs, x, back, blocks):
    return pl.pallas_call(
        functools.partial(return_kernel, blocks),
        in_specs=specs("ssvv"),
        out_specs=specs("v")[0],
        out_shape=pltpu.VMEM(back.shape, bf16),
        input_output_aliases={3: 0},
        compiler_params=params(8),
        cost_estimate=CHEAP,
        name="returned",
    )(turn, theirs, keep(x), keep(back))


def unpack_kernel(far, blocks, lasts, limit, bounds, *refs):
    theirs, rows_far, refs = refs[:far], refs[far : 2 * far], refs[2 * far :]
    parts, refs = refs[: far * len(lasts)], refs[far * len(lasts) :]
    part_ref, refs = refs[0], refs[1 + far :]
    out_ref, backs, moved = refs[0], refs[1 : 1 + far], refs[-1]
    for k in range(far):
        for j, step_no in enumerate(lasts):
            take_back(step_no, theirs[k], blocks, parts[k * len(lasts) + j], backs[k], limit)
        cut = tiles_of(bounds, 2 + 2 * k, blocks) * TILE

        def pick(n, first, count):
            return backs[k][pl.ds(pl.multiple_of(first + n * cut, 16), count), :]

        def emit(b, value):
            at = slice(b * BLOCK, (b + 1) * BLOCK)
            before = part_ref if k == 0 else out_ref
            out_ref[at, :] = (value + before[at, :].astype(f32)).astype(bf16)

        unsort_rows(bounds, rows_far[k], [2 + 2 * k, 3 + 2 * k], blocks, pick, moved, emit)


def unpack(bounds, theirs, rows_far, lasts, limit, parts, part, backs):
    points, width = part.shape
    blocks = points // BLOCK
    far = len(theirs)
    extra = far * len(lasts)
    return pl.pallas_call(
        functools.partial(unpack_kernel, far, blocks, lasts, limit),
        in_specs=specs("s" + "s" * far + "v" * (2 * far + extra + 1)),
        out_specs=specs("v" * (1 + far)),
        out_shape=[jax.ShapeDtypeStruct(part.shape, bf16)] + [pltpu.VMEM(b.shape, bf16) for b in backs],
        input_output_aliases={2 * far + extra + 2 + k: 1 + k for k in range(far)},
        scratch_shapes=[pltpu.VMEM((blocks, window_rows(2, 128) + WIN, width), bf16)],
        compiler_params=params(20),
        cost_estimate=CHEAP,
        name="unpack",
    )(bounds, *theirs, *rows_far, *[keep(x) for x in parts], keep(part), *[keep(b) for b in backs])[0]


def merge_kernel(cap, kxs, oct_axis, lox_ref, lo_in, lo_hbm, sem):
    other = lax.axis_index(oct_axis) ^ 1
    for go in (lambda c: c.start(), lambda c: c.wait()):
        for n, k in enumerate(kxs):
            at = pl.ds(pl.multiple_of((other ^ (2 * k)) * cap, cap), cap)
            go(pltpu.make_async_copy(lox_ref.at[pl.ds(n * cap, cap), :], lo_hbm.at[at, :], sem.at[n]))


def merge(lox, lo, cap, kxs):
    return pl.pallas_call(
        functools.partial(merge_kernel, cap, tuple(kxs), "oct"),
        in_specs=specs("va"),
        out_specs=specs("a")[0],
        out_shape=pltpu.HBM(lo.shape, lo.dtype),
        input_output_aliases={1: 0},
        scratch_shapes=[pltpu.SemaphoreType.DMA((len(kxs),))],
        compiler_params=params(4),
        cost_estimate=CHEAP,
        name="merge",
    )(keep(lox), stay(lo))


def column_block(axes, n):
    a, b = (lax.axis_index(axis) % 2 for axis in axes)
    return (a ^ (n % 2)) * 2 + (b ^ (n // 2))


def collect_kernel(axes, shape_axis, oct_axis, shapes, span, extra, blocks, late, *refs):
    mine, refs = refs[0], refs[1:]
    theirs, refs = refs[:extra], refs[extra:]
    gw_ref, info_ref, codes_ref, outs, full = *refs[:3], refs[3:7], refs[7]
    width = gw_ref.shape[0] - 16
    cols = gw_ref.shape[1]
    code_width = codes_ref.shape[1]
    base = lax.axis_index(shape_axis) * span
    full[:width, :] = gw_ref[:width, :]
    ps = jnp.zeros((shapes, cols), f32)
    for s in range(span):
        ps = ps + jnp.where(iota((shapes, 1), 0) == base + s, gw_ref[width + s : width + s + 1, :], 0.0)
    full[width : width + shapes, :] = ps
    if late:
        full[width + shapes :, :] = jnp.zeros((full.shape[0] - width - shapes, cols), f32)
    else:
        lane = iota((1, cols - code_width), 1)
        info = jnp.zeros((shapes, cols), f32)
        for s in range(span):
            number = info_ref[s : s + 1, :1]
            high = jnp.floor(number / 1024.0)
            mid = jnp.floor((number - 1024.0 * high) / 32.0)
            low = number - 1024.0 * high - 32.0 * mid
            digits = jnp.where(lane < 64, low, jnp.where(lane < 128, mid, high))
            code = jnp.where(lax.axis_index(oct_axis) == 0, codes_ref[s : s + 1, :].astype(f32), 0.0)
            info = info + jnp.where(iota((shapes, 1), 0) == base + s, jnp.concatenate([code, digits], axis=1), 0.0)
        full[width + shapes : width + 2 * shapes, :] = info
        flag = jnp.int32(0)
        for k in range(extra):
            ours = chunks(tiles_of(mine, 2 + 2 * k, blocks) + tiles_of(mine, 3 + 2 * k, blocks))
            other = chunks(tiles_of(theirs[k], 0, blocks, 0) + tiles_of(theirs[k], 1, blocks, 0))
            most = jnp.maximum(jnp.maximum(ours, LEAD) + other, jnp.maximum(other, LEAD) + ours)
            flag = flag | ((jnp.maximum(ours, other) > USUAL) | (most > STEPS)).astype(i32)
        full[width + 2 * shapes :, :] = jnp.zeros((16, cols), f32) + flag.astype(f32)
    for n in range(4):
        at = pl.ds(pl.multiple_of(column_block(axes, n) * 128, 128), 128)
        outs[n][...] = full[:, at].astype(bf16)


def finish_kernel(axes, shape_axis, hid, span, categories, momentum, *refs):
    parts, refs = refs[:4], refs[4:]
    direction_ref, gain_ref, norm_ref, w_ref, mean_ref, var_ref, refs = *refs[:6], refs[6:]
    dg_ref, gg_ref, bg_ref, cg_ref, mean_out, var_out, full = refs
    for n in range(4):
        at = pl.ds(pl.multiple_of(column_block(axes, n) * 128, 128), 128)
        full[:, at] = parts[n][...].astype(f32)
    ins, cols = direction_ref.shape
    cats, code_width = mean_ref.shape
    shapes = (full.shape[0] - 16 - (ins - code_width)) // 2
    width = ins - code_width
    ps = full[width : width + shapes, :]
    info = full[width + shapes : width + 2 * shapes, :]
    codes = info[:, :code_width]
    at = code_width
    number = info[:, at : at + 1] + 32.0 * info[:, at + 64 : at + 65] + 1024.0 * info[:, at + 128 : at + 129]
    for c in range(cats):
        chosen = jnp.zeros((shapes, 1), f32)
        for s in range(shapes):
            chosen = jnp.where((iota((shapes, 1), 0) == s) & (categories[s] == c), 1.0, chosen)
        weight = chosen * number
        count = jnp.sum(weight, axis=0, keepdims=True)
        mean = jnp.sum(weight * codes, axis=0, keepdims=True) / count
        var = jnp.sum(weight * codes * codes, axis=0, keepdims=True) / count - mean * mean
        rate = momentum[c]
        mean_out[c : c + 1, :] = (1.0 - rate) * mean_ref[c : c + 1, :] + rate * mean
        var_out[c : c + 1, :] = (1.0 - rate) * var_ref[c : c + 1, :] + rate * var

    gw = full[:width, :]
    codes_all = jnp.concatenate(
        [jnp.zeros((shapes, hid), f32), codes, jnp.zeros((shapes, ins - hid - code_width), f32)], axis=1
    )
    wg = lax.dot_general(codes_all, ps, (((0,), (0,)), ((), ())), precision=lax.Precision.HIGHEST, preferred_element_type=f32)
    head = jnp.where(iota((width, 1), 0) < hid, gw, wg[:width])
    tail = jnp.where(iota((8, 1), 0) + (width - 8) >= hid, gw[width - 8 :], wg[ins - 8 :])
    wg = jnp.concatenate([head, wg[width : ins - 8], tail], axis=0)
    direction = direction_ref[...]
    norms = norm_ref[...]
    dots = jnp.sum(wg * direction, axis=0, keepdims=True)
    gg_ref[...] = dots / norms
    dg_ref[...] = (gain_ref[...] / norms) * (wg - direction * (dots / (norms * norms)))
    bg_ref[...] = jnp.sum(ps, axis=0, keepdims=True)
    base = lax.axis_index(shape_axis) * span
    own = jnp.zeros((8, cols), f32)
    for s in range(span):
        row = jnp.sum(jnp.where(iota((shapes, 1), 0) == base + s, ps, 0.0), axis=0, keepdims=True)
        own = own + jnp.where(iota((8, 1), 0) == s, row, 0.0)
    cg_ref[...] = lax.dot_general(own, w_ref[...].astype(f32), (((1,), (1,)), ((), ())), precision=lax.Precision.HIGHEST, preferred_element_type=f32)


def finish(axes, span, categories, momentum, parts, direction, gain, norms, weight, prev_mean, prev_var):
    ins, outs = direction.shape
    return pl.pallas_call(
        functools.partial(finish_kernel, axes, "shape", HID, span),
        in_specs=specs("ss" + "v" * 10),
        out_specs=specs("v" * 6),
        out_shape=[
            jax.ShapeDtypeStruct((ins, outs), f32),
            jax.ShapeDtypeStruct((1, outs), f32),
            jax.ShapeDtypeStruct((1, outs), f32),
            jax.ShapeDtypeStruct((8, ins), f32),
            jax.ShapeDtypeStruct(prev_mean.shape, f32),
            jax.ShapeDtypeStruct(prev_mean.shape, f32),
        ],
        scratch_shapes=[pltpu.VMEM((parts[0].shape[0], outs), f32)],
        compiler_params=params(12),
        cost_estimate=CHEAP,
        name="finish",
    )(categories, momentum, *[keep(p) for p in parts], keep(direction), gain[None, :], keep(norms), keep(weight), prev_mean, prev_var)


def swap(v, axis, k):
    n = lax.axis_size(axis)
    return lax.ppermute(v, axis, [(i, i ^ k) for i in range(n)])


def swap_both(v, k):
    n, m = lax.axis_size("shape"), lax.axis_size("oct")
    return lax.ppermute(v, ("shape", "oct"), [(i, i ^ k) for i in range(n * m)])


def bits(axis, first):
    n = lax.axis_size(axis)
    return [(axis, 1 << j) for j in range(first, n.bit_length() - 1)]


def after(x, *others):
    return lax.optimization_barrier((x, *others))[0]


def quarters_to(parts):
    m = lax.axis_size("oct")
    return [swap(parts[0], "oct", 1), swap(parts[1], "shape", 1), swap_both(parts[2], m + 1)]


def total_quarter(parts):
    got = quarters_to(parts[1:])
    v = (parts[0].astype(f32) + got[0].astype(f32) + got[1].astype(f32) + got[2].astype(f32)).astype(bf16)
    yield v
    for axis, k in bits("shape", 1) + bits("oct", 1):
        v = (v.astype(f32) + swap(v, axis, k).astype(f32)).astype(bf16)
        yield v


AXES = ("oct", "shape")


def collect(mine, theirs, gw, info, codes, shapes, blocks, late):
    span = codes.shape[0]
    rows = gw.shape[0] - 16 + 2 * shapes + 16
    return pl.pallas_call(
        functools.partial(collect_kernel, AXES, "shape", "oct", shapes, span, len(theirs), blocks, late),
        in_specs=specs("s" + "s" * len(theirs) + "vvv"),
        out_specs=specs("vvvv"),
        out_shape=[pltpu.VMEM((rows, 128), bf16)] * 4,
        scratch_shapes=[pltpu.VMEM((rows, gw.shape[1]), f32)],
        compiler_params=params(8),
        cost_estimate=CHEAP,
        name="collect",
    )(mine, *theirs, keep(gw), info, codes)


def body(point_inputs, shape_ids, octants, categories, codes, direction, gain, bias, cotangent, prev_mean, prev_var, momentum):
    points, width = point_inputs.shape
    oct_count, shape_dev = lax.axis_size("oct"), lax.axis_size("shape")
    cap = 2 * points // oct_count
    span, code_width = codes.shape
    shapes = shape_dev * span
    blocks = points // BLOCK
    rows = CHUNK * TILE
    far = list(range(1, oct_count // 2))
    most = chunks(2 * cap // TILE)
    usual = min(USUAL, most)
    steps = min(STEPS, max(most, LEAD) + most)
    loop = (usual, steps) != (most, max(most, LEAD) + most)
    assert most - usual <= 1

    ctx = swap(cotangent, "oct", 1)
    heads, queues, rows_far, (row_near, mine, near_names, info) = pack(
        octants, shape_ids, point_inputs, oct_count, span, cap)
    got = {(k, j): swap(heads[(k - 1) * LEAD + j], "oct", 2 * k) for k in far for j in range(LEAD)}
    lo, lon, lof, gw, buf, wp, wpt, weight, cb, norms = prepare(
        mine, row_near, point_inputs, direction, gain, bias, codes, oct_count, cap)
    weights = (wp, wpt, cb)

    queue = {k: queues[k - 1] for k in far}
    named, theirs, back, ahead = {}, {}, {}, {}
    for k in far:
        named[k], theirs[k], back[k] = make_names(after(got[k, 0], gw)[rows:], k, span, cap)
        ahead[k] = None
    lo, lon, gw, buf = local(mine, near_names, cotangent, ctx, weights, lo, lon, after(gw, back[1]), buf, blocks, span, cap)
    for c in range(usual):
        for k in far:
            x = got[k, c]
            if c == min(4, usual - 1):
                part = unlocal(mine, row_near, buf)
                x = after(x, part)
            (queue[k], lo, lof, gw, back[k]), payload, ahead[k] = far_step(
                c, k, mine, theirs[k], named[k], x, cotangent, ctx, weights, (queue[k], lo, lof, gw, back[k]), ahead[k],
                blocks, span, cap, c == usual - 1)
            if c + LEAD < steps:
                got[k, c + LEAD] = swap(payload, "oct", 2 * k)
        if c == 1:
            lo = merge(swap(lon, "oct", 1), lo, cap, [0])
    their = [theirs[k] for k in far]
    sums = total_quarter(collect(mine, their, gw, info, codes, shapes, blocks, False))
    v = next(sums)
    for k in far:
        lo, lof = flush(usual - 1, k, theirs[k], after(ahead[k][1], v), lo, lof, blocks, cap)
    v = next(sums)
    lo = merge(after(swap(lof, "oct", 1), v), lo, cap, far)
    for v in sums:
        pass
    parts = [v] + quarters_to([v] * 3)
    lasts = list(range(usual, steps))

    if loop:
        left = jnp.where(v[-1, 0] > 0, max(most, LEAD) + most - (STEPS - 1), 0).astype(i32)
        zeros = jnp.zeros(gw.shape, f32)

        def more(carry):
            i, queue, lo, lof, back, parts = carry
            turn = i.reshape(1)
            queue, back = dict(zip(far, queue)), dict(zip(far, back))
            gw = zeros
            for k in far:
                (queue[k], lo, lof, gw, back[k]), payload, _ = far_step(
                    usual, k, mine, theirs[k], named[k], got[k, usual], cotangent, ctx, weights, (queue[k], lo, lof, gw, back[k]),
                    None, blocks, span, cap, True, turn)
                back[k] = return_step(turn, theirs[k], swap(payload, "oct", 2 * k), back[k], blocks)
            lo = merge(swap(lof, "oct", 1), lo, cap, far)
            sums = list(total_quarter(collect(mine, their, gw, info, codes, shapes, blocks, True)))[-1]
            parts = [(a.astype(f32) + b.astype(f32)).astype(bf16) for a, b in zip(parts, [sums] + quarters_to([sums] * 3))]
            return i + 1, [queue[k] for k in far], lo, lof, [back[k] for k in far], parts

        carry = (jnp.int32(0), [queue[k] for k in far], lo, lof, [back[k] for k in far], parts)
        _, _, lo, _, backs, parts = lax.while_loop(lambda c: c[0] < left, more, carry)
    else:
        backs = [back[k] for k in far]
    direction_grad, gain_grad, bias_grad, code_grad, running_mean, running_var = finish(
        AXES, span, categories, momentum, parts, direction, gain, norms, weight, prev_mean, prev_var)
    input_grad = unpack(mine, their, rows_far, lasts, usual, [got[k, t] for k in far for t in lasts], part, backs)
    return (
        lo,
        input_grad,
        code_grad[:span, HID : HID + code_width],
        direction_grad,
        gain_grad[0],
        bias_grad[0],
        running_mean,
        running_var,
    )


def solution(mesh):
    both = P(("shape", "oct"), None)
    in_specs = (both, P(("shape", "oct")), both, P(), P("shape", None), P(), P(), P(), both, P(), P(), P())
    out_specs = (both, both, P("shape", None), P(), P(), P(), P(), P())
    return jax.shard_map(body, mesh=mesh, in_specs=in_specs, out_specs=out_specs, check_vma=False)
```

time: 323 us -> 124 us (0.38)
  blocking collectives: 82.7 us -> 0 us
  waiting for transfers between devices: 95.6 us -> 35.3 us
  local copies, waits for them, and re-layouts: 59.4 us -> 8.76 us
  Pallas kernels: 0 us -> 49.3 us
  matrix products: 44.2 us -> 0 us
  starting transfers between devices: 14.2 us -> 27.8 us
  between operations: 14.3 us -> 1.65 us
  other arithmetic: 11.4 us -> 0.12 us
    psum x2 -> x0, blocking collectives: 82.7 us -> none  [the longest x1 76.1 us: body(): lax.psum((grad_weight, grad_bias, code_sums, code_squares, cat_counts), (...]
    pallas_call x0 -> x18, Pallas kernels: none -> 49.3 us  [the longest x7 15.2 us: far_step(): pl.pallas_call(functools.partial(far_kernel, chunk, first, last, loop, kx...]
    psum x1 -> x0, waiting for transfers between devices: 48.4 us -> none  [body(): lax.psum((grad_weight, grad_bias, code_sums, code_squares, cat_counts), (...]
    all_to_all x3 -> x0, waiting for transfers between devices: 47.2 us -> none  [the longest x1 47.2 us: body(): lax.all_to_all(send_rows.reshape(oct_count, capacity, point_width), 'oct'...]
    dot_general x8 -> x0, matrix products: 44.2 us -> none  [the longest x1 26.1 us: forward_rows(): jnp.dot(select, code_proj, precision=lax.Precision.HIGHEST)]
    scatter x2 -> x0, local copies, waits for them, and re-layouts: 37 us -> none  [the longest x1 20.9 us: body(): jnp.zeros((oct_count * capacity, point_width), jnp.bfloat16).at[slots]]
    ppermute x0 -> x23, waiting for transfers between devices: none -> 35.3 us  [the longest x21 34.1 us: swap(): return lax.ppermute(v, axis, [(i, i ^ k) for i in range(n)])]
    ppermute x0 -> x23, starting transfers between devices: none -> 27.8 us  [the longest x21 26.7 us: swap(): return lax.ppermute(v, axis, [(i, i ^ k) for i in range(n)])]
  transfers between devices with their start and end apart: 4 -> 23, of which waited for: 2 -> 11; matrix products, arithmetic and copies ran while one was open for 12% -> 1% of each run, Pallas kernels for 0% -> 27%
where the time goes in v1:
time: 124 us; the launch traced here: 123 us
  Pallas kernels  49.3 us (40%)
  waiting for transfers between devices  35.3 us (28%)
  starting transfers between devices  27.8 us (22%)
  local copies, waits for them, and re-layouts  8.76 us (7%)
  between operations  1.65 us (1%)
    ppermute x21, waiting for transfers between devices, swap(): return lax.ppermute(v, axis, [(i, i ^ k) for i in range(n)])  34.1 us
    ppermute x21, starting transfers between devices, swap(): return lax.ppermute(v, axis, [(i, i ^ k) for i in range(n)])  26.7 us
    pallas_call x7, Pallas kernels, far_step(): pl.pallas_call(functools.partial(far_kernel, chunk, first, last, loop, kx...  15.2 us
    pallas_call x1, Pallas kernels, local(): pl.pallas_call(functools.partial(local_kernel, 'oct', blocks, span, cap),...  9.06 us
    unnamed x32, local copies, waits for them, and re-layouts  7.6 us
    pallas_call x1, Pallas kernels, prepare(): pl.pallas_call(functools.partial(prepare_kernel, oct_count, 'oct', cap),...  4.9 us
    pallas_call x2, Pallas kernels, merge(): pl.pallas_call(functools.partial(merge_kernel, cap, tuple(kxs), 'oct'), i...  4.25 us
    pallas_call x1, Pallas kernels, unpack(): pl.pallas_call(functools.partial(unpack_kernel, far, blocks, lasts, limit...  4.16 us
  transfers between devices with their start and end apart: 23, of which 11 were waited for; matrix products, arithmetic and copies ran while one was open for 1% of the time, Pallas kernels for 27%

profile of v1, /device:TPU:0, one launch (start us, length us, event | category | flops | bytes accessed | tf_op | source)
XLA Modules:
  0.0 123.2 jit_solution(15605487380673034781)
XLA Ops:
  1.2 3.6 %pack.1 = (bf16[528,256]{1,0:T(8,128)(2,1)S(1)}, bf16[512,256]{1,0:T(8,128)(2,1)S(1)}, bf16[512,256]{1,0:T(8,128)(2,1)S(1)}, bf16[512,256]{1,0:T(8,128)(2,1)S(1)...) custom-call(s32[32,128]{1,0:T(8,128)} %bitcast.12, ...), custom_call_target="tpu_custom_call" | custom-call | flops 1 | bytes 1 | tf_op jit(solution)/shard_map/pack/pallas_call | solution.py:245
  4.8 2.6 %collective-permute-start.11 = (bf16[528,256]{1,0:T(8,128)(2,1)S(1)}, bf16[528,256]{1,0:T(8,128)(2,1)S(1)}, u32[]{:S(2)}, u32[]{:S(2)}) collective-permute-start(bf16[528,256]{1,0:T(8,128)(2,1)S(1)} %get-tuple-element.232), channel_id=1, source_target_pairs={{0,2},{1,3},{2,0},{3,1},{4,6},{5,7},{6,4},{7,5},{8,10},{9,11},{10,... | collective-permute-start | bytes 811016 | tf_op jit(solution)/shard_map/ppermute | solution.py:866
  7.4 1.6 %copy-done.13 = bf16[4096,256]{1,0:T(8,128)(2,1)S(1)} copy-done((bf16[4096,256]{1,0:T(8,128)(2,1)S(1)}, bf16[4096,256]{1,0:T(8,128)(2,1)}, u32[]{:S(2)}) %copy-start.13) | copy-done | bytes 2097176
  8.9 4.9 %prepare.1 = (bf16[8192,512]{1,0:T(8,128)(2,1)}, bf16[2048,512]{1,0:T(8,128)(2,1)}, bf16[2048,512]{1,0:T(8,128)(2,1)}, f32[272,512]{1,0:T(8,128)S(1)}, bf16[2,23...) custom-call(s32[8,128]{1,0:T(8,128)S(1)} %get-tuple-element.543.boun, ...), custom_call_target="tpu_custom_call" | custom-call | flops 4000000000 | bytes 1 | tf_op jit(solution)/shard_map/prepare/pallas_call | solution.py:330
  13.9 0.8 copy-done.15
  14.7 0.9 names.1
  15.6 9.1 %local.1 = (bf16[8192,512]{1,0:T(8,128)(2,1)}, bf16[2048,512]{1,0:T(8,128)(2,1)}, f32[272,512]{1,0:T(8,128)S(1)}, bf16[2,2320,256]{2,1,0:T(8,128)(2,1)S(1)}) custom-call(s32[8,128]{1,0:T(8,128)S(1)} %get-tuple-element.543.bounds.mine.refs_0_, ...), custom_call_target="tpu_custom_call", output_to_operand_aliasing={{0}: (7, {}), {1}: (8, {}), {2}: (9, {}), {3}: (10, {})} | custom-call | flops 8000000000 | bytes 1 | tf_op jit(solution)/shard_map/local/pallas_call | solution.py:429
  24.9 6.1 %collective-permute-start.14 = (bf16[512,256]{1,0:T(8,128)(2,1)S(1)}, bf16[512,256]{1,0:T(8,128)(2,1)S(1)}, u32[]{:S(2)}, u32[]{:S(2)}) collective-permute-start(bf16[512,256]{1,0:T(8,128)(2,1)S(1)} %get-tuple-element.242), channel_id=1, source_target_pairs={{0,2},{1,3},{2,0},{3,1},{4,6},{5,7},{6,4},{7,5},{8,10},{9,11},{10,... | collective-permute-start | bytes 786440 | tf_op jit(solution)/shard_map/ppermute | solution.py:866
  31.0 3.5 %far.8 = (bf16[8192,256]{1,0:T(8,128)(2,1)S(1)}, bf16[8192,512]{1,0:T(8,128)(2,1)}, bf16[2048,512]{1,0:T(8,128)(2,1)}, f32[272,512]{1,0:T(8,128)S(1)}, bf16[4608...) custom-call(s32[8,128]{1,0:T(8,128)S(1)} %get-tuple-element.543.boun, ...), custom_call_target="tpu_custom_call", output_to_operand_aliasing={{0}: (9, {}), {1}: (10, {}), {2}: (11, {}), {3}: (12, {}), ... | custom-call | flops 1 | bytes 1 | tf_op jit(solution)/shard_map/far/pallas_call | solution.py:621
  34.5 2.1 %collective-permute-start.18 = (bf16[512,256]{1,0:T(8,128)(2,1)S(1)}, bf16[512,256]{1,0:T(8,128)(2,1)S(1)}, u32[]{:S(2)}, u32[]{:S(2)}) collective-permute-start(bf16[512,256]{1,0:T(8,128)(2,1)S(1)} %get-tuple-element.270), channel_id=1, source_target_pairs={{0,2},{1,3},{2,0},{3,1},{4,6},{5,7},{6,4},{7,5},{8,10},{9,11},{10,... | collective-permute-start | bytes 786440 | tf_op jit(solution)/shard_map/ppermute | solution.py:866
  36.7 1.4 %collective-permute-done.14.refs_1_ = bf16[512,256]{1,0:T(8,128)(2,1)S(1)} collective-permute-done((bf16[512,256]{1,0:T(8,128)(2,1)S(1)}, bf16[512,256]{1,0:T(8,128)(2,1)S(1)}, u32[]{:S(2)}, u32[]{:S(2)}) %collective-permute-start.14) | collective-permute-done | bytes 262176 | tf_op jit(solution)/shard_map/ppermute | solution.py:866
  38.0 2.7 %far.9 = (bf16[8192,256]{1,0:T(8,128)(2,1)S(1)}, bf16[8192,512]{1,0:T(8,128)(2,1)}, bf16[2048,512]{1,0:T(8,128)(2,1)}, f32[272,512]{1,0:T(8,128)S(1)}, bf16[4608...) custom-call(s32[8,128]{1,0:T(8,128)S(1)} %get-tuple-element.543.boun, ...), custom_call_target="tpu_custom_call", output_to_operand_aliasing={{0}: (9, {}), {1}: (10, {}), {2}: (11, {}), {3}: (12, {}), ... | custom-call | flops 1 | bytes 1 | tf_op jit(solution)/shard_map/far/pallas_call | solution.py:621
  40.7 2.1 %collective-permute-start.17 = (bf16[512,256]{1,0:T(8,128)(2,1)S(1)}, bf16[512,256]{1,0:T(8,128)(2,1)S(1)}, u32[]{:S(2)}, u32[]{:S(2)}) collective-permute-start(bf16[512,256]{1,0:T(8,128)(2,1)S(1)} %get-tuple-element.269), channel_id=1, source_target_pairs={{0,2},{1,3},{2,0},{3,1},{4,6},{5,7},{6,4},{7,5},{8,10},{9,11},{10,... | collective-permute-start | bytes 786440 | tf_op jit(solution)/shard_map/ppermute | solution.py:866
  42.8 1.3 %merge.3.refs_8_ = bf16[8192,512]{1,0:T(8,128)(2,1)} custom-call(bf16[2048,512]{1,0:T(8,128)(2,1)S(1)} %collective-permute-done.15.lox_ref, bf16[8192,512]{1,0:T(8,128)(2,1)} %get-tuple-element.262.lo_in), custom_call_target="tpu_custom_call", output_to_operand_aliasing={{}: (1, {})} | custom-call | flops 1 | bytes 1 | tf_op jit(solution)/shard_map/merge/pallas_call | solution.py:736
  44.2 2.8 %far.10 = (bf16[8192,256]{1,0:T(8,128)(2,1)S(1)}, bf16[8192,512]{1,0:T(8,128)(2,1)}, bf16[2048,512]{1,0:T(8,128)(2,1)}, f32[272,512]{1,0:T(8,128)S(1)}, bf16[460...) custom-call(s32[8,128]{1,0:T(8,128)S(1)} %get-tuple-element.543.boun, ...), custom_call_target="tpu_custom_call", output_to_operand_aliasing={{0}: (9, {}), {1}: (10, {}), {2}: (11, {}), {3}: (12, {}), ... | custom-call | flops 1 | bytes 1 | tf_op jit(solution)/shard_map/far/pallas_call | solution.py:621
  47.0 1.6 %collective-permute-start.16 = (bf16[512,256]{1,0:T(8,128)(2,1)S(1)}, bf16[512,256]{1,0:T(8,128)(2,1)S(1)}, u32[]{:S(2)}, u32[]{:S(2)}) collective-permute-start(bf16[512,256]{1,0:T(8,128)(2,1)S(1)} %get-tuple-element.268), channel_id=1, source_target_pairs={{0,2},{1,3},{2,0},{3,1},{4,6},{5,7},{6,4},{7,5},{8,10},{9,11},{10,... | collective-permute-start | bytes 786440 | tf_op jit(solution)/shard_map/ppermute | solution.py:866
  48.6 2.2 %unlocal.1.refs_6_ = bf16[4096,256]{1,0:T(8,128)(2,1)S(1)} custom-call(s32[8,128]{1,0:T(8,128)S(1)} %get-tuple-element.543.bounds.mine.refs_0_, s32[16,256]{1,0:T(8,128)S(1)} %get-tuple-element.233.row_ref, bf16[2,2320,256]{2,1,0:T(8,128)(2,1)S(1)} %get-tuple-element.271.gbuf), custom_call_target="tpu_custom_call" | custom-call | flops 1 | bytes 1 | tf_op jit(solution)/shard_map/unlocal/pallas_call | solution.py:458
  50.9 1.3 %copy-done.5 = bf16[4096,256]{1,0:T(8,128)(2,1)} copy-done((bf16[4096,256]{1,0:T(8,128)(2,1)}, bf16[4096,256]{1,0:T(8,128)(2,1)S(1)}, u32[]{:S(2)}) %copy-start.5) | copy-done | bytes 2097176
  52.2 2.7 %collective-permute-done.19.refs_1_ = bf16[512,256]{1,0:T(8,128)(2,1)S(1)} collective-permute-done((bf16[512,256]{1,0:T(8,128)(2,1)S(1)}, bf16[512,256]{1,0:T(8,128)(2,1)S(1)}, u32[]{:S(2)}, u32[]{:S(2)}) %collective-permute-start.19) | collective-permute-done | bytes 262176 | tf_op jit(solution)/shard_map/ppermute | solution.py:866
  54.9 2.4 %far.11 = (bf16[8192,256]{1,0:T(8,128)(2,1)S(1)}, bf16[8192,512]{1,0:T(8,128)(2,1)}, bf16[2048,512]{1,0:T(8,128)(2,1)}, f32[272,512]{1,0:T(8,128)S(1)}, bf16[460...) custom-call(s32[8,128]{1,0:T(8,128)S(1)} %get-tuple-element.543.boun, ...), custom_call_target="tpu_custom_call", output_to_operand_aliasing={{0}: (9, {}), {1}: (10, {}), {2}: (11, {}), {3}: (12, {}), ... | custom-call | flops 1 | bytes 1 | tf_op jit(solution)/shard_map/far/pallas_call | solution.py:621
  57.3 1.5 %far.12 = (bf16[8192,256]{1,0:T(8,128)(2,1)S(1)}, bf16[8192,512]{1,0:T(8,128)(2,1)}, bf16[2048,512]{1,0:T(8,128)(2,1)}, f32[272,512]{1,0:T(8,128)S(1)}, bf16[460...) custom-call(s32[8,128]{1,0:T(8,128)S(1)} %get-tuple-element.543.boun, ...), custom_call_target="tpu_custom_call", output_to_operand_aliasing={{0}: (9, {}), {1}: (10, {}), {2}: (11, {}), {3}: (12, {}), ... | custom-call | flops 1 | bytes 1 | tf_op jit(solution)/shard_map/far/pallas_call | solution.py:621
  58.8 1.7 %collective-permute-done.17.refs_1_ = bf16[512,256]{1,0:T(8,128)(2,1)S(1)} collective-permute-done((bf16[512,256]{1,0:T(8,128)(2,1)S(1)}, bf16[512,256]{1,0:T(8,128)(2,1)S(1)}, u32[]{:S(2)}, u32[]{:S(2)}) %collective-permute-start.17) | collective-permute-done | bytes 262176 | tf_op jit(solution)/shard_map/ppermute | solution.py:866
  60.5 1.6 %far.13 = (bf16[8192,256]{1,0:T(8,128)(2,1)S(1)}, bf16[8192,512]{1,0:T(8,128)(2,1)}, bf16[2048,512]{1,0:T(8,128)(2,1)}, f32[272,512]{1,0:T(8,128)S(1)}, bf16[460...) custom-call(s32[8,128]{1,0:T(8,128)S(1)} %get-tuple-element.543.boun, ...), custom_call_target="tpu_custom_call", output_to_operand_aliasing={{0}: (9, {}), {1}: (10, {}), {2}: (11, {}), {3}: (12, {}), ... | custom-call | flops 1 | bytes 1 | tf_op jit(solution)/shard_map/far/pallas_call | solution.py:621
  62.1 3.5 %collective-permute-done.16.refs_1_ = bf16[512,256]{1,0:T(8,128)(2,1)S(1)} collective-permute-done((bf16[512,256]{1,0:T(8,128)(2,1)S(1)}, bf16[512,256]{1,0:T(8,128)(2,1)S(1)}, u32[]{:S(2)}, u32[]{:S(2)}) %collective-permute-start.16) | collective-permute-done | bytes 262176 | tf_op jit(solution)/shard_map/ppermute | solution.py:866
  65.6 0.8 far.14
  66.4 0.8 collect.2
  67.3 1.6 %collective-permute-start.21 = (bf16[304,128]{1,0:T(8,128)(2,1)S(1)}, bf16[304,128]{1,0:T(8,128)(2,1)S(1)}, u32[]{:S(2)}, u32[]{:S(2)}) collective-permute-start(bf16[304,128]{1,0:T(8,128)(2,1)S(1)} %get-tuple-element.308), channel_id=1, source_target_pairs={{0,4},{4,0},{8,12},{12,8},{16,20},{20,16},{24,28},{28,24},{1,5},{5... | collective-permute-start | bytes 233480 | tf_op jit(solution)/shard_map/ppermute | solution.py:866
  69.2 3.1 %collective-permute-done.21 = bf16[304,128]{1,0:T(8,128)(2,1)S(1)} collective-permute-done((bf16[304,128]{1,0:T(8,128)(2,1)S(1)}, bf16[304,128]{1,0:T(8,128)(2,1)S(1)}, u32[]{:S(2)}, u32[]{:S(2)}) %collective-permute-start.21) | collective-permute-done | bytes 77856 | tf_op jit(solution)/shard_map/ppermute | solution.py:866
  72.3 1.3 %collective-permute-done.22 = bf16[304,128]{1,0:T(8,128)(2,1)S(1)} collective-permute-done((bf16[304,128]{1,0:T(8,128)(2,1)S(1)}, bf16[304,128]{1,0:T(8,128)(2,1)S(1)}, u32[]{:S(2)}, u32[]{:S(2)}) %collective-permute-start.22) | collective-permute-done | bytes 77856 | tf_op jit(solution)/shard_map/ppermute | solution.py:871
  73.6 0.7 flush.1
  74.5 0.9 collective-permute-start.24
  75.3 3.8 %collective-permute-done.24 = bf16[304,128]{1,0:T(8,128)(2,1)S(1)} collective-permute-done((bf16[304,128]{1,0:T(8,128)(2,1)S(1)}, bf16[304,128]{1,0:T(8,128)(2,1)S(1)}, u32[]{:S(2)}, u32[]{:S(2)}) %collective-permute-start.24) | collective-permute-done | bytes 77856 | tf_op jit(solution)/shard_map/ppermute | solution.py:866
  79.2 1.3 %collective-permute-start.25 = (bf16[304,128]{1,0:T(8,128)(2,1)S(1)}, bf16[304,128]{1,0:T(8,128)(2,1)S(1)}, u32[]{:S(2)}, u32[]{:S(2)}) collective-permute-start(bf16[304,128]{1,0:T(8,128)(2,1)S(1)} %add_convert_fusion.10), channel_id=1, source_target_pairs={{0,16},{4,20},{8,24},{12,28},{16,0},{20,4},{24,8},{28,12},{1,17},{... | collective-permute-start | bytes 233480 | tf_op jit(solution)/shard_map/ppermute | solution.py:866
  80.5 5.2 %collective-permute-done.25 = bf16[304,128]{1,0:T(8,128)(2,1)S(1)} collective-permute-done((bf16[304,128]{1,0:T(8,128)(2,1)S(1)}, bf16[304,128]{1,0:T(8,128)(2,1)S(1)}, u32[]{:S(2)}, u32[]{:S(2)}) %collective-permute-start.25) | collective-permute-done | bytes 77856 | tf_op jit(solution)/shard_map/ppermute | solution.py:866
  85.7 2.0 %collective-permute-start.26 = (bf16[304,128]{1,0:T(8,128)(2,1)S(1)}, bf16[304,128]{1,0:T(8,128)(2,1)S(1)}, u32[]{:S(2)}, u32[]{:S(2)}) collective-permute-start(bf16[304,128]{1,0:T(8,128)(2,1)S(1)} %add_convert_fusion.9), channel_id=1, source_target_pairs={{0,2},{1,3},{2,0},{3,1},{4,6},{5,7},{6,4},{7,5},{8,10},{9,11},{10,... | collective-permute-start | bytes 233480 | tf_op jit(solution)/shard_map/ppermute | solution.py:866
  87.8 3.2 %collective-permute-done.26 = bf16[304,128]{1,0:T(8,128)(2,1)S(1)} collective-permute-done((bf16[304,128]{1,0:T(8,128)(2,1)S(1)}, bf16[304,128]{1,0:T(8,128)(2,1)S(1)}, u32[]{:S(2)}, u32[]{:S(2)}) %collective-permute-start.26) | collective-permute-done | bytes 77856 | tf_op jit(solution)/shard_map/ppermute | solution.py:866
  91.1 1.1 collective-permute-start.28
  92.2 0.8 collective-permute-start.29
  94.2 2.9 %merge.4 = bf16[8192,512]{1,0:T(8,128)(2,1)} custom-call(bf16[2048,512]{1,0:T(8,128)(2,1)} %collective-permute-done.23.lox_ref, bf16[8192,512]{1,0:T(8,128)(2,1)} %get-tuple-element.315.lo_in), custom_call_target="tpu_custom_call", output_to_operand_aliasing={{}: (1, {})} | custom-call | flops 1 | bytes 1 | tf_op jit(solution)/shard_map/merge/pallas_call | solution.py:736
  97.1 2.0 %collective-permute-start.32 = (bf16[512,256]{1,0:T(8,128)(2,1)}, bf16[512,256]{1,0:T(8,128)(2,1)}, u32[]{:S(2)}, u32[]{:S(2)}) collective-permute-start(bf16[512,256]{1,0:T(8,128)(2,1)} %get-tuple-element.321), channel_id=1, source_target_pairs={{0,2},{1,3},{2,0},{3,1},{4,6},{5,7},{6,4},{7,5},{8,10},{9,11},{10,... | collective-permute-start | bytes 786440 | tf_op jit(solution)/shard_map/ppermute | solution.py:866
  99.6 2.0 %collective-permute-start.33 = (bf16[512,256]{1,0:T(8,128)(2,1)}, bf16[512,256]{1,0:T(8,128)(2,1)S(1)}, u32[]{:S(2)}, u32[]{:S(2)}) collective-permute-start(bf16[512,256]{1,0:T(8,128)(2,1)} %copy-done.23), channel_id=1, source_target_pairs={{0,2},{1,3},{2,0},{3,1},{4,6},{5,7},{6,4},{7,5},{8,10},{9,11},{10,... | collective-permute-start | bytes 786440 | tf_op jit(solution)/shard_map/ppermute | solution.py:866
  101.6 1.2 copy-done.14
  102.8 1.0 copy-done.16
  103.9 3.5 %finish.1 = (f32[512,512]{1,0:T(8,128)}, f32[1,512]{1,0:T(1,128)}, f32[1,512]{1,0:T(1,128)}, f32[8,512]{1,0:T(8,128)S(1)}, f32[5,256]{1,0:T(8,128)}, /*index=5*/f32[5,256]{1,0:T(8,128)}) custom-call(s32[16]{0:T(128)S(1)} %copy-done.20, f32[5]{0:T(128)S(1)} %copy-done.21, bf16[304,128]{1,0:T(8,128)(2,1)S(1)} %get-tuple-element.668, ...), custom_call_target="tpu_custom_call" | custom-call | flops 1 | bytes 1 | tf_op jit(solution)/shard_map/finish/pallas_call | solution.py:845
  108.0 4.1 %collective-permute-done.31.refs_3_ = bf16[512,256]{1,0:T(8,128)(2,1)S(1)} collective-permute-done((bf16[512,256]{1,0:T(8,128)(2,1)}, bf16[512,256]{1,0:T(8,128)(2,1)S(1)}, u32[]{:S(2)}, u32[]{:S(2)}) %collective-permute-start.31) | collective-permute-done | bytes 262176 | tf_op jit(solution)/shard_map/ppermute | solution.py:866
  112.1 5.3 %collective-permute-done.33.refs_5_ = bf16[512,256]{1,0:T(8,128)(2,1)S(1)} collective-permute-done((bf16[512,256]{1,0:T(8,128)(2,1)}, bf16[512,256]{1,0:T(8,128)(2,1)S(1)}, u32[]{:S(2)}, u32[]{:S(2)}) %collective-permute-start.33) | collective-permute-done | bytes 262176 | tf_op jit(solution)/shard_map/ppermute | solution.py:866
  117.4 1.6 %copy-done.6 = bf16[4096,256]{1,0:T(8,128)(2,1)S(1)} copy-done((bf16[4096,256]{1,0:T(8,128)(2,1)S(1)}, bf16[4096,256]{1,0:T(8,128)(2,1)}, u32[]{:S(2)}) %copy-start.6) | copy-done | bytes 2097176
  119.0 4.2 %unpack.1 = (bf16[4096,256]{1,0:T(8,128)(2,1)}, bf16[4608,256]{1,0:T(8,128)(2,1)S(1)}) custom-call(s32[8,128]{1,0:T(8,128)S(1)} %get-tuple-element.673, s32[8,128]{1,0:T(8,128)S(1)} %get-tuple-element.674, s32[16,256]{1,0:T(8,128)S(1)} %get-tuple-element.319.refs_1_, bf16[512,256]{1,0:T(8,128)(2,1)S(1)} %get-tuple-element.676, ...), custom_call_target="tpu_custom_call", output_to_operand_aliasing={{1}: (8, {})} | custom-call | flops 1 | bytes 1 | tf_op jit(solution)/shard_map/unpack/pallas_call | solution.py:714
  (56 shorter events, 3.3 us)
Async XLA Ops:
  0.6 14.9 %collective-permute-start.13 = (bf16[8192,512]{1,0:T(8,128)(2,1)}, bf16[8192,512]{1,0:T(8,128)(2,1)S(1)}, u32[]{:S(2)}, u32[]{:S(2)}) collective-permute-start(bf16[8192,512]{1,0:T(8,128)(2,1)} %refs_2_.13), channel_id=1, source_target_pairs={{0,1},{1,0},{2,3},{3,2},{4,5},{5,4},{6,7},{7,6},{8,9},{9,8},{10,11... | collective-permute-start | bytes 25165832 | tf_op jit(solution)/shard_map/ppermute | solution.py:866
  4.8 9.9 %collective-permute-start.11 = (bf16[528,256]{1,0:T(8,128)(2,1)S(1)}, bf16[528,256]{1,0:T(8,128)(2,1)S(1)}, u32[]{:S(2)}, u32[]{:S(2)}) collective-permute-start(bf16[528,256]{1,0:T(8,128)(2,1)S(1)} %get-tuple-element.232), channel_id=1, source_target_pairs={{0,2},{1,3},{2,0},{3,1},{4,6},{5,7},{6,4},{7,5},{8,10},{9,11},{10,... | collective-permute-start | bytes 811016 | tf_op jit(solution)/shard_map/ppermute | solution.py:866
  7.4 1.6 %copy-start.13 = (bf16[4096,256]{1,0:T(8,128)(2,1)S(1)}, bf16[4096,256]{1,0:T(8,128)(2,1)}, u32[]{:S(2)}) copy-start(bf16[4096,256]{1,0:T(8,128)(2,1)} %x_ref.1) | copy-start | bytes 6291460
  13.9 0.8 copy-start.15
  15.6 50.0 %copy-start = (bf16[8192,512]{1,0:T(8,128)(2,1)}, bf16[8192,512]{1,0:T(8,128)(2,1)S(1)}, u32[]{:S(2)}) copy-start(bf16[8192,512]{1,0:T(8,128)(2,1)S(1)} %collective-permute-done.13.ctx_ref.refs_3_) | copy-start | bytes 25165828
  24.6 18.2 %collective-permute-start.15 = (bf16[2048,512]{1,0:T(8,128)(2,1)}, bf16[2048,512]{1,0:T(8,128)(2,1)S(1)}, u32[]{:S(2)}, u32[]{:S(2)}) collective-permute-start(bf16[2048,512]{1,0:T(8,128)(2,1)} %get-tuple-element.261), channel_id=1, source_target_pairs={{0,1},{1,0},{2,3},{3,2},{4,5},{5,4},{6,7},{7,6},{8,9},{9,8},{10,11... | collective-permute-start | bytes 6291464 | tf_op jit(solution)/shard_map/ppermute | solution.py:866
  24.9 13.2 %collective-permute-start.14 = (bf16[512,256]{1,0:T(8,128)(2,1)S(1)}, bf16[512,256]{1,0:T(8,128)(2,1)S(1)}, u32[]{:S(2)}, u32[]{:S(2)}) collective-permute-start(bf16[512,256]{1,0:T(8,128)(2,1)S(1)} %get-tuple-element.242), channel_id=1, source_target_pairs={{0,2},{1,3},{2,0},{3,1},{4,6},{5,7},{6,4},{7,5},{8,10},{9,11},{10,... | collective-permute-start | bytes 786440 | tf_op jit(solution)/shard_map/ppermute | solution.py:866
  30.9 13.2 %collective-permute-start.12 = (bf16[512,256]{1,0:T(8,128)(2,1)S(1)}, bf16[512,256]{1,0:T(8,128)(2,1)S(1)}, u32[]{:S(2)}, u32[]{:S(2)}) collective-permute-start(bf16[512,256]{1,0:T(8,128)(2,1)S(1)} %get-tuple-element.238), channel_id=1, source_target_pairs={{0,2},{1,3},{2,0},{3,1},{4,6},{5,7},{6,4},{7,5},{8,10},{9,11},{10,... | collective-permute-start | bytes 786440 | tf_op jit(solution)/shard_map/ppermute | solution.py:866
  34.5 17.7 %collective-permute-start.18 = (bf16[512,256]{1,0:T(8,128)(2,1)S(1)}, bf16[512,256]{1,0:T(8,128)(2,1)S(1)}, u32[]{:S(2)}, u32[]{:S(2)}) collective-permute-start(bf16[512,256]{1,0:T(8,128)(2,1)S(1)} %get-tuple-element.270), channel_id=1, source_target_pairs={{0,2},{1,3},{2,0},{3,1},{4,6},{5,7},{6,4},{7,5},{8,10},{9,11},{10,... | collective-permute-start | bytes 786440 | tf_op jit(solution)/shard_map/ppermute | solution.py:866
  36.6 18.3 %collective-permute-start.19 = (bf16[512,256]{1,0:T(8,128)(2,1)S(1)}, bf16[512,256]{1,0:T(8,128)(2,1)S(1)}, u32[]{:S(2)}, u32[]{:S(2)}) collective-permute-start(bf16[512,256]{1,0:T(8,128)(2,1)S(1)} %get-tuple-element.273), channel_id=1, source_target_pairs={{0,2},{1,3},{2,0},{3,1},{4,6},{5,7},{6,4},{7,5},{8,10},{9,11},{10,... | collective-permute-start | bytes 786440 | tf_op jit(solution)/shard_map/ppermute | solution.py:866
  40.7 19.8 %collective-permute-start.17 = (bf16[512,256]{1,0:T(8,128)(2,1)S(1)}, bf16[512,256]{1,0:T(8,128)(2,1)S(1)}, u32[]{:S(2)}, u32[]{:S(2)}) collective-permute-start(bf16[512,256]{1,0:T(8,128)(2,1)S(1)} %get-tuple-element.269), channel_id=1, source_target_pairs={{0,2},{1,3},{2,0},{3,1},{4,6},{5,7},{6,4},{7,5},{8,10},{9,11},{10,... | collective-permute-start | bytes 786440 | tf_op jit(solution)/shard_map/ppermute | solution.py:866
  47.0 18.6 %collective-permute-start.16 = (bf16[512,256]{1,0:T(8,128)(2,1)S(1)}, bf16[512,256]{1,0:T(8,128)(2,1)S(1)}, u32[]{:S(2)}, u32[]{:S(2)}) collective-permute-start(bf16[512,256]{1,0:T(8,128)(2,1)S(1)} %get-tuple-element.268), channel_id=1, source_target_pairs={{0,2},{1,3},{2,0},{3,1},{4,6},{5,7},{6,4},{7,5},{8,10},{9,11},{10,... | collective-permute-start | bytes 786440 | tf_op jit(solution)/shard_map/ppermute | solution.py:866
  50.9 1.3 %copy-start.5 = (bf16[4096,256]{1,0:T(8,128)(2,1)}, bf16[4096,256]{1,0:T(8,128)(2,1)S(1)}, u32[]{:S(2)}) copy-start(bf16[4096,256]{1,0:T(8,128)(2,1)S(1)} %unlocal.1.refs_6_) | copy-start | bytes 6291460
  58.8 3.3 %copy-start.22 = (bf16[512,256]{1,0:T(8,128)(2,1)}, bf16[512,256]{1,0:T(8,128)(2,1)S(1)}, u32[]{:S(2)}) copy-start(bf16[512,256]{1,0:T(8,128)(2,1)S(1)} %get-tuple-element.320) | copy-start | bytes 786436
  65.6 0.8 copy-start.30
  66.4 7.9 %copy-start.2 = (bf16[8192,256]{1,0:T(8,128)(2,1)}, bf16[8192,256]{1,0:T(8,128)(2,1)S(1)}, u32[]{:S(2)}) copy-start(bf16[8192,256]{1,0:T(8,128)(2,1)S(1)} %get-tuple-element.534) | copy-start | bytes 12582916
  66.4 7.9 %copy-start.23 = (bf16[512,256]{1,0:T(8,128)(2,1)}, bf16[512,256]{1,0:T(8,128)(2,1)S(1)}, u32[]{:S(2)}) copy-start(bf16[512,256]{1,0:T(8,128)(2,1)S(1)} %get-tuple-element.322) | copy-start | bytes 786436
  67.3 1.9 %collective-permute-start.20 = (bf16[304,128]{1,0:T(8,128)(2,1)S(1)}, bf16[304,128]{1,0:T(8,128)(2,1)S(1)}, u32[]{:S(2)}, u32[]{:S(2)}) collective-permute-start(bf16[304,128]{1,0:T(8,128)(2,1)S(1)} %get-tuple-element.307), channel_id=1, source_target_pairs={{0,1},{1,0},{2,3},{3,2},{4,5},{5,4},{6,7},{7,6},{8,9},{9,8},{10,11... | collective-permute-start | bytes 233480 | tf_op jit(solution)/shard_map/ppermute | solution.py:866
  67.3 5.0 %collective-permute-start.21 = (bf16[304,128]{1,0:T(8,128)(2,1)S(1)}, bf16[304,128]{1,0:T(8,128)(2,1)S(1)}, u32[]{:S(2)}, u32[]{:S(2)}) collective-permute-start(bf16[304,128]{1,0:T(8,128)(2,1)S(1)} %get-tuple-element.308), channel_id=1, source_target_pairs={{0,4},{4,0},{8,12},{12,8},{16,20},{20,16},{24,28},{28,24},{1,5},{5... | collective-permute-start | bytes 233480 | tf_op jit(solution)/shard_map/ppermute | solution.py:866
  68.9 4.6 %collective-permute-start.22 = (bf16[304,128]{1,0:T(8,128)(2,1)S(1)}, bf16[304,128]{1,0:T(8,128)(2,1)S(1)}, u32[]{:S(2)}, u32[]{:S(2)}) collective-permute-start(bf16[304,128]{1,0:T(8,128)(2,1)S(1)} %get-tuple-element.309), channel_id=1, source_target_pairs={{0,5},{1,4},{2,7},{3,6},{4,1},{5,0},{6,3},{7,2},{8,13},{9,12},{10,... | collective-permute-start | bytes 233480 | tf_op jit(solution)/shard_map/ppermute | solution.py:871
  74.3 19.9 %collective-permute-start.23 = (bf16[2048,512]{1,0:T(8,128)(2,1)}, bf16[2048,512]{1,0:T(8,128)(2,1)}, u32[]{:S(2)}, u32[]{:S(2)}) collective-permute-start(bf16[2048,512]{1,0:T(8,128)(2,1)} %get-tuple-element.536), channel_id=1, source_target_pairs={{0,1},{1,0},{2,3},{3,2},{4,5},{5,4},{6,7},{7,6},{8,9},{9,8},{10,11... | collective-permute-start | bytes 6291464 | tf_op jit(solution)/shard_map/ppermute | solution.py:866
  74.5 4.7 %collective-permute-start.24 = (bf16[304,128]{1,0:T(8,128)(2,1)S(1)}, bf16[304,128]{1,0:T(8,128)(2,1)S(1)}, u32[]{:S(2)}, u32[]{:S(2)}) collective-permute-start(bf16[304,128]{1,0:T(8,128)(2,1)S(1)} %add_convert_fusion.11), channel_id=1, source_target_pairs={{0,8},{4,12},{8,0},{12,4},{16,24},{20,28},{24,16},{28,20},{1,9},{5... | collective-permute-start | bytes 233480 | tf_op jit(solution)/shard_map/ppermute | solution.py:866
  79.2 6.5 %collective-permute-start.25 = (bf16[304,128]{1,0:T(8,128)(2,1)S(1)}, bf16[304,128]{1,0:T(8,128)(2,1)S(1)}, u32[]{:S(2)}, u32[]{:S(2)}) collective-permute-start(bf16[304,128]{1,0:T(8,128)(2,1)S(1)} %add_convert_fusion.10), channel_id=1, source_target_pairs={{0,16},{4,20},{8,24},{12,28},{16,0},{20,4},{24,8},{28,12},{1,17},{... | collective-permute-start | bytes 233480 | tf_op jit(solution)/shard_map/ppermute | solution.py:866
  85.7 5.4 %collective-permute-start.26 = (bf16[304,128]{1,0:T(8,128)(2,1)S(1)}, bf16[304,128]{1,0:T(8,128)(2,1)S(1)}, u32[]{:S(2)}, u32[]{:S(2)}) collective-permute-start(bf16[304,128]{1,0:T(8,128)(2,1)S(1)} %add_convert_fusion.9), channel_id=1, source_target_pairs={{0,2},{1,3},{2,0},{3,1},{4,6},{5,7},{6,4},{7,5},{8,10},{9,11},{10,... | collective-permute-start | bytes 233480 | tf_op jit(solution)/shard_map/ppermute | solution.py:866
  87.7 11.4 %collective-permute-start.30 = (bf16[512,256]{1,0:T(8,128)(2,1)}, bf16[512,256]{1,0:T(8,128)(2,1)S(1)}, u32[]{:S(2)}, u32[]{:S(2)}) collective-permute-start(bf16[512,256]{1,0:T(8,128)(2,1)} %get-tuple-element.317), channel_id=1, source_target_pairs={{0,2},{1,3},{2,0},{3,1},{4,6},{5,7},{6,4},{7,5},{8,10},{9,11},{10,... | collective-permute-start | bytes 786440 | tf_op jit(solution)/shard_map/ppermute | solution.py:866
  91.0 8.1 %collective-permute-start.27 = (bf16[304,128]{1,0:T(8,128)(2,1)S(1)}, bf16[304,128]{1,0:T(8,128)(2,1)S(1)}, u32[]{:S(2)}, u32[]{:S(2)}) collective-permute-start(bf16[304,128]{1,0:T(8,128)(2,1)S(1)} %add_convert_fusion.8), channel_id=1, source_target_pairs={{0,1},{1,0},{2,3},{3,2},{4,5},{5,4},{6,7},{7,6},{8,9},{9,8},{10,11... | collective-permute-start | bytes 233480 | tf_op jit(solution)/shard_map/ppermute | solution.py:866
  91.1 8.0 %collective-permute-start.28 = (bf16[304,128]{1,0:T(8,128)(2,1)S(1)}, bf16[304,128]{1,0:T(8,128)(2,1)S(1)}, u32[]{:S(2)}, u32[]{:S(2)}) collective-permute-start(bf16[304,128]{1,0:T(8,128)(2,1)S(1)} %add_convert_fusion.8), channel_id=1, source_target_pairs={{0,4},{4,0},{8,12},{12,8},{16,20},{20,16},{24,28},{28,24},{1,5},{5... | collective-permute-start | bytes 233480 | tf_op jit(solution)/shard_map/ppermute | solution.py:866
  92.2 6.9 %collective-permute-start.29 = (bf16[304,128]{1,0:T(8,128)(2,1)S(1)}, bf16[304,128]{1,0:T(8,128)(2,1)S(1)}, u32[]{:S(2)}, u32[]{:S(2)}) collective-permute-start(bf16[304,128]{1,0:T(8,128)(2,1)S(1)} %add_convert_fusion.8), channel_id=1, source_target_pairs={{0,5},{1,4},{2,7},{3,6},{4,1},{5,0},{6,3},{7,2},{8,13},{9,12},{10,... | collective-permute-start | bytes 233480 | tf_op jit(solution)/shard_map/ppermute | solution.py:871
  97.1 10.9 %collective-permute-start.32 = (bf16[512,256]{1,0:T(8,128)(2,1)}, bf16[512,256]{1,0:T(8,128)(2,1)}, u32[]{:S(2)}, u32[]{:S(2)}) collective-permute-start(bf16[512,256]{1,0:T(8,128)(2,1)} %get-tuple-element.321), channel_id=1, source_target_pairs={{0,2},{1,3},{2,0},{3,1},{4,6},{5,7},{6,4},{7,5},{8,10},{9,11},{10,... | collective-permute-start | bytes 786440 | tf_op jit(solution)/shard_map/ppermute | solution.py:866
  99.2 2.4 %copy-start.17 = (f32[5,256]{1,0:T(8,128)S(1)}, f32[5,256]{1,0:T(8,128)}, u32[]{:S(2)}) copy-start(f32[5,256]{1,0:T(8,128)} %refs_8_.1) | copy-start | bytes 15364
  99.2 2.4 %copy-start.18 = (f32[5,256]{1,0:T(8,128)S(1)}, f32[5,256]{1,0:T(8,128)}, u32[]{:S(2)}) copy-start(f32[5,256]{1,0:T(8,128)} %refs_9_.1) | copy-start | bytes 15364
  99.2 2.4 %copy-start.19 = (f32[512]{0:T(512)S(1)}, f32[512]{0:T(512)}, u32[]{:S(2)}) copy-start(f32[512]{0:T(512)} %param.20) | copy-start | bytes 6148
  99.2 2.4 %copy-start.20 = (s32[16]{0:T(128)S(1)}, s32[16]{0:T(128)}, u32[]{:S(2)}) copy-start(s32[16]{0:T(128)} %categories.1) | copy-start | bytes 196
  99.2 2.4 %copy-start.21 = (f32[5]{0:T(128)S(1)}, f32[5]{0:T(128)}, u32[]{:S(2)}) copy-start(f32[5]{0:T(128)} %momentum.1) | copy-start | bytes 64
  99.5 12.6 %collective-permute-start.31 = (bf16[512,256]{1,0:T(8,128)(2,1)}, bf16[512,256]{1,0:T(8,128)(2,1)S(1)}, u32[]{:S(2)}, u32[]{:S(2)}) collective-permute-start(bf16[512,256]{1,0:T(8,128)(2,1)} %copy-done.22), channel_id=1, source_target_pairs={{0,2},{1,3},{2,0},{3,1},{4,6},{5,7},{6,4},{7,5},{8,10},{9,11},{10,... | collective-permute-start | bytes 786440 | tf_op jit(solution)/shard_map/ppermute | solution.py:866
  99.6 17.8 %collective-permute-start.33 = (bf16[512,256]{1,0:T(8,128)(2,1)}, bf16[512,256]{1,0:T(8,128)(2,1)S(1)}, u32[]{:S(2)}, u32[]{:S(2)}) collective-permute-start(bf16[512,256]{1,0:T(8,128)(2,1)} %copy-done.23), channel_id=1, source_target_pairs={{0,2},{1,3},{2,0},{3,1},{4,6},{5,7},{6,4},{7,5},{8,10},{9,11},{10,... | collective-permute-start | bytes 786440 | tf_op jit(solution)/shard_map/ppermute | solution.py:866
  101.6 1.2 copy-start.14
  102.8 1.0 copy-start.16
  117.4 1.6 %copy-start.6 = (bf16[4096,256]{1,0:T(8,128)(2,1)S(1)}, bf16[4096,256]{1,0:T(8,128)(2,1)}, u32[]{:S(2)}) copy-start(bf16[4096,256]{1,0:T(8,128)(2,1)} %copy-done.5) | copy-start | bytes 6291460

commit v2 on v1

v2 whole, which is shorter than its diff:
```python
import functools

import jax
import jax.numpy as jnp
from jax import lax
from jax.experimental import pallas as pl
from jax.experimental.pallas import tpu as pltpu
from jax.sharding import PartitionSpec as P

HID = 253
CATS = 5
BLOCK = 256
TILE = 256
UNIT = 2 * TILE
WIN = BLOCK + 16
LEAD = 4
USUAL = 7
STEPS = 11
FAR = 1 << 20

norm_eps = 1e-06
COSTS = dict(pack=30, prepare=30, local=30, unlocal=0.01, names=30, far=30, last=0.01, flush=0.01, unpack=30, merge=0.01, finish=30, collect=0.01)


def cost(name):
    return pl.CostEstimate(flops=max(1, int(COSTS[name] * 10**9)), bytes_accessed=1, transcendentals=0)


f32, bf16, i32 = jnp.float32, jnp.bfloat16, jnp.int32


def params(mib):
    return pltpu.CompilerParams(vmem_limit_bytes=mib * 1024 * 1024)


def keep(x):
    return pltpu.with_memory_space_constraint(x, pltpu.VMEM)


def stay(x):
    return pltpu.with_memory_space_constraint(x, pltpu.HBM)


def specs(text):
    kinds = {"v": pltpu.VMEM, "s": pltpu.SMEM, "a": pl.ANY}
    return [pl.BlockSpec(memory_space=kinds[c]) for c in text]


def iota(shape, dim):
    return lax.broadcasted_iota(i32, shape, dim)


def units(tiles):
    return (tiles + 1) // 2


def plan_messages(usual, steps):
    tail = [c for c in range(usual, steps, 2)]
    cuts = list(range(0, usual, 2)) + tail + [steps]
    return [(a, b - a) for a, b in zip(cuts, cuts[1:])]


def ceil_to(n, step):
    return -(-n // step) * step


def plan(labels, groups, span):
    rows = labels.shape[0]
    count = len(groups)
    mask = jnp.concatenate([(labels >= g * span) & (labels < (g + 1) * span) for g in groups], axis=0)
    one = jnp.where(mask, 1.0, 0.0)
    m = one.astype(bf16)
    total = count * rows
    upper = jnp.where(iota((BLOCK, BLOCK), 0) <= iota((BLOCK, BLOCK), 1), 1.0, 0.0).astype(bf16)
    cum = jnp.dot(m, upper, preferred_element_type=f32)
    a, b = iota((total, total), 0), iota((total, total), 1)
    lower = jnp.where((a // rows == b // rows) & (b < a), 1.0, 0.0).astype(bf16)
    tot = jnp.sum(one, axis=1, keepdims=True)
    base = jnp.dot(lower, jnp.broadcast_to(tot, (total, 128)).astype(bf16), preferred_element_type=f32)[:, :1]
    lo, hi = base.astype(i32), (base + tot).astype(i32)
    pos = jnp.where(mask, lo + cum.astype(i32) - 1, -FAR)
    tot_row = lax.dot_general(jnp.ones((8, BLOCK), bf16), m, (((1,), (1,)), ((), ())), preferred_element_type=f32)
    base_row = lax.dot_general(tot_row.astype(bf16), lower, (((1,), (1,)), ((), ())), preferred_element_type=f32)
    return pos, lo, hi, base_row.astype(i32), (base_row + tot_row).astype(i32)


def sorted_rows(pos, lo, hi, rows, first, count):
    row, at = None, 0
    for n in range(first, first + count):
        s = slice(n * rows, (n + 1) * rows)
        start = lo[s] // 16 * 16
        r = pos[s] + (at - start)
        row = r if row is None else jnp.maximum(row, r)
        at = at + (hi[s] + 15) // 16 * 16 - start
    return row


def squeeze(pos, labels, group, span):
    rows, lanes = pos.shape
    at = iota((rows, lanes), 0) * lanes + iota((rows, lanes), 1)
    v = jnp.where(pos >= 0, (at - pos) * 16 + (labels - group * span + 1), 0)
    for bit in range((rows * lanes).bit_length() - 1):
        step = 1 << bit
        go = jnp.where(((v >> (4 + bit)) & 1) == 1, v, 0)
        if step < lanes:
            moved = pltpu.roll(go, lanes - step, 1)
            moved = jnp.where(iota((rows, lanes), 1) < lanes - step, moved, pltpu.roll(moved, rows - 1, 0))
        else:
            moved = pltpu.roll(go, rows - step // lanes, 0)
        v = v - go + moved
    return v & 15


def tiles_of(bounds, group, blocks, row=1):
    return (bounds[row, (group + 1) * blocks - 1] + TILE - 1) // TILE


def spans(bounds, groups, blocks, b):
    at, result = 0, []
    for g in groups:
        lo, hi = bounds[0, g * blocks + b], bounds[1, g * blocks + b]
        first = pl.multiple_of(lo // 16 * 16, 16)
        result.append((first, pl.multiple_of(at, 16) if result else 0, lo - first))
        at = at + ((hi + 15) // 16 * 16 - first)
    return result


def window_rows(count, step):
    return ceil_to(BLOCK + 30 * count, step)


def sort_rows(bounds, row_ref, x_ref, groups, blocks, moved, put):
    rows = window_rows(len(groups), 64)
    for b in range(blocks):
        hot = jnp.where(iota((rows, BLOCK), 0) == row_ref[b : b + 1, :], 1.0, 0.0).astype(bf16)
        out = jnp.dot(hot, x_ref[b * BLOCK : (b + 1) * BLOCK, :], preferred_element_type=f32).astype(bf16)
        moved[b * rows : (b + 1) * rows, :] = out
    moved[blocks * rows :, :] = jnp.zeros((moved.shape[0] - blocks * rows, moved.shape[1]), bf16)
    for n in range(len(groups)):
        for b in range(blocks):
            first, at, over = spans(bounds, groups, blocks, b)[n]
            dst, start = put(n, first)
            at = at + b * rows
            old = dst[pl.ds(start, 16), :]
            new = moved[pl.ds(pl.multiple_of(at, 16), 16), :]
            dst[pl.ds(start, 16), :] = jnp.where(iota((16, 1), 0) < over, old, new)
            rest = pl.ds(pl.multiple_of(start + 16, 16), BLOCK)
            dst[rest, :] = moved[pl.ds(pl.multiple_of(at + 16, 16), BLOCK), :]


def unsort_rows(bounds, row_ref, groups, blocks, pick, moved, emit):
    rows = window_rows(len(groups), 128)
    for b in range(blocks):
        moved[b * rows + WIN : (b + 1) * rows, :] = jnp.zeros((rows - WIN, moved.shape[1]), bf16)
        for n, (first, at, _) in enumerate(spans(bounds, groups, blocks, b)):
            moved[pl.ds(pl.multiple_of(at + b * rows, 16), WIN), :] = pick(n, first, WIN)
    for b in range(blocks):
        hot = jnp.where(iota((rows, BLOCK), 0) == row_ref[b : b + 1, :], 1.0, 0.0).astype(bf16)
        emit(b, jnp.dot(jnp.transpose(hot), moved[b * rows : (b + 1) * rows, :], preferred_element_type=f32))


def layer_tile(x, named, ct, wp_ref, wpt_ref, cb_ref, gw_ref, span):
    rows = x.shape[0]
    col = jnp.transpose(jnp.broadcast_to(named.astype(f32), (8, rows)))[:, :1]
    pre = jnp.dot(x, wp_ref[...], preferred_element_type=f32)
    add = cb_ref[0:1, :]
    for s in range(1, span):
        add = jnp.where(col == s + 1.0, cb_ref[s : s + 1, :], add)
    pre = pre + add
    valid = col > 0.0
    e = jnp.exp(-jnp.abs(pre))
    u = 1.0 + e
    r = 1.0 / u
    soft = jnp.maximum(pre, 0.0) + jnp.where(e < 2.0**-12, e, jnp.log(u))
    sig = jnp.where(pre >= 0.0, r, e * r)
    lo = jnp.where(valid, soft, 0.0).astype(bf16)
    gp = jnp.where(valid, ct.astype(f32) * sig, 0.0).astype(bf16)
    gx = jnp.dot(gp, wpt_ref[...], preferred_element_type=f32).astype(bf16)
    sel = jnp.where(jnp.broadcast_to(named, (16, rows)) == iota((16, rows), 0) + 1, 1.0, 0.0).astype(bf16)
    left = jnp.concatenate([jnp.transpose(x), sel], axis=0)
    gw_ref[...] += jnp.dot(left, gp, preferred_element_type=f32)
    return lo, gx


def pack_kernel(oct_count, sizes, shape_axis, oct_axis, span, cap, octants_hbm, ids_hbm, x_hbm, ct_hbm, *refs):
    far = oct_count // 2 - 1
    octants_ref, ids_ref, in_sem, ct_sem = refs[-4:]
    refs = refs[:-4]
    ct_near, ct_far, x_ref, refs = *refs[:3], refs[3:]
    other = lax.axis_index(oct_axis) ^ 1
    blocks_out = []
    for k in range(oct_count // 2):
        there = ct_hbm.at[pl.ds(pl.multiple_of((other ^ (2 * k)) * cap, cap), cap), :]
        here = ct_far.at[pl.ds((k - 1) * cap, cap), :] if k else ct_near
        blocks_out.append(pltpu.make_async_copy(there, here, ct_sem.at[k]))
    fetches = [
        pltpu.make_async_copy(a, b, in_sem.at[i])
        for i, (a, b) in enumerate(zip((octants_hbm, ids_hbm, x_hbm), (octants_ref, ids_ref, x_ref)))
    ]
    for f in fetches + blocks_out:
        f.start()
    heads, refs = refs[: 2 * far], refs[2 * far :]
    queues, rows_far, refs = refs[:far], refs[far : 2 * far], refs[2 * far :]
    row_near, bounds_ref, names_ref, info_ref, moved, bounds_v, bounds, sem = refs
    blocks = row_near.shape[0]
    me = lax.axis_index(oct_axis)
    first_shape = lax.axis_index(shape_axis) * span

    def wide(ref):
        return jnp.concatenate([ref[pl.ds(h, blocks, 2), :] for h in range(2)], axis=1)

    for f in fetches[:2]:
        f.wait()
    ids = wide(ids_ref) - first_shape
    labels = (wide(octants_ref) ^ me) * span + ids
    pos, lo, hi, first_row, last_row = plan(labels, range(oct_count), span)
    n = oct_count * blocks
    bounds_v[...] = jnp.zeros(bounds_v.shape, i32)
    bounds_v[0:1, :n] = first_row[:1]
    bounds_v[1:2, :n] = last_row[:1]
    bounds_ref[...] = bounds_v[...]
    copy = pltpu.make_async_copy(bounds_v, bounds, sem)
    copy.start()
    row_near[...] = sorted_rows(pos, lo, hi, blocks, 0, 2)
    for k in range(far):
        rows_far[k][...] = sorted_rows(pos, lo, hi, blocks, 2 + 2 * k, 2)
    tiles = cap // TILE
    names_ref[...] = jnp.zeros(names_ref.shape, i32)
    for g in range(2):
        names_ref[g * 8 : g * 8 + tiles, :] = squeeze(pos[g * blocks : (g + 1) * blocks], labels, g, span)[:tiles]

    info_ref[...] = jnp.zeros(info_ref.shape, f32)
    for s in range(span):
        number = jnp.sum(jnp.sum(jnp.where(ids == s, 1.0, 0.0), axis=1, keepdims=True), axis=0, keepdims=True)
        info_ref[s : s + 1, :] = jnp.broadcast_to(number, (1, 128))

    for k in range(far):
        queues[k][...] = jnp.zeros(queues[k].shape, bf16)
    copy.wait()
    fetches[2].wait()
    for k in range(far):
        groups = [2 + 2 * k, 3 + 2 * k]
        cut = tiles_of(bounds, groups[0], blocks) * TILE
        sort_rows(bounds, rows_far[k], x_ref, groups, blocks, moved,
                  lambda n, first: (queues[k], pl.multiple_of(first + n * cut, 16)))
        heads[2 * k][: sizes[0], :] = queues[k][: sizes[0], :]
        heads[2 * k][sizes[0] :, :] = labels.astype(f32).astype(bf16)
        heads[2 * k + 1][...] = queues[k][sizes[0] : sizes[0] + sizes[1], :]
    for f in blocks_out:
        f.wait()


def pack(octants, ids, points, cotangent, messages, oct_count, span, cap):
    count, width = points.shape
    blocks = count // BLOCK
    far = oct_count // 2 - 1
    shape = jax.ShapeDtypeStruct
    sizes = [n * UNIT for _, n in messages[:2]]
    heads = [pltpu.VMEM((sizes[0] + blocks, width), bf16), pltpu.VMEM((sizes[1], width), bf16)] * far
    cols = cotangent.shape[1]
    outs = [pltpu.VMEM((cap, cols), bf16), pltpu.VMEM((far * cap, cols), bf16), pltpu.VMEM(points.shape, bf16)] + heads + [pltpu.VMEM((4 * cap, width), bf16)] * far
    outs += [shape((blocks, BLOCK), i32)] * (far + 1)
    outs += [shape((8, 128), i32), shape((16, BLOCK), i32), shape((8, 128), f32)]
    out = pl.pallas_call(
        functools.partial(pack_kernel, oct_count, sizes, "shape", "oct", span, cap),
        in_specs=specs("aaaa"),
        out_specs=specs("v" * len(outs)),
        out_shape=outs,
        scratch_shapes=[
            pltpu.VMEM((blocks * window_rows(2, 64) + WIN, width), bf16),
            pltpu.VMEM((8, 128), i32),
            pltpu.SMEM((8, 128), i32),
            pltpu.SemaphoreType.DMA,
            pltpu.VMEM((count // 128, 128), i32),
            pltpu.VMEM((count // 128, 128), i32),
            pltpu.SemaphoreType.DMA((3,)),
            pltpu.SemaphoreType.DMA((oct_count // 2,)),
        ],
        compiler_params=params(16),
        cost_estimate=cost("pack"),
        name="pack",
    )(stay(octants.reshape(-1, 128)), stay(ids.reshape(-1, 128)), stay(points), stay(cotangent))
    x, out = out[:3], out[3:]
    heads, queues, rows_far, out = out[: 2 * far], out[2 * far : 3 * far], out[3 * far : 4 * far], out[4 * far :]
    return x, heads, queues, rows_far, out


def set_weights(hid, direction_ref, gain_ref, bias_ref, codes_ref, wp_ref, wpt_ref, w_ref, cb_ref, norm_ref):
    direction = direction_ref[...]
    norms = jnp.sqrt(jnp.sum(direction * direction, axis=0, keepdims=True) + norm_eps)
    weight = (direction * (gain_ref[...] / norms)).astype(bf16)
    norm_ref[...] = norms
    w_ref[...] = weight
    width = wp_ref.shape[0]
    wf = weight.astype(f32)
    last = jnp.where(iota((8, 1), 0) + (width - 8) < hid, wf[width - 8 : width, :], wf[-8:, :])
    wp = jnp.concatenate([wf[: width - 8, :], last], axis=0)
    wp_ref[...] = wp.astype(bf16)
    wpt_ref[...] = wp.T.astype(bf16)
    span, code_width = codes_ref.shape
    w_code = wf[hid : hid + code_width, :].astype(bf16)
    codes = jnp.concatenate([codes_ref[...].astype(f32), jnp.zeros((8 - span, code_width), f32)], axis=0).astype(bf16)
    cb_ref[...] = jnp.dot(codes, w_code, preferred_element_type=f32) + bias_ref[...]


def prepare_kernel(oct_count, oct_axis, cap, bounds, row_ref, x_ref, codes_v, direction_hbm, gain_hbm, bias_hbm,
                   lo_hbm, lon_hbm, gw_ref, buf, wp_ref, wpt_ref, w_ref, cb_ref, norm_ref, direction_v, gain_v,
                   moved, zero, bias_v, zero_sem, in_sem):
    blocks = row_ref.shape[0]
    tiles = cap // TILE
    source = lax.axis_index(oct_axis)
    cut = [tiles_of(bounds, r, blocks) for r in range(2)]
    fetches = [
        pltpu.make_async_copy(a, b, in_sem.at[i])
        for i, (a, b) in enumerate(((direction_hbm, direction_v), (gain_hbm, gain_v), (bias_hbm, bias_v)))
    ]
    for f in fetches:
        f.start()

    def clear(go):
        for t in range(tiles):
            @pl.when(t >= cut[0])
            def _():
                at = source * cap + t * TILE
                go(pltpu.make_async_copy(zero, lo_hbm.at[pl.ds(pl.multiple_of(at, TILE), TILE), :], zero_sem))

            @pl.when(t >= cut[1])
            def _():
                go(pltpu.make_async_copy(zero, lon_hbm.at[pl.ds(t * TILE, TILE), :], zero_sem))

    zero[...] = jnp.zeros(zero.shape, bf16)
    clear(lambda c: c.start())
    gw_ref[...] = jnp.zeros(gw_ref.shape, f32)
    buf[...] = jnp.zeros(buf.shape, bf16)
    sort_rows(bounds, row_ref, x_ref, [0, 1], blocks, moved,
              lambda n, first: (buf, pl.multiple_of(first + n * cut[0] * TILE, 16)))
    for f in fetches:
        f.wait()
    set_weights(HID, direction_v, gain_v, bias_v, codes_v, wp_ref, wpt_ref, w_ref, cb_ref, norm_ref)
    clear(lambda c: c.wait())


def prepare(bounds, row, points, direction, gain, bias, codes, oct_count, cap):
    width = points.shape[1]
    ins, outs = direction.shape
    blocks = row.shape[0]
    return pl.pallas_call(
        functools.partial(prepare_kernel, oct_count, "oct", cap),
        in_specs=specs("svvvaaa"),
        out_specs=specs("aavvvvvvvvv"),
        out_shape=[
            pltpu.HBM((oct_count * cap, outs), bf16),
            pltpu.HBM((cap, outs), bf16),
            pltpu.VMEM((width + 16, outs), f32),
            pltpu.VMEM((2 * cap + BLOCK + WIN, width), bf16),
            pltpu.VMEM((width, outs), bf16),
            pltpu.VMEM((outs, width), bf16),
            pltpu.VMEM((ins, outs), bf16),
            pltpu.VMEM((8, outs), f32),
            pltpu.VMEM((1, outs), f32),
            pltpu.VMEM((ins, outs), f32),
            pltpu.VMEM((1, outs), f32),
        ],
        scratch_shapes=[
            pltpu.VMEM((blocks * window_rows(2, 64) + WIN, width), bf16),
            pltpu.VMEM((TILE, outs), bf16),
            pltpu.VMEM((1, outs), f32),
            pltpu.SemaphoreType.DMA,
            pltpu.SemaphoreType.DMA((3,)),
        ],
        compiler_params=params(14),
        cost_estimate=cost("prepare"),
        name="prepare",
    )(bounds, row, keep(points), codes, stay(direction), stay(gain[None, :]), stay(bias[None, :]))


class Rows:
    def __init__(self, bounds, cut, source, cap, place):
        self.cut, self.source, self.cap, self.place = cut, source, cap, place
        self.count = cut[0] + cut[1]

    def split(self, unit, i):
        t = unit * 2 + i
        second = (t >= self.cut[0]).astype(i32)
        return t, second, t - second * self.cut[0]

    def live(self, unit):
        return unit * 2 < self.count

    def move(self, unit, own, other, other_at, mine, mine_at, sem, out, go):
        for i in range(2):
            t, second, slot = self.split(unit, i)
            here = mine.at[pl.ds(mine_at + i * TILE, TILE), :]

            def one(array, row):
                there = array.at[pl.ds(pl.multiple_of(row + slot * TILE, TILE), TILE), :]
                go(pltpu.make_async_copy(here, there, sem) if out else pltpu.make_async_copy(there, here, sem))

            @pl.when((t < self.count) & (second == 0))
            def _():
                one(own, self.source * self.cap)

            @pl.when((t < self.count) & (second == 1))
            def _():
                one(other, other_at)

    def fetch(self, unit, ct, ctx, mine, at, sem, go):
        self.move(unit, ct, ctx, self.place * self.cap, mine, at, sem, False, go)

    def store(self, unit, lo, lox, mine, at, sem, go):
        self.move(unit, lo, lox, self.place * self.cap, mine, at, sem, True, go)

    def names(self, unit, names_ref):
        rows = []
        for i in range(2):
            t, second, slot = self.split(unit, i)
            row = names_ref[pl.ds(jnp.minimum(second * 8 + slot, names_ref.shape[0] - 1), 1), :]
            rows.append(jnp.where(t < self.count, row, 0))
        return jnp.concatenate(rows, axis=1)


def go_start(copy):
    copy.start()


def go_wait(copy):
    copy.wait()


def local_kernel(oct_axis, far, blocks, span, cap, bounds, *refs):
    names_ref, ct_hbm, ctx_ref, wp_ref, wpt_ref, cb_ref, lo_in, lon_in, gw_in, buf_in, refs = *refs[:10], refs[10:]
    lo_hbm, lon_hbm, lof_hbm, gw_ref, buf, refs = *refs[:5], refs[5:]
    ct_v, lo_v, zero, ct_sem, lo_sem, zero_sem = refs
    source = lax.axis_index(oct_axis)
    near = Rows(bounds, [tiles_of(bounds, r, blocks) for r in range(2)], source, cap, 0)
    count = units(near.count)

    def clear(go):
        for k in range(1, far + 1):
            for t in range(cap // TILE):
                at = (source ^ (2 * k)) * cap + t * TILE
                go(pltpu.make_async_copy(zero, lo_hbm.at[pl.ds(pl.multiple_of(at, TILE), TILE), :], zero_sem))
        for t in range(lof_hbm.shape[0] // TILE):
            go(pltpu.make_async_copy(zero, lof_hbm.at[pl.ds(t * TILE, TILE), :], zero_sem))

    @pl.when(count > 0)
    def _():
        near.fetch(0, ct_hbm, ctx_ref, ct_v.at[0], 0, ct_sem.at[0], go_start)

    zero[...] = jnp.zeros(zero.shape, bf16)
    clear(go_start)

    def step(i, carry):
        slot = i % 2

        @pl.when(i + 1 < count)
        def _():
            near.fetch(i + 1, ct_hbm, ctx_ref, ct_v.at[1 - slot], 0, ct_sem.at[1 - slot], go_start)

        near.fetch(i, ct_hbm, ctx_ref, ct_v.at[slot], 0, ct_sem.at[slot], go_wait)

        @pl.when(i >= 2)
        def _():
            near.store(i - 2, lo_hbm, lon_hbm, lo_v.at[slot], 0, lo_sem.at[slot], go_wait)

        at = pl.ds(pl.multiple_of(i * UNIT, UNIT), UNIT)
        lo, gx = layer_tile(buf[at, :], near.names(i, names_ref), ct_v[slot], wp_ref, wpt_ref, cb_ref, gw_ref, span)
        lo_v[slot] = lo
        buf[at, :] = gx
        near.store(i, lo_hbm, lon_hbm, lo_v.at[slot], 0, lo_sem.at[slot], go_start)
        return carry

    lax.fori_loop(0, count, step, 0)
    for back in (2, 1):
        @pl.when(count >= back)
        def _():
            slot = (count - back) % 2
            near.store(count - back, lo_hbm, lon_hbm, lo_v.at[slot], 0, lo_sem.at[slot], go_wait)

    clear(go_wait)


def local(bounds, names, cotangent, ctx, weights, lo, lon, gw, buf, far, blocks, span, cap):
    outs = lo.shape[1]
    return pl.pallas_call(
        functools.partial(local_kernel, "oct", far, blocks, span, cap),
        in_specs=specs("svavvvvaavv"),
        out_specs=specs("aaavv"),
        out_shape=[pltpu.HBM(lo.shape, bf16), pltpu.HBM(lon.shape, bf16), pltpu.HBM((far * cap, outs), bf16),
                   pltpu.VMEM(gw.shape, f32), pltpu.VMEM(buf.shape, bf16)],
        input_output_aliases={7: 0, 8: 1, 9: 3, 10: 4},
        scratch_shapes=[
            pltpu.VMEM((2, UNIT, outs), bf16),
            pltpu.VMEM((2, UNIT, outs), bf16),
            pltpu.VMEM((TILE, outs), bf16),
            pltpu.SemaphoreType.DMA((2,)),
            pltpu.SemaphoreType.DMA((2,)),
            pltpu.SemaphoreType.DMA,
        ],
        compiler_params=params(12),
        cost_estimate=cost("local"),
        name="local",
    )(bounds, names, stay(cotangent), keep(ctx), *[keep(w) for w in weights], stay(lo), stay(lon), keep(gw), keep(buf))


def unlocal_kernel(oct_axis, cap, bounds, row_ref, gbuf, lon_ref, lo_in, part_ref, lo_hbm, moved, sem):
    blocks = row_ref.shape[0]
    join(cap, [0], oct_axis, lon_ref, lo_hbm, sem, go_start)

    def emit(b, rows):
        part_ref[b * BLOCK : (b + 1) * BLOCK, :] = rows.astype(bf16)

    cut = tiles_of(bounds, 0, blocks) * TILE
    unsort_rows(bounds, row_ref, [0, 1], blocks,
                lambda n, first, rows: gbuf[pl.ds(pl.multiple_of(first + n * cut, 16), rows), :], moved, emit)
    join(cap, [0], oct_axis, lon_ref, lo_hbm, sem, go_wait)


def unlocal(bounds, row, gbuf, lon, lo, cap):
    blocks, width = row.shape[0], gbuf.shape[1]
    return pl.pallas_call(
        functools.partial(unlocal_kernel, "oct", cap),
        in_specs=specs("svvva"),
        out_specs=specs("va"),
        out_shape=[pltpu.VMEM((blocks * BLOCK, width), bf16), pltpu.HBM(lo.shape, bf16)],
        input_output_aliases={4: 1},
        scratch_shapes=[pltpu.VMEM((blocks * window_rows(2, 128) + WIN, width), bf16), pltpu.SemaphoreType.DMA((1,))],
        compiler_params=params(16),
        cost_estimate=cost("unlocal"),
        name="unlocal",
    )(bounds, row, keep(gbuf), keep(lon), stay(lo))


def names_kernel(kx, span, cap, labels_ref, names_ref, count_ref, back_ref):
    labels = labels_ref[...].astype(f32).astype(i32)
    blocks = labels.shape[0]
    groups = [2 * kx, 2 * kx + 1]
    pos, _, _, _, last = plan(labels, groups, span)
    tiles = cap // TILE
    names_ref[...] = jnp.zeros(names_ref.shape, i32)
    for n, g in enumerate(groups):
        names_ref[n * 8 : n * 8 + tiles, :] = squeeze(pos[n * blocks : (n + 1) * blocks], labels, g, span)[:tiles]
    count_ref[...] = jnp.zeros(count_ref.shape, i32)
    count_ref[0:1, : 2 * blocks] = last[:1]
    back_ref[...] = jnp.zeros(back_ref.shape, bf16)


def make_names(labels, kx, span, cap):
    return pl.pallas_call(
        functools.partial(names_kernel, kx, span, cap),
        in_specs=specs("v"),
        out_specs=specs("vvv"),
        out_shape=[
            jax.ShapeDtypeStruct((16, BLOCK), i32),
            jax.ShapeDtypeStruct((8, 128), i32),
            pltpu.VMEM((2 * cap + UNIT, labels.shape[1]), bf16),
        ],
        compiler_params=params(8),
        cost_estimate=cost("names"),
        name="names",
    )(labels)


def lead_of(tiles):
    return jnp.maximum(units(tiles), LEAD)


def take_back(place, theirs, blocks, x_ref, at, back):
    n = place - lead_of(tiles_of(theirs, 0, blocks, 0) + tiles_of(theirs, 1, blocks, 0))

    @pl.when((n >= 0) & (n < back.shape[0] // UNIT - 1))
    def _():
        back[pl.ds(pl.multiple_of(n * UNIT, UNIT), UNIT), :] = x_ref[at : at + UNIT, :]


def far_kernel(message, before, after_it, emits, kx, oct_axis, blocks, span, cap, mine, theirs, *refs):
    names_ref, x_ref, ct_hbm, ctx_ref, wp_ref, wpt_ref, cb_ref, queue_in, lo_in, lof_in, gw_in, back_in, refs = *refs[:12], refs[12:]
    if before:
        ct_v, lo_old, refs = *refs[:2], refs[2:]
    queue, lo_hbm, lof_hbm, gw_ref, back, refs = *refs[:5], refs[5:]
    payloads, refs = refs[: len(emits)], refs[len(emits) :]
    if after_it:
        ct_new, refs = refs[0], refs[1:]
    lo_v, refs = refs[0], refs[1:]
    if not before:
        ct_v, refs = refs[0], refs[1:]
    ct_sem, new_sem, lo_sem = refs
    first, number = message
    source = lax.axis_index(oct_axis) ^ (2 * kx)
    rows = Rows(theirs, [tiles_of(theirs, r, blocks, 0) for r in range(2)], source, cap, kx - 1)
    lead = lead_of(tiles_of(mine, 2 * kx, blocks) + tiles_of(mine, 2 * kx + 1, blocks))

    def fetch(u, go):
        if not before:
            rows.fetch(first + u, ct_hbm, ctx_ref, ct_v, u * UNIT, ct_sem.at[u], go)

    def ahead(go):
        if before:
            for u in range(before[1]):
                rows.store(before[0] + u, lo_hbm, lof_hbm, lo_old, u * UNIT, lo_sem, go)
        if after_it:
            for u in range(after_it[1]):
                rows.fetch(after_it[0] + u, ct_hbm, ctx_ref, ct_new, u * UNIT, new_sem, go)

    for u in range(number):
        fetch(u, go_start)
    ahead(go_start)
    for u in range(number):
        take_back(first + u, theirs, blocks, x_ref, u * UNIT, back)
        fetch(u, go_wait)

        @pl.when(rows.live(first + u))
        def _():
            at = slice(u * UNIT, (u + 1) * UNIT)
            lo, gx = layer_tile(x_ref[at, :], rows.names(first + u, names_ref), ct_v[at, :], wp_ref, wpt_ref, cb_ref, gw_ref, span)
            lo_v[at, :] = lo
            queue[pl.ds(pl.multiple_of((lead + first + u) * UNIT, UNIT), UNIT), :] = gx

    for payload, (place, count) in zip(payloads, emits):
        payload[...] = queue[place * UNIT : (place + count) * UNIT, :]
    ahead(go_wait)


def far_step(messages, m, points_in, kx, mine, theirs, names, x, cotangent, ctx, weights, state, ahead, blocks, span, cap):
    wp, wpt, cb = weights
    queue, lo, lof, gw, back = state
    width, outs = wp.shape
    last = points_in[-1] == m
    message, before, after_it = messages[m], (messages[m - 1] if m > 0 else None), (None if last else messages[m + 1])
    emits = messages[m + 2 :] if last else [messages[m + 2]]
    own = (message[1] * UNIT, outs)
    shapes = [pltpu.VMEM(queue.shape, bf16), pltpu.HBM(lo.shape, bf16), pltpu.HBM(lof.shape, bf16), pltpu.VMEM(gw.shape, f32),
              pltpu.VMEM(back.shape, bf16)] + [pltpu.VMEM((count * UNIT, width), bf16) for _, count in emits]
    if after_it:
        shapes.append(pltpu.VMEM((after_it[1] * UNIT, outs), bf16))
    shapes.append(pltpu.VMEM(own, bf16))
    args = [mine, theirs, names, keep(x), stay(cotangent), keep(ctx), keep(wp), keep(wpt), keep(cb), keep(queue), stay(lo),
            stay(lof), keep(gw), keep(back)] + [keep(a) for a in ahead]
    out = pl.pallas_call(
        functools.partial(far_kernel, message, before, after_it, emits, kx, "oct", blocks, span, cap),
        in_specs=specs("ssvvavvvvvaavv" + "v" * len(ahead)),
        out_specs=specs("vaavv" + "v" * (len(shapes) - 5)),
        out_shape=shapes,
        input_output_aliases={9 + i: i for i in range(5)},
        scratch_shapes=([] if before else [pltpu.VMEM(own, bf16)])
        + [pltpu.SemaphoreType.DMA((message[1],)), pltpu.SemaphoreType.DMA, pltpu.SemaphoreType.DMA],
        compiler_params=params(12),
        cost_estimate=cost("last" if last else "far"),
        name="far",
    )(*args)
    return tuple(out[:5]), out[5 : 5 + len(emits)], tuple(out[5 + len(emits) :])


def unpack_kernel(far, blocks, lasts, bounds, *refs):
    theirs, rows_far, refs = refs[:far], refs[far : 2 * far], refs[2 * far :]
    parts, refs = refs[: far * len(lasts)], refs[far * len(lasts) :]
    part_ref, refs = refs[0], refs[1 + far :]
    out_ref, backs, moved = refs[0], refs[1 : 1 + far], refs[-1]
    for k in range(far):
        for j, (first, number) in enumerate(lasts):
            for u in range(number):
                take_back(first + u, theirs[k], blocks, parts[k * len(lasts) + j], u * UNIT, backs[k])
        cut = tiles_of(bounds, 2 + 2 * k, blocks) * TILE

        def pick(n, first, count):
            return backs[k][pl.ds(pl.multiple_of(first + n * cut, 16), count), :]

        def emit(b, value):
            at = slice(b * BLOCK, (b + 1) * BLOCK)
            before = part_ref if k == 0 else out_ref
            out_ref[at, :] = (value + before[at, :].astype(f32)).astype(bf16)

        unsort_rows(bounds, rows_far[k], [2 + 2 * k, 3 + 2 * k], blocks, pick, moved, emit)


def unpack(bounds, theirs, rows_far, lasts, parts, part, backs):
    points, width = part.shape
    blocks = points // BLOCK
    far = len(theirs)
    extra = far * len(lasts)
    return pl.pallas_call(
        functools.partial(unpack_kernel, far, blocks, lasts),
        in_specs=specs("s" + "s" * far + "v" * (2 * far + extra + 1)),
        out_specs=specs("v" * (1 + far)),
        out_shape=[jax.ShapeDtypeStruct(part.shape, bf16)] + [pltpu.VMEM(b.shape, bf16) for b in backs],
        input_output_aliases={2 * far + extra + 2 + k: 1 + k for k in range(far)},
        scratch_shapes=[pltpu.VMEM((blocks * window_rows(2, 128) + WIN, width), bf16)],
        compiler_params=params(20),
        cost_estimate=cost("unpack"),
        name="unpack",
    )(bounds, *theirs, *rows_far, *[keep(x) for x in parts], keep(part), *[keep(b) for b in backs])[0]


def join(cap, kxs, oct_axis, lox_ref, lo_hbm, sem, go):
    other = lax.axis_index(oct_axis) ^ 1
    for n, k in enumerate(kxs):
        at = pl.ds(pl.multiple_of((other ^ (2 * k)) * cap, cap), cap)
        go(pltpu.make_async_copy(lox_ref.at[pl.ds(n * cap, cap), :], lo_hbm.at[at, :], sem.at[n]))


def column_block(axes, n):
    a, b = (lax.axis_index(axis) % 2 for axis in axes)
    return (a ^ (n % 2)) * 2 + (b ^ (n // 2))


def collect_kernel(axes, shape_axis, oct_axis, shapes, span, extra, blocks, cap, message, usual, steps, *refs):
    mine, refs = refs[0], refs[1:]
    theirs, olds, refs = refs[:extra], refs[extra : 2 * extra], refs[2 * extra :]
    gw_ref, info_ref, codes_ref, lo_in, lof_in, outs, lo_hbm, lof_hbm, full, sem = *refs[:5], refs[5:9], *refs[9:]
    source = lax.axis_index(oct_axis)

    def store(go):
        for k in range(extra):
            rows = Rows(theirs[k], [tiles_of(theirs[k], r, blocks, 0) for r in range(2)], source ^ (2 * k + 2), cap, k)
            for u in range(message[1]):
                rows.store(message[0] + u, lo_hbm, lof_hbm, olds[k], u * UNIT, sem, go)

    store(go_start)
    width = gw_ref.shape[0] - 16
    cols = gw_ref.shape[1]
    code_width = codes_ref.shape[1]
    base = lax.axis_index(shape_axis) * span
    full[:width, :] = gw_ref[:width, :]
    ps = jnp.zeros((shapes, cols), f32)
    for s in range(span):
        ps = ps + jnp.where(iota((shapes, 1), 0) == base + s, gw_ref[width + s : width + s + 1, :], 0.0)
    full[width : width + shapes, :] = ps
    lane = iota((1, cols - code_width), 1)
    info = jnp.zeros((shapes, cols), f32)
    for s in range(span):
        number = info_ref[s : s + 1, :1]
        high = jnp.floor(number / 1024.0)
        mid = jnp.floor((number - 1024.0 * high) / 32.0)
        low = number - 1024.0 * high - 32.0 * mid
        digits = jnp.where(lane < 64, low, jnp.where(lane < 128, mid, high))
        code = jnp.where(lax.axis_index(oct_axis) == 0, codes_ref[s : s + 1, :].astype(f32), 0.0)
        info = info + jnp.where(iota((shapes, 1), 0) == base + s, jnp.concatenate([code, digits], axis=1), 0.0)
    full[width + shapes : width + 2 * shapes, :] = info
    flag = jnp.int32(0)
    for k in range(extra):
        ours = units(tiles_of(mine, 2 + 2 * k, blocks) + tiles_of(mine, 3 + 2 * k, blocks))
        other = units(tiles_of(theirs[k], 0, blocks, 0) + tiles_of(theirs[k], 1, blocks, 0))
        most = jnp.maximum(jnp.maximum(ours, LEAD) + other, jnp.maximum(other, LEAD) + ours)
        flag = flag | ((jnp.maximum(ours, other) > usual) | (most > steps)).astype(i32)
    full[width + 2 * shapes :, :] = jnp.zeros((16, cols), f32) + flag.astype(f32)
    for n in range(4):
        at = pl.ds(pl.multiple_of(column_block(axes, n) * 128, 128), 128)
        outs[n][...] = full[:, at].astype(bf16)
    store(go_wait)


def halves(x):
    high = x.astype(bf16)
    return high, (x - high.astype(f32)).astype(bf16)


def finish_kernel(axes, shape_axis, oct_axis, hid, span, cap, kxs, categories, momentum, *refs):
    lox_ref, lo_in, parts, refs = *refs[:2], refs[2:6], refs[6:]
    direction_ref, gain_ref, norm_ref, w_ref, mean_ref, var_ref, refs = *refs[:6], refs[6:]
    dg_ref, gg_ref, bg_ref, cg_ref, mean_out, var_out, left_ref, lo_hbm, full, sem = refs
    join(cap, kxs, oct_axis, lox_ref, lo_hbm, sem, go_start)
    for n in range(4):
        at = pl.ds(pl.multiple_of(column_block(axes, n) * 128, 128), 128)
        full[:, at] = parts[n][...].astype(f32)
    ins, cols = direction_ref.shape
    cats, code_width = mean_ref.shape
    shapes = (full.shape[0] - 16 - (ins - code_width)) // 2
    width = ins - code_width
    ps = full[width : width + shapes, :]
    info = full[width + shapes : width + 2 * shapes, :]
    codes = info[:, :code_width]
    at = code_width
    number = info[:, at : at + 1] + 32.0 * info[:, at + 64 : at + 65] + 1024.0 * info[:, at + 128 : at + 129]
    for c in range(cats):
        chosen = jnp.zeros((shapes, 1), f32)
        for s in range(shapes):
            chosen = jnp.where((iota((shapes, 1), 0) == s) & (categories[s] == c), 1.0, chosen)
        weight = chosen * number
        count = jnp.sum(weight, axis=0, keepdims=True)
        mean = jnp.sum(weight * codes, axis=0, keepdims=True) / count
        var = jnp.sum(weight * codes * codes, axis=0, keepdims=True) / count - mean * mean
        rate = momentum[c]
        mean_out[c : c + 1, :] = (1.0 - rate) * mean_ref[c : c + 1, :] + rate * mean
        var_out[c : c + 1, :] = (1.0 - rate) * var_ref[c : c + 1, :] + rate * var

    gw = full[:width, :]
    codes_all = jnp.concatenate(
        [jnp.zeros((shapes, hid), f32), codes, jnp.zeros((shapes, ins - hid - code_width), f32)], axis=1
    )
    high, low = halves(ps)
    wg = lax.dot_general(jnp.concatenate([codes_all, codes_all], axis=0).astype(bf16), jnp.concatenate([high, low], axis=0),
                         (((0,), (0,)), ((), ())), preferred_element_type=f32)
    head = jnp.where(iota((width, 1), 0) < hid, gw, wg[:width])
    tail = jnp.where(iota((8, 1), 0) + (width - 8) >= hid, gw[width - 8 :], wg[ins - 8 :])
    wg = jnp.concatenate([head, wg[width : ins - 8], tail], axis=0)
    direction = direction_ref[...]
    norms = norm_ref[...]
    dots = jnp.sum(wg * direction, axis=0, keepdims=True)
    gg_ref[...] = dots / norms
    dg_ref[...] = (gain_ref[...] / norms) * (wg - direction * (dots / (norms * norms)))
    bg_ref[...] = jnp.sum(ps, axis=0, keepdims=True)
    base = lax.axis_index(shape_axis) * span
    own = jnp.zeros((8, cols), f32)
    for s in range(span):
        row = jnp.sum(jnp.where(iota((shapes, 1), 0) == base + s, ps, 0.0), axis=0, keepdims=True)
        own = own + jnp.where(iota((8, 1), 0) == s, row, 0.0)
    both = lax.dot_general(jnp.concatenate(halves(own), axis=0), w_ref[...], (((1,), (1,)), ((), ())), preferred_element_type=f32)
    cg_ref[...] = (both[:8] + both[8:])[:span, hid : hid + code_width]
    left_ref[0] = jnp.max(full[width + 2 * shapes : width + 2 * shapes + 8, :128])
    join(cap, kxs, oct_axis, lox_ref, lo_hbm, sem, go_wait)


def finish(axes, span, cap, kxs, categories, momentum, lox, lo, parts, direction, gain, norms, weight, prev_mean, prev_var):
    ins, outs = direction.shape
    return pl.pallas_call(
        functools.partial(finish_kernel, axes, "shape", "oct", HID, span, cap, kxs),
        in_specs=specs("ssva" + "v" * 10),
        out_specs=specs("v" * 6 + "sa"),
        out_shape=[
            jax.ShapeDtypeStruct((ins, outs), f32),
            jax.ShapeDtypeStruct((1, outs), f32),
            jax.ShapeDtypeStruct((1, outs), f32),
            jax.ShapeDtypeStruct((span, prev_mean.shape[1]), f32),
            jax.ShapeDtypeStruct(prev_mean.shape, f32),
            jax.ShapeDtypeStruct(prev_mean.shape, f32),
            jax.ShapeDtypeStruct((1,), f32),
            pltpu.HBM(lo.shape, bf16),
        ],
        input_output_aliases={3: 7},
        scratch_shapes=[pltpu.VMEM((parts[0].shape[0], outs), f32), pltpu.SemaphoreType.DMA((len(kxs),))],
        compiler_params=params(12),
        cost_estimate=cost("finish"),
        name="finish",
    )(categories, momentum, keep(lox), stay(lo), *[keep(p) for p in parts], keep(direction), keep(gain), keep(norms), keep(weight), prev_mean, prev_var)


def swap(v, axis, k):
    n = lax.axis_size(axis)
    return lax.ppermute(v, axis, [(i, i ^ k) for i in range(n)])


def swap_both(v, k):
    n, m = lax.axis_size("shape"), lax.axis_size("oct")
    return lax.ppermute(v, ("shape", "oct"), [(i, i ^ k) for i in range(n * m)])


def bits(axis, first):
    n = lax.axis_size(axis)
    return [(axis, 1 << j) for j in range(first, n.bit_length() - 1)]


def after(x, *others):
    return lax.optimization_barrier((x, *others))[0]


def quarters_to(parts):
    m = lax.axis_size("oct")
    return [swap(parts[0], "oct", 1), swap(parts[1], "shape", 1), swap_both(parts[2], m + 1)]


def total_quarter(parts, before):
    got = quarters_to(parts[1:])
    v = parts[0].astype(f32) + got[0].astype(f32) + got[1].astype(f32) + after(got[2], *before[0]).astype(f32)
    v = v.astype(bf16)
    yield v
    for n, (axis, k) in enumerate(bits("shape", 1) + bits("oct", 1)):
        v = (v.astype(f32) + after(swap(v, axis, k), *before[n + 1]).astype(f32)).astype(bf16)
        yield v


AXES = ("oct", "shape")


def collect(mine, theirs, olds, gw, info, codes, lo, lof, shapes, blocks, cap, message, usual, steps):
    span = codes.shape[0]
    far = len(theirs)
    rows = gw.shape[0] - 16 + 2 * shapes + 16
    out = pl.pallas_call(
        functools.partial(collect_kernel, AXES, "shape", "oct", shapes, span, far, blocks, cap, message, usual, steps),
        in_specs=specs("s" + "s" * far + "v" * far + "vvvaa"),
        out_specs=specs("vvvvaa"),
        out_shape=[pltpu.VMEM((rows, 128), bf16)] * 4 + [pltpu.HBM(lo.shape, bf16), pltpu.HBM(lof.shape, bf16)],
        input_output_aliases={2 * far + 4: 4, 2 * far + 5: 5},
        scratch_shapes=[pltpu.VMEM((rows, gw.shape[1]), f32), pltpu.SemaphoreType.DMA],
        compiler_params=params(8),
        cost_estimate=cost("collect"),
        name="collect",
    )(mine, *theirs, *[keep(o) for o in olds], keep(gw), info, codes, stay(lo), stay(lof))
    return out[:4], out[4], out[5]


def run(usual, steps, point_inputs, shape_ids, octants, categories, codes, direction, gain, bias, cotangent, prev_mean, prev_var, momentum):
    points, width = point_inputs.shape
    oct_count, shape_dev = lax.axis_size("oct"), lax.axis_size("shape")
    cap = 2 * points // oct_count
    span, code_width = codes.shape
    shapes = shape_dev * span
    blocks = points // BLOCK
    far = list(range(1, oct_count // 2))
    messages = plan_messages(usual, steps)
    points_in = [m for m, (first, _) in enumerate(messages) if first < usual]

    (ct_near, ct_far, x_near), heads, queues, rows_far, (row_near, mine, near_names, info) = pack(
        octants, shape_ids, point_inputs, cotangent, messages, oct_count, span, cap)
    ctn, ctf = swap(ct_near, "oct", 1), swap(ct_far, "oct", 1)
    got = {(k, m): swap(heads[2 * (k - 1) + m], "oct", 2 * k) for k in far for m in range(2)}
    lo, lon, gw, buf, wp, wpt, weight, cb, norms, direction_v, gain_v = prepare(
        mine, row_near, x_near, direction, gain, bias, codes, oct_count, cap)
    weights = (wp, wpt, cb)
    lo, lon, lof, gw, buf = local(mine, near_names, cotangent, ctn, weights, lo, lon, gw, buf, len(far), blocks, span, cap)

    queue = {k: queues[k - 1] for k in far}
    named, theirs, back, ahead = {}, {}, {}, {}
    for k in far:
        named[k], theirs[k], back[k] = make_names(after(got[k, 0], gw)[messages[0][1] * UNIT :], k, span, cap)
        ahead[k] = ()
    for m in points_in:
        for k in far:
            (queue[k], lo, lof, gw, back[k]), payloads, ahead[k] = far_step(
                messages, m, points_in, k, mine, theirs[k], named[k], got[k, m], cotangent, ctf, weights,
                (queue[k], lo, lof, gw, back[k]), ahead[k], blocks, span, cap)
            for j, payload in enumerate(payloads):
                got[k, m + 2 + j] = swap(payload, "oct", 2 * k)
        if m == min(1, points_in[-1] - 1):
            part, lo = unlocal(mine, row_near, after(buf, gw), swap(lon, "oct", 1), lo, cap)
            gw = after(gw, part)
    their = [theirs[k] for k in far]
    lasts = list(range(len(points_in), len(messages)))
    order = ((), (0,), (), (1,)) if usual % 2 else ()
    before = [[got[k, lasts[i]] for k in far for i in ii] for ii in order] + [[] for _ in range(20)]
    parts, lo, lof = collect(mine, their, [ahead[k][-1] for k in far], gw, info, codes, lo, lof, shapes, blocks, cap,
                             messages[points_in[-1]], usual, steps)
    lox = swap(lof, "oct", 1)
    for v in total_quarter(parts, before):
        pass
    parts = [v] + quarters_to([v] * 3)
    input_grad = unpack(mine, their, rows_far, [messages[m] for m in lasts], [got[k, m] for k in far for m in lasts], part,
                        [back[k] for k in far])
    direction_grad, gain_grad, bias_grad, code_grad, running_mean, running_var, left, lo = finish(
        AXES, span, cap, tuple(far), categories, momentum, lox, lo, [after(parts[0], input_grad)] + parts[1:], direction_v, gain_v, norms, weight, prev_mean, prev_var)
    outputs = (
        lo,
        input_grad,
        code_grad,
        direction_grad,
        gain_grad[0],
        bias_grad[0],
        running_mean,
        running_var,
    )
    return outputs, left[0]


def body(*args):
    points, oct_count = args[0].shape[0], lax.axis_size("oct")
    most = units(2 * (2 * points // oct_count) // TILE)
    all_steps = max(most, LEAD) + most
    usual, steps = min(USUAL, most), min(STEPS, all_steps)
    outputs, left = run(usual, steps, *args)
    if (usual, steps) == (most, all_steps):
        return outputs

    def more(carry):
        return jnp.float32(0), run(most, all_steps, *args)[0]

    return lax.while_loop(lambda carry: carry[0] > 0, more, (left, outputs))[1]


def solution(mesh):
    both = P(("shape", "oct"), None)
    in_specs = (both, P(("shape", "oct")), both, P(), P("shape", None), P(), P(), P(), both, P(), P(), P())
    out_specs = (both, both, P("shape", None), P(), P(), P(), P(), P())
    return jax.shard_map(body, mesh=mesh, in_specs=in_specs, out_specs=out_specs, check_vma=False)
```

time: 124 us -> 85.9 us (0.69)
  waiting for transfers between devices: 35.3 us -> 17.1 us
  Pallas kernels: 49.3 us -> 35.3 us
  local copies, waits for them, and re-layouts: 8.76 us -> 0.03 us
  starting transfers between devices: 27.8 us -> 31.7 us
    ppermute x21 -> x17, waiting for transfers between devices: 34.1 us -> 14.9 us  [swap(): return lax.ppermute(v, axis, [(i, i ^ k) for i in range(n)])]
    pallas_call x15 -> x9, Pallas kernels: 42.7 us -> 29.2 us  [the longest x4 9.22 us: far_step(): pl.pallas_call(functools.partial(far_kernel, message, before, after_it, e...]
    unnamed x32 -> x14, local copies, waits for them, and re-layouts: 7.6 us -> 0.03 us
    ppermute x21 -> x17, starting transfers between devices: 26.7 us -> 29.5 us  [swap(): return lax.ppermute(v, axis, [(i, i ^ k) for i in range(n)])]
  transfers between devices with their start and end apart: 23 -> 19, of which waited for: 11 -> 10; matrix products, arithmetic and copies ran while one was open for 1% -> 0% of each run, Pallas kernels for 27% -> 33%
where the time goes in v2:
time: 85.9 us; the launch traced here: 86 us
  Pallas kernels  35.3 us (41%)
  starting transfers between devices  31.7 us (37%)
  waiting for transfers between devices  17.1 us (20%)
  between operations  1.01 us (1%)
    ppermute x17, starting transfers between devices, swap(): return lax.ppermute(v, axis, [(i, i ^ k) for i in range(n)])  29.5 us
    ppermute x17, waiting for transfers between devices, swap(): return lax.ppermute(v, axis, [(i, i ^ k) for i in range(n)])  14.9 us
    pallas_call x4, Pallas kernels, far_step(): pl.pallas_call(functools.partial(far_kernel, message, before, after_it, e...  9.22 us
    pallas_call x1, Pallas kernels, local(): pl.pallas_call(functools.partial(local_kernel, 'oct', far, blocks, span,...  6.52 us
    pallas_call x1, Pallas kernels, prepare(): pl.pallas_call(functools.partial(prepare_kernel, oct_count, 'oct', cap),...  4.36 us
    pallas_call x1, Pallas kernels, unpack(): pl.pallas_call(functools.partial(unpack_kernel, far, blocks, lasts), in_s...  3.86 us
    pallas_call x1, Pallas kernels, finish(): pl.pallas_call(functools.partial(finish_kernel, axes, 'shape', 'oct', HID...  3.73 us
    pallas_call x1, Pallas kernels, pack(): pl.pallas_call(functools.partial(pack_kernel, oct_count, sizes, 'shape',...  3.56 us
  transfers between devices with their start and end apart: 19, of which 10 were waited for; matrix products, arithmetic and copies ran while one was open for 0% of the time, Pallas kernels for 33%

profile of v2, /device:TPU:0, one launch (start us, length us, event | category | flops | bytes accessed | tf_op | source)
XLA Modules:
  0.0 86.0 jit_solution(3408346963478302453)
XLA Ops:
  0.6 0.0 copy-start.6
  0.6 3.6 %pack.3 = (bf16[2048,512]{1,0:T(8,128)(2,1)S(1)}, bf16[2048,512]{1,0:T(8,128)(2,1)S(1)}, bf16[4096,256]{1,0:T(8,128)(2,1)S(1)}, bf16[1040,256]{1,0:T(8,128)(2,1)...) custom-call(s32[32,128]{1,0:T(8,128)} %bitcast.13, ...), custom_call_target="tpu_custom_call" | custom-call | flops 30000001024 | bytes 1 | tf_op jit(solution)/shard_map/pack/pallas_call | solution.py:264
  4.2 0.5 collective-permute-start.22
  4.7 2.6 %collective-permute-start.21 = (bf16[1040,256]{1,0:T(8,128)(2,1)S(1)}, bf16[1040,256]{1,0:T(8,128)(2,1)S(1)}, u32[]{:S(2)}, u32[]{:S(2)}) collective-permute-start(bf16[1040,256]{1,0:T(8,128)(2,1)S(1)} %get-tuple-element.279), channel_id=1, source_target_pairs={{0,2},{1,3},{2,0},{3,1},{4,6},{5,7},{6,4},{7,5},{8,10},{9,11},{10,... | collective-permute-start | bytes 1597448 | tf_op jit(solution)/shard_map/ppermute | solution.py:839
  7.3 0.2 collective-permute-start.24
  7.5 0.3 collective-permute-start.23
  7.7 4.4 %prepare.3 = (bf16[8192,512]{1,0:T(8,128)(2,1)}, bf16[2048,512]{1,0:T(8,128)(2,1)}, f32[272,512]{1,0:T(8,128)S(1)}, bf16[4624,256]{1,0:T(8,128)(2,1)S(1)}, bf16[...) custom-call(s32[8,128]{1,0:T(8,128)S(1)} %get-tuple-element.278.boun, ...), custom_call_target="tpu_custom_call" | custom-call | flops 30000001024 | bytes 1 | tf_op jit(solution)/shard_map/prepare/pallas_call | solution.py:347
  12.1 0.0 collective-permute-done.22.refs_2_
  12.1 6.5 %local.3 = (bf16[8192,512]{1,0:T(8,128)(2,1)}, bf16[2048,512]{1,0:T(8,128)(2,1)}, bf16[2048,512]{1,0:T(8,128)(2,1)}, f32[272,512]{1,0:T(8,128)S(1)}, bf16[4624,256]{1,0:T(8,128)(2,1)S(1)}) custom-call(s32[8,128]{1,0:T(8,128)S(1)} %get-tuple-element.278.bounds.mine.refs_0_, ...), custom_call_target="tpu_custom_call", output_to_operand_aliasing={{0}: (7, {}), {1}: (8, {}), {3}: (9, {}), {4}: (10, {})} | custom-call | flops 30000001024 | bytes 1 | tf_op jit(solution)/shard_map/local/pallas_call | solution.py:485
  18.6 1.6 %collective-permute-done.21.refs_1_ = bf16[1040,256]{1,0:T(8,128)(2,1)S(1)} collective-permute-done((bf16[1040,256]{1,0:T(8,128)(2,1)S(1)}, bf16[1040,256]{1,0:T(8,128)(2,1)S(1)}, u32[]{:S(2)}, u32[]{:S(2)}) %collective-permute-start.21) | collective-permute-done | bytes 532512 | tf_op jit(solution)/shard_map/ppermute | solution.py:839
  20.2 0.9 %names.3 = (s32[16,256]{1,0:T(8,128)S(1)}, s32[8,128]{1,0:T(8,128)S(1)}, bf16[4608,256]{1,0:T(8,128)(2,1)S(1)}) custom-call(bf16[16,256]{1,0:T(8,128)(2,1)S(1)} %slice.6.labels_ref), custom_call_target="tpu_custom_call" | custom-call | flops 30000001024 | bytes 1 | tf_op jit(solution)/shard_map/names/pallas_call | solution.py:549
  21.1 4.5 %far.12 = (bf16[8192,256]{1,0:T(8,128)(2,1)S(1)}, bf16[8192,512]{1,0:T(8,128)(2,1)}, bf16[2048,512]{1,0:T(8,128)(2,1)}, f32[272,512]{1,0:T(8,128)S(1)}, bf16[460...) custom-call(s32[8,128]{1,0:T(8,128)S(1)} %get-tuple-element.278.boun, ...), custom_call_target="tpu_custom_call", output_to_operand_aliasing={{0}: (9, {}), {1}: (10, {}), {2}: (11, {}), {3}: (12, {}), ... | custom-call | flops 30000001024 | bytes 1 | tf_op jit(solution)/shard_map/far/pallas_call | solution.py:639
  25.7 4.3 %collective-permute-start.26 = (bf16[1024,256]{1,0:T(8,128)(2,1)S(1)}, bf16[1024,256]{1,0:T(8,128)(2,1)S(1)}, u32[]{:S(2)}, u32[]{:S(2)}) collective-permute-start(bf16[1024,256]{1,0:T(8,128)(2,1)S(1)} %get-tuple-element.309), channel_id=1, source_target_pairs={{0,2},{1,3},{2,0},{3,1},{4,6},{5,7},{6,4},{7,5},{8,10},{9,11},{10,... | collective-permute-start | bytes 1572872 | tf_op jit(solution)/shard_map/ppermute | solution.py:839
  29.9 1.3 %collective-permute-done.23.refs_1_ = bf16[1024,256]{1,0:T(8,128)(2,1)S(1)} collective-permute-done((bf16[1024,256]{1,0:T(8,128)(2,1)S(1)}, bf16[1024,256]{1,0:T(8,128)(2,1)S(1)}, u32[]{:S(2)}, u32[]{:S(2)}) %collective-permute-start.23) | collective-permute-done | bytes 524320 | tf_op jit(solution)/shard_map/ppermute | solution.py:839
  31.2 2.5 %far.13 = (bf16[8192,256]{1,0:T(8,128)(2,1)S(1)}, bf16[8192,512]{1,0:T(8,128)(2,1)}, bf16[2048,512]{1,0:T(8,128)(2,1)}, f32[272,512]{1,0:T(8,128)S(1)}, bf16[460...) custom-call(s32[8,128]{1,0:T(8,128)S(1)} %get-tuple-element.278.boun, ...), custom_call_target="tpu_custom_call", output_to_operand_aliasing={{0}: (9, {}), {1}: (10, {}), {2}: (11, {}), {3}: (12, {}), ... | custom-call | flops 30000001024 | bytes 1 | tf_op jit(solution)/shard_map/far/pallas_call | solution.py:639
  33.7 3.2 %collective-permute-start.25 = (bf16[512,256]{1,0:T(8,128)(2,1)S(1)}, bf16[512,256]{1,0:T(8,128)(2,1)S(1)}, u32[]{:S(2)}, u32[]{:S(2)}) collective-permute-start(bf16[512,256]{1,0:T(8,128)(2,1)S(1)} %get-tuple-element.308), channel_id=1, source_target_pairs={{0,2},{1,3},{2,0},{3,1},{4,6},{5,7},{6,4},{7,5},{8,10},{9,11},{10,... | collective-permute-start | bytes 786440 | tf_op jit(solution)/shard_map/ppermute | solution.py:839
  36.9 0.0 collective-permute-done.27.lon_ref
  36.9 2.3 %unlocal.3 = (bf16[4096,256]{1,0:T(8,128)(2,1)S(1)}, bf16[8192,512]{1,0:T(8,128)(2,1)}) custom-call(s32[8,128]{1,0:T(8,128)S(1)} %get-tuple-element.278.bounds.mine.refs_0_, s32[16,256]{1,0:T(8,128)S(1)} %get-tuple-element.282.row_ref, bf16[4624,256]{1,0:T(8,128)(2,1)S(1)} %get-tuple-element.313.gbuf, ...), custom_call_target="tpu_custom_call", output_to_operand_aliasing={{1}: (4, {})} | custom-call | flops 10000000 | bytes 1 | tf_op jit(solution)/shard_map/unlocal/pallas_call | solution.py:521
  39.2 3.5 %collective-permute-done.26.refs_1_ = bf16[1024,256]{1,0:T(8,128)(2,1)S(1)} collective-permute-done((bf16[1024,256]{1,0:T(8,128)(2,1)S(1)}, bf16[1024,256]{1,0:T(8,128)(2,1)S(1)}, u32[]{:S(2)}, u32[]{:S(2)}) %collective-permute-start.26) | collective-permute-done | bytes 524320 | tf_op jit(solution)/shard_map/ppermute | solution.py:839
  42.7 1.4 %far.14 = (bf16[8192,256]{1,0:T(8,128)(2,1)S(1)}, bf16[8192,512]{1,0:T(8,128)(2,1)}, bf16[2048,512]{1,0:T(8,128)(2,1)}, f32[272,512]{1,0:T(8,128)S(1)}, bf16[460...) custom-call(s32[8,128]{1,0:T(8,128)S(1)} %get-tuple-element.278.boun, ...), custom_call_target="tpu_custom_call", output_to_operand_aliasing={{0}: (9, {}), {1}: (10, {}), {2}: (11, {}), {3}: (12, {}), ... | custom-call | flops 30000001024 | bytes 1 | tf_op jit(solution)/shard_map/far/pallas_call | solution.py:639
  44.1 4.2 %collective-permute-start.33 = (bf16[1024,256]{1,0:T(8,128)(2,1)S(1)}, bf16[1024,256]{1,0:T(8,128)(2,1)S(1)}, u32[]{:S(2)}, u32[]{:S(2)}) collective-permute-start(bf16[1024,256]{1,0:T(8,128)(2,1)S(1)} %get-tuple-element.341), channel_id=1, source_target_pairs={{0,2},{1,3},{2,0},{3,1},{4,6},{5,7},{6,4},{7,5},{8,10},{9,11},{10,... | collective-permute-start | bytes 1572872 | tf_op jit(solution)/shard_map/ppermute | solution.py:839
  48.3 0.0 collective-permute-done.25.refs_1_
  48.3 0.8 far.15
  49.2 0.8 collect.3
  50.0 2.1 %collective-permute-start.31 = (bf16[304,128]{1,0:T(8,128)(2,1)S(1)}, bf16[304,128]{1,0:T(8,128)(2,1)S(1)}, u32[]{:S(2)}, u32[]{:S(2)}) collective-permute-start(bf16[304,128]{1,0:T(8,128)(2,1)S(1)} %get-tuple-element.340), channel_id=1, source_target_pairs={{0,5},{1,4},{2,7},{3,6},{4,1},{5,0},{6,3},{7,2},{8,13},{9,12},{10,... | collective-permute-start | bytes 233480 | tf_op jit(solution)/shard_map/ppermute | solution.py:844
  52.2 0.8 collective-permute-start.29
  53.0 0.0 collective-permute-start.30
  53.0 1.8 %collective-permute-done.31 = bf16[304,128]{1,0:T(8,128)(2,1)S(1)} collective-permute-done((bf16[304,128]{1,0:T(8,128)(2,1)S(1)}, bf16[304,128]{1,0:T(8,128)(2,1)S(1)}, u32[]{:S(2)}, u32[]{:S(2)}) %collective-permute-start.31) | collective-permute-done | bytes 77856 | tf_op jit(solution)/shard_map/ppermute | solution.py:844
  54.8 0.0 collective-permute-done.29
  54.8 2.6 %collective-permute-done.30 = bf16[304,128]{1,0:T(8,128)(2,1)S(1)} collective-permute-done((bf16[304,128]{1,0:T(8,128)(2,1)S(1)}, bf16[304,128]{1,0:T(8,128)(2,1)S(1)}, u32[]{:S(2)}, u32[]{:S(2)}) %collective-permute-start.30) | collective-permute-done | bytes 77856 | tf_op jit(solution)/shard_map/ppermute | solution.py:839
  57.4 2.0 %collective-permute-start.32 = (bf16[304,128]{1,0:T(8,128)(2,1)S(1)}, bf16[304,128]{1,0:T(8,128)(2,1)S(1)}, u32[]{:S(2)}, u32[]{:S(2)}) collective-permute-start(bf16[304,128]{1,0:T(8,128)(2,1)S(1)} %add_convert_fusion.7), channel_id=1, source_target_pairs={{0,8},{4,12},{8,0},{12,4},{16,24},{20,28},{24,16},{28,20},{1,9},{5... | collective-permute-start | bytes 233480 | tf_op jit(solution)/shard_map/ppermute | solution.py:839
  59.4 2.0 %collective-permute-start.36 = (bf16[1024,256]{1,0:T(8,128)(2,1)S(1)}, bf16[1024,256]{1,0:T(8,128)(2,1)S(1)}, u32[]{:S(2)}, u32[]{:S(2)}) collective-permute-start(bf16[1024,256]{1,0:T(8,128)(2,1)S(1)} %get-tuple-element.343), channel_id=1, source_target_pairs={{0,2},{1,3},{2,0},{3,1},{4,6},{5,7},{6,4},{7,5},{8,10},{9,11},{10,... | collective-permute-start | bytes 1572872 | tf_op jit(solution)/shard_map/ppermute | solution.py:839
  61.5 0.4 collective-permute-done.32
  61.9 0.0 collective-permute-done.33.refs_2_
  61.9 2.9 %collective-permute-start.34 = (bf16[304,128]{1,0:T(8,128)(2,1)S(1)}, bf16[304,128]{1,0:T(8,128)(2,1)S(1)}, u32[]{:S(2)}, u32[]{:S(2)}) collective-permute-start(bf16[304,128]{1,0:T(8,128)(2,1)S(1)} %add_convert_fusion.6), channel_id=1, source_target_pairs={{0,16},{4,20},{8,24},{12,28},{16,0},{20,4},{24,8},{28,12},{1,17},{... | collective-permute-start | bytes 233480 | tf_op jit(solution)/shard_map/ppermute | solution.py:839
  64.8 2.4 %collective-permute-done.34 = bf16[304,128]{1,0:T(8,128)(2,1)S(1)} collective-permute-done((bf16[304,128]{1,0:T(8,128)(2,1)S(1)}, bf16[304,128]{1,0:T(8,128)(2,1)S(1)}, u32[]{:S(2)}, u32[]{:S(2)}) %collective-permute-start.34) | collective-permute-done | bytes 77856 | tf_op jit(solution)/shard_map/ppermute | solution.py:839
  67.3 3.9 %collective-permute-start.35 = (bf16[304,128]{1,0:T(8,128)(2,1)S(1)}, bf16[304,128]{1,0:T(8,128)(2,1)S(1)}, u32[]{:S(2)}, u32[]{:S(2)}) collective-permute-start(bf16[304,128]{1,0:T(8,128)(2,1)S(1)} %add_convert_fusion.5), channel_id=1, source_target_pairs={{0,2},{1,3},{2,0},{3,1},{4,6},{5,7},{6,4},{7,5},{8,10},{9,11},{10,... | collective-permute-start | bytes 233480 | tf_op jit(solution)/shard_map/ppermute | solution.py:839
  71.2 0.0 collective-permute-start.28
  71.2 2.3 %collective-permute-done.36.refs_3_ = bf16[1024,256]{1,0:T(8,128)(2,1)S(1)} collective-permute-done((bf16[1024,256]{1,0:T(8,128)(2,1)S(1)}, bf16[1024,256]{1,0:T(8,128)(2,1)S(1)}, u32[]{:S(2)}, u32[]{:S(2)}) %collective-permute-start.36) | collective-permute-done | bytes 524320 | tf_op jit(solution)/shard_map/ppermute | solution.py:839
  73.5 0.8 collective-permute-done.35
  74.4 0.1 collective-permute-start.37
  74.5 2.5 %collective-permute-start.38 = (bf16[304,128]{1,0:T(8,128)(2,1)S(1)}, bf16[304,128]{1,0:T(8,128)(2,1)S(1)}, u32[]{:S(2)}, u32[]{:S(2)}) collective-permute-start(bf16[304,128]{1,0:T(8,128)(2,1)S(1)} %add_convert_fusion.4.refs_2_), channel_id=1, source_target_pairs={{0,4},{4,0},{8,12},{12,8},{16,20},{20,16},{24,28},{28,24},{1,5},{5... | collective-permute-start | bytes 233480 | tf_op jit(solution)/shard_map/ppermute | solution.py:839
  76.9 0.1 collective-permute-start.39
  77.0 3.9 %unpack.3 = (bf16[4096,256]{1,0:T(8,128)(2,1)}, bf16[4608,256]{1,0:T(8,128)(2,1)S(1)}) custom-call(s32[8,128]{1,0:T(8,128)S(1)} %get-tuple-element.278.bounds.mine.refs_0_, s32[8,128]{1,0:T(8,128)S(1)} %get-tuple-element.293.theirs.refs_1_.refs_0_, s32[16,256]{1,0:T(8,128)S(1)} %get-tuple-element.345.refs_1_, ...), custom_call_target="tpu_custom_call", output_to_operand_aliasing={{1}: (6, {})} | custom-call | flops 30000001024 | bytes 1 | tf_op jit(solution)/shard_map/unpack/pallas_call | solution.py:681
  80.9 0.4 collective-permute-done.39.refs_5_
  81.3 0.0 copy-start.8
  81.3 3.7 %finish.3 = (f32[512,512]{1,0:T(8,128)}, f32[1,512]{1,0:T(1,128)}, f32[1,512]{1,0:T(1,128)}, f32[2,256]{1,0:T(2,128)}, f32[5,256]{1,0:T(8,128)}, /*index=5*/f32[...) custom-call(s32[16]{0:T(128)S(1)} %copy-done.14, f32[5]{0:T(128)S(1)} %copy-done.16, ...), custom_call_target="tpu_custom_call", output_to_operand_aliasing={{7}: (3, {})} | custom-call | flops 30000001024 | bytes 1 | tf_op jit(solution)/shard_map/finish/pallas_call | solution.py:815
  85.0 0.8 while.23
  (22 shorter events, 0.2 us)
Async XLA Ops:
  0.6 7.1 %copy-start.6 = (bf16[2,256]{1,0:T(2,128)(2,1)S(1)}, bf16[2,256]{1,0:T(2,128)(2,1)}, u32[]{:S(2)}) copy-start(bf16[2,256]{1,0:T(2,128)(2,1)} %refs_5_.1) | copy-start | bytes 3076
  4.2 7.9 %collective-permute-start.22 = (bf16[2048,512]{1,0:T(8,128)(2,1)S(1)}, bf16[2048,512]{1,0:T(8,128)(2,1)S(1)}, u32[]{:S(2)}, u32[]{:S(2)}) collective-permute-start(bf16[2048,512]{1,0:T(8,128)(2,1)S(1)} %get-tuple-element.281), channel_id=1, source_target_pairs={{0,1},{1,0},{2,3},{3,2},{4,5},{5,4},{6,7},{7,6},{8,9},{9,8},{10,11... | collective-permute-start | bytes 6291464 | tf_op jit(solution)/shard_map/ppermute | solution.py:839
  4.7 15.5 %collective-permute-start.21 = (bf16[1040,256]{1,0:T(8,128)(2,1)S(1)}, bf16[1040,256]{1,0:T(8,128)(2,1)S(1)}, u32[]{:S(2)}, u32[]{:S(2)}) collective-permute-start(bf16[1040,256]{1,0:T(8,128)(2,1)S(1)} %get-tuple-element.279), channel_id=1, source_target_pairs={{0,2},{1,3},{2,0},{3,1},{4,6},{5,7},{6,4},{7,5},{8,10},{9,11},{10,... | collective-permute-start | bytes 1597448 | tf_op jit(solution)/shard_map/ppermute | solution.py:839
  7.3 13.8 %collective-permute-start.24 = (bf16[2048,512]{1,0:T(8,128)(2,1)S(1)}, bf16[2048,512]{1,0:T(8,128)(2,1)S(1)}, u32[]{:S(2)}, u32[]{:S(2)}) collective-permute-start(bf16[2048,512]{1,0:T(8,128)(2,1)S(1)} %get-tuple-element.296), channel_id=1, source_target_pairs={{0,1},{1,0},{2,3},{3,2},{4,5},{5,4},{6,7},{7,6},{8,9},{9,8},{10,11... | collective-permute-start | bytes 6291464 | tf_op jit(solution)/shard_map/ppermute | solution.py:839
  7.5 23.8 %collective-permute-start.23 = (bf16[1024,256]{1,0:T(8,128)(2,1)S(1)}, bf16[1024,256]{1,0:T(8,128)(2,1)S(1)}, u32[]{:S(2)}, u32[]{:S(2)}) collective-permute-start(bf16[1024,256]{1,0:T(8,128)(2,1)S(1)} %get-tuple-element.295), channel_id=1, source_target_pairs={{0,2},{1,3},{2,0},{3,1},{4,6},{5,7},{6,4},{7,5},{8,10},{9,11},{10,... | collective-permute-start | bytes 1572872 | tf_op jit(solution)/shard_map/ppermute | solution.py:839
  20.2 16.7 %collective-permute-start.27 = (bf16[2048,512]{1,0:T(8,128)(2,1)}, bf16[2048,512]{1,0:T(8,128)(2,1)S(1)}, u32[]{:S(2)}, u32[]{:S(2)}) collective-permute-start(bf16[2048,512]{1,0:T(8,128)(2,1)} %get-tuple-element.314), channel_id=1, source_target_pairs={{0,1},{1,0},{2,3},{3,2},{4,5},{5,4},{6,7},{7,6},{8,9},{9,8},{10,11... | collective-permute-start | bytes 6291464 | tf_op jit(solution)/shard_map/ppermute | solution.py:839
  25.7 17.1 %collective-permute-start.26 = (bf16[1024,256]{1,0:T(8,128)(2,1)S(1)}, bf16[1024,256]{1,0:T(8,128)(2,1)S(1)}, u32[]{:S(2)}, u32[]{:S(2)}) collective-permute-start(bf16[1024,256]{1,0:T(8,128)(2,1)S(1)} %get-tuple-element.309), channel_id=1, source_target_pairs={{0,2},{1,3},{2,0},{3,1},{4,6},{5,7},{6,4},{7,5},{8,10},{9,11},{10,... | collective-permute-start | bytes 1572872 | tf_op jit(solution)/shard_map/ppermute | solution.py:839
  33.7 14.6 %collective-permute-start.25 = (bf16[512,256]{1,0:T(8,128)(2,1)S(1)}, bf16[512,256]{1,0:T(8,128)(2,1)S(1)}, u32[]{:S(2)}, u32[]{:S(2)}) collective-permute-start(bf16[512,256]{1,0:T(8,128)(2,1)S(1)} %get-tuple-element.308), channel_id=1, source_target_pairs={{0,2},{1,3},{2,0},{3,1},{4,6},{5,7},{6,4},{7,5},{8,10},{9,11},{10,... | collective-permute-start | bytes 786440 | tf_op jit(solution)/shard_map/ppermute | solution.py:839
  44.1 17.7 %collective-permute-start.33 = (bf16[1024,256]{1,0:T(8,128)(2,1)S(1)}, bf16[1024,256]{1,0:T(8,128)(2,1)S(1)}, u32[]{:S(2)}, u32[]{:S(2)}) collective-permute-start(bf16[1024,256]{1,0:T(8,128)(2,1)S(1)} %get-tuple-element.341), channel_id=1, source_target_pairs={{0,2},{1,3},{2,0},{3,1},{4,6},{5,7},{6,4},{7,5},{8,10},{9,11},{10,... | collective-permute-start | bytes 1572872 | tf_op jit(solution)/shard_map/ppermute | solution.py:839
  48.3 0.8 copy-start.7
  50.0 4.8 %collective-permute-start.31 = (bf16[304,128]{1,0:T(8,128)(2,1)S(1)}, bf16[304,128]{1,0:T(8,128)(2,1)S(1)}, u32[]{:S(2)}, u32[]{:S(2)}) collective-permute-start(bf16[304,128]{1,0:T(8,128)(2,1)S(1)} %get-tuple-element.340), channel_id=1, source_target_pairs={{0,5},{1,4},{2,7},{3,6},{4,1},{5,0},{6,3},{7,2},{8,13},{9,12},{10,... | collective-permute-start | bytes 233480 | tf_op jit(solution)/shard_map/ppermute | solution.py:844
  52.2 2.6 %collective-permute-start.29 = (bf16[304,128]{1,0:T(8,128)(2,1)S(1)}, bf16[304,128]{1,0:T(8,128)(2,1)S(1)}, u32[]{:S(2)}, u32[]{:S(2)}) collective-permute-start(bf16[304,128]{1,0:T(8,128)(2,1)S(1)} %get-tuple-element.338), channel_id=1, source_target_pairs={{0,1},{1,0},{2,3},{3,2},{4,5},{5,4},{6,7},{7,6},{8,9},{9,8},{10,11... | collective-permute-start | bytes 233480 | tf_op jit(solution)/shard_map/ppermute | solution.py:839
  53.0 4.4 %collective-permute-start.30 = (bf16[304,128]{1,0:T(8,128)(2,1)S(1)}, bf16[304,128]{1,0:T(8,128)(2,1)S(1)}, u32[]{:S(2)}, u32[]{:S(2)}) collective-permute-start(bf16[304,128]{1,0:T(8,128)(2,1)S(1)} %get-tuple-element.339), channel_id=1, source_target_pairs={{0,4},{4,0},{8,12},{12,8},{16,20},{20,16},{24,28},{28,24},{1,5},{5... | collective-permute-start | bytes 233480 | tf_op jit(solution)/shard_map/ppermute | solution.py:839
  57.4 4.5 %collective-permute-start.32 = (bf16[304,128]{1,0:T(8,128)(2,1)S(1)}, bf16[304,128]{1,0:T(8,128)(2,1)S(1)}, u32[]{:S(2)}, u32[]{:S(2)}) collective-permute-start(bf16[304,128]{1,0:T(8,128)(2,1)S(1)} %add_convert_fusion.7), channel_id=1, source_target_pairs={{0,8},{4,12},{8,0},{12,4},{16,24},{20,28},{24,16},{28,20},{1,9},{5... | collective-permute-start | bytes 233480 | tf_op jit(solution)/shard_map/ppermute | solution.py:839
  59.4 14.1 %collective-permute-start.36 = (bf16[1024,256]{1,0:T(8,128)(2,1)S(1)}, bf16[1024,256]{1,0:T(8,128)(2,1)S(1)}, u32[]{:S(2)}, u32[]{:S(2)}) collective-permute-start(bf16[1024,256]{1,0:T(8,128)(2,1)S(1)} %get-tuple-element.343), channel_id=1, source_target_pairs={{0,2},{1,3},{2,0},{3,1},{4,6},{5,7},{6,4},{7,5},{8,10},{9,11},{10,... | collective-permute-start | bytes 1572872 | tf_op jit(solution)/shard_map/ppermute | solution.py:839
  61.9 5.4 %collective-permute-start.34 = (bf16[304,128]{1,0:T(8,128)(2,1)S(1)}, bf16[304,128]{1,0:T(8,128)(2,1)S(1)}, u32[]{:S(2)}, u32[]{:S(2)}) collective-permute-start(bf16[304,128]{1,0:T(8,128)(2,1)S(1)} %add_convert_fusion.6), channel_id=1, source_target_pairs={{0,16},{4,20},{8,24},{12,28},{16,0},{20,4},{24,8},{28,12},{1,17},{... | collective-permute-start | bytes 233480 | tf_op jit(solution)/shard_map/ppermute | solution.py:839
  67.3 7.1 %collective-permute-start.35 = (bf16[304,128]{1,0:T(8,128)(2,1)S(1)}, bf16[304,128]{1,0:T(8,128)(2,1)S(1)}, u32[]{:S(2)}, u32[]{:S(2)}) collective-permute-start(bf16[304,128]{1,0:T(8,128)(2,1)S(1)} %add_convert_fusion.5), channel_id=1, source_target_pairs={{0,2},{1,3},{2,0},{3,1},{4,6},{5,7},{6,4},{7,5},{8,10},{9,11},{10,... | collective-permute-start | bytes 233480 | tf_op jit(solution)/shard_map/ppermute | solution.py:839
  71.2 10.0 %collective-permute-start.28 = (bf16[2048,512]{1,0:T(8,128)(2,1)}, bf16[2048,512]{1,0:T(8,128)(2,1)S(1)}, u32[]{:S(2)}, u32[]{:S(2)}) collective-permute-start(bf16[2048,512]{1,0:T(8,128)(2,1)} %get-tuple-element.335), channel_id=1, source_target_pairs={{0,1},{1,0},{2,3},{3,2},{4,5},{5,4},{6,7},{7,6},{8,9},{9,8},{10,11... | collective-permute-start | bytes 6291464 | tf_op jit(solution)/shard_map/ppermute | solution.py:839
  74.4 6.5 %collective-permute-start.37 = (bf16[304,128]{1,0:T(8,128)(2,1)S(1)}, bf16[304,128]{1,0:T(8,128)(2,1)S(1)}, u32[]{:S(2)}, u32[]{:S(2)}) collective-permute-start(bf16[304,128]{1,0:T(8,128)(2,1)S(1)} %add_convert_fusion.4.refs_2_), channel_id=1, source_target_pairs={{0,1},{1,0},{2,3},{3,2},{4,5},{5,4},{6,7},{7,6},{8,9},{9,8},{10,11... | collective-permute-start | bytes 233480 | tf_op jit(solution)/shard_map/ppermute | solution.py:839
  74.5 6.4 %collective-permute-start.38 = (bf16[304,128]{1,0:T(8,128)(2,1)S(1)}, bf16[304,128]{1,0:T(8,128)(2,1)S(1)}, u32[]{:S(2)}, u32[]{:S(2)}) collective-permute-start(bf16[304,128]{1,0:T(8,128)(2,1)S(1)} %add_convert_fusion.4.refs_2_), channel_id=1, source_target_pairs={{0,4},{4,0},{8,12},{12,8},{16,20},{20,16},{24,28},{28,24},{1,5},{5... | collective-permute-start | bytes 233480 | tf_op jit(solution)/shard_map/ppermute | solution.py:839
  76.9 4.3 %collective-permute-start.39 = (bf16[304,128]{1,0:T(8,128)(2,1)S(1)}, bf16[304,128]{1,0:T(8,128)(2,1)S(1)}, u32[]{:S(2)}, u32[]{:S(2)}) collective-permute-start(bf16[304,128]{1,0:T(8,128)(2,1)S(1)} %add_convert_fusion.4.refs_2_), channel_id=1, source_target_pairs={{0,5},{1,4},{2,7},{3,6},{4,1},{5,0},{6,3},{7,2},{8,13},{9,12},{10,... | collective-permute-start | bytes 233480 | tf_op jit(solution)/shard_map/ppermute | solution.py:844
  77.0 4.2 %copy-start.10 = (f32[5,256]{1,0:T(8,128)S(1)}, f32[5,256]{1,0:T(8,128)}, u32[]{:S(2)}) copy-start(f32[5,256]{1,0:T(8,128)} %refs_10_.1) | copy-start | bytes 15364
  77.0 4.2 %copy-start.12 = (f32[5,256]{1,0:T(8,128)S(1)}, f32[5,256]{1,0:T(8,128)}, u32[]{:S(2)}) copy-start(f32[5,256]{1,0:T(8,128)} %refs_11_.1) | copy-start | bytes 15364
  77.0 4.3 %copy-start.14 = (s32[16]{0:T(128)S(1)}, s32[16]{0:T(128)}, u32[]{:S(2)}) copy-start(s32[16]{0:T(128)} %categories.1) | copy-start | bytes 196
  77.0 4.3 %copy-start.16 = (f32[5]{0:T(128)S(1)}, f32[5]{0:T(128)}, u32[]{:S(2)}) copy-start(f32[5]{0:T(128)} %momentum.1) | copy-start | bytes 64
  81.3 3.7 %copy-start.8 = (bf16[2,256]{1,0:T(2,128)(2,1)S(1)}, bf16[2,256]{1,0:T(2,128)(2,1)}, u32[]{:S(2)}) copy-start(bf16[2,256]{1,0:T(2,128)(2,1)} %refs_5_.1) | copy-start | bytes 3076

commit v3 on v2

--- a/solution.py
+++ b/solution.py
@@ -11,11 +11,13 @@
 CATS = 5
 BLOCK = 256
 TILE = 256
+ALIGN = 64
 UNIT = 2 * TILE
 WIN = BLOCK + 16
-LEAD = 4
-USUAL = 7
-STEPS = 11
+LEAD = 8
+USUAL = 13
+STEPS = 21
+PART = 4
 FAR = 1 << 20
 
 norm_eps = 1e-06
@@ -50,13 +52,10 @@
     return lax.broadcasted_iota(i32, shape, dim)
 
 
-def units(tiles):
-    return (tiles + 1) // 2
-
-
 def plan_messages(usual, steps):
-    tail = [c for c in range(usual, steps, 2)]
-    cuts = list(range(0, usual, 2)) + tail + [steps]
+    cuts = list(range(0, usual, PART)) + list(range(usual, steps, PART)) + [steps]
+    if usual % PART == 1:
+        cuts[usual // PART] -= 1
     return [(a, b - a) for a, b in zip(cuts, cuts[1:])]
 
 
@@ -95,24 +94,51 @@
     return row
 
 
+def ahead_by(v, step):
+    rows, lanes = v.shape
+    if step >= lanes:
+        return pltpu.roll(v, rows - step // lanes, 0)
+    moved = pltpu.roll(v, lanes - step, 1)
+    return jnp.where(iota((rows, lanes), 1) < lanes - step, moved, pltpu.roll(moved, rows - 1, 0))
+
+
+def back_by(v, step):
+    rows, lanes = v.shape
+    if step >= lanes:
+        return pltpu.roll(v, step // lanes, 0)
+    moved = pltpu.roll(v, step, 1)
+    return jnp.where(iota((rows, lanes), 1) >= step, moved, pltpu.roll(moved, 1, 0))
+
+
 def squeeze(pos, labels, group, span):
     rows, lanes = pos.shape
     at = iota((rows, lanes), 0) * lanes + iota((rows, lanes), 1)
     v = jnp.where(pos >= 0, (at - pos) * 16 + (labels - group * span + 1), 0)
     for bit in range((rows * lanes).bit_length() - 1):
-        step = 1 << bit
         go = jnp.where(((v >> (4 + bit)) & 1) == 1, v, 0)
-        if step < lanes:
-            moved = pltpu.roll(go, lanes - step, 1)
-            moved = jnp.where(iota((rows, lanes), 1) < lanes - step, moved, pltpu.roll(moved, rows - 1, 0))
-        else:
-            moved = pltpu.roll(go, rows - step // lanes, 0)
-        v = v - go + moved
+        v = v - go + ahead_by(go, 1 << bit)
     return v & 15
 
 
+def stream_names(pos, labels, group, span, cap):
+    rows = labels.shape[0]
+    first, second = (squeeze(pos[n * rows : (n + 1) * rows], labels, group + n, span) for n in range(2))
+    one = jnp.where(pos[:rows] >= 0, 1.0, 0.0)
+    count = jnp.sum(jnp.sum(one, axis=1, keepdims=True), axis=0, keepdims=True).astype(i32)
+    skip = (count + (ALIGN - 1)) // ALIGN * ALIGN
+    step = ALIGN
+    while step <= cap:
+        second = jnp.where((skip & step) > 0, back_by(second, step), second)
+        step *= 2
+    return first + second
+
+
+def filled(bounds, group, blocks, row=1):
+    return (bounds[row, (group + 1) * blocks - 1] + (ALIGN - 1)) // ALIGN * ALIGN
+
+
 def tiles_of(bounds, group, blocks, row=1):
-    return (bounds[row, (group + 1) * blocks - 1] + TILE - 1) // TILE
+    return (filled(bounds, group, blocks, row) + filled(bounds, group + 1, blocks, row) + (TILE - 1)) // TILE
 
 
 def spans(bounds, groups, blocks, b):
@@ -169,10 +195,8 @@
     pre = pre + add
     valid = col > 0.0
     e = jnp.exp(-jnp.abs(pre))
-    u = 1.0 + e
-    r = 1.0 / u
-    soft = jnp.maximum(pre, 0.0) + jnp.where(e < 2.0**-12, e, jnp.log(u))
-    sig = jnp.where(pre >= 0.0, r, e * r)
+    soft = jnp.maximum(pre, 0.0) + jnp.where(e < 2.0**-12, e, jnp.log(1.0 + e))
+    sig = jnp.exp(pre - soft)
     lo = jnp.where(valid, soft, 0.0).astype(bf16)
     gp = jnp.where(valid, ct.astype(f32) * sig, 0.0).astype(bf16)
     gx = jnp.dot(gp, wpt_ref[...], preferred_element_type=f32).astype(bf16)
@@ -201,7 +225,7 @@
         f.start()
     heads, refs = refs[: 2 * far], refs[2 * far :]
     queues, rows_far, refs = refs[:far], refs[far : 2 * far], refs[2 * far :]
-    row_near, bounds_ref, names_ref, info_ref, moved, bounds_v, bounds, sem = refs
+    row_near, bounds_ref, labels_ref, pos_ref, moved, bounds_v, bounds, sem = refs
     blocks = row_near.shape[0]
     me = lax.axis_index(oct_axis)
     first_shape = lax.axis_index(shape_axis) * span
@@ -224,23 +248,15 @@
     row_near[...] = sorted_rows(pos, lo, hi, blocks, 0, 2)
     for k in range(far):
         rows_far[k][...] = sorted_rows(pos, lo, hi, blocks, 2 + 2 * k, 2)
-    tiles = cap // TILE
-    names_ref[...] = jnp.zeros(names_ref.shape, i32)
-    for g in range(2):
-        names_ref[g * 8 : g * 8 + tiles, :] = squeeze(pos[g * blocks : (g + 1) * blocks], labels, g, span)[:tiles]
-
-    info_ref[...] = jnp.zeros(info_ref.shape, f32)
-    for s in range(span):
-        number = jnp.sum(jnp.sum(jnp.where(ids == s, 1.0, 0.0), axis=1, keepdims=True), axis=0, keepdims=True)
-        info_ref[s : s + 1, :] = jnp.broadcast_to(number, (1, 128))
-
+    labels_ref[...] = labels
+    pos_ref[...] = pos[: 2 * blocks]
     for k in range(far):
         queues[k][...] = jnp.zeros(queues[k].shape, bf16)
     copy.wait()
     fetches[2].wait()
     for k in range(far):
         groups = [2 + 2 * k, 3 + 2 * k]
-        cut = tiles_of(bounds, groups[0], blocks) * TILE
+        cut = filled(bounds, groups[0], blocks)
         sort_rows(bounds, rows_far[k], x_ref, groups, blocks, moved,
                   lambda n, first: (queues[k], pl.multiple_of(first + n * cut, 16)))
         heads[2 * k][: sizes[0], :] = queues[k][: sizes[0], :]
@@ -255,12 +271,12 @@
     blocks = count // BLOCK
     far = oct_count // 2 - 1
     shape = jax.ShapeDtypeStruct
-    sizes = [n * UNIT for _, n in messages[:2]]
+    sizes = [n * TILE for _, n in messages[:2]]
     heads = [pltpu.VMEM((sizes[0] + blocks, width), bf16), pltpu.VMEM((sizes[1], width), bf16)] * far
     cols = cotangent.shape[1]
     outs = [pltpu.VMEM((cap, cols), bf16), pltpu.VMEM((far * cap, cols), bf16), pltpu.VMEM(points.shape, bf16)] + heads + [pltpu.VMEM((4 * cap, width), bf16)] * far
     outs += [shape((blocks, BLOCK), i32)] * (far + 1)
-    outs += [shape((8, 128), i32), shape((16, BLOCK), i32), shape((8, 128), f32)]
+    outs += [shape((8, 128), i32), shape((blocks, BLOCK), i32), shape((2 * blocks, BLOCK), i32)]
     out = pl.pallas_call(
         functools.partial(pack_kernel, oct_count, sizes, "shape", "oct", span, cap),
         in_specs=specs("aaaa"),
@@ -303,13 +319,11 @@
     cb_ref[...] = jnp.dot(codes, w_code, preferred_element_type=f32) + bias_ref[...]
 
 
-def prepare_kernel(oct_count, oct_axis, cap, bounds, row_ref, x_ref, codes_v, direction_hbm, gain_hbm, bias_hbm,
-                   lo_hbm, lon_hbm, gw_ref, buf, wp_ref, wpt_ref, w_ref, cb_ref, norm_ref, direction_v, gain_v,
-                   moved, zero, bias_v, zero_sem, in_sem):
+def prepare_kernel(oct_count, oct_axis, span, cap, bounds, row_ref, labels_ref, pos_ref, x_ref, codes_v, direction_hbm, gain_hbm, bias_hbm,
+                   gw_ref, buf, wp_ref, wpt_ref, w_ref, cb_ref, norm_ref, direction_v, gain_v,
+                   names_ref, info_ref, moved, bias_v, in_sem):
     blocks = row_ref.shape[0]
-    tiles = cap // TILE
-    source = lax.axis_index(oct_axis)
-    cut = [tiles_of(bounds, r, blocks) for r in range(2)]
+    cut = [filled(bounds, r, blocks) for r in range(2)]
     fetches = [
         pltpu.make_async_copy(a, b, in_sem.at[i])
         for i, (a, b) in enumerate(((direction_hbm, direction_v), (gain_hbm, gain_v), (bias_hbm, bias_v)))
@@ -317,40 +331,31 @@
     for f in fetches:
         f.start()
 
-    def clear(go):
-        for t in range(tiles):
-            @pl.when(t >= cut[0])
-            def _():
-                at = source * cap + t * TILE
-                go(pltpu.make_async_copy(zero, lo_hbm.at[pl.ds(pl.multiple_of(at, TILE), TILE), :], zero_sem))
-
-            @pl.when(t >= cut[1])
-            def _():
-                go(pltpu.make_async_copy(zero, lon_hbm.at[pl.ds(t * TILE, TILE), :], zero_sem))
-
-    zero[...] = jnp.zeros(zero.shape, bf16)
-    clear(lambda c: c.start())
     gw_ref[...] = jnp.zeros(gw_ref.shape, f32)
     buf[...] = jnp.zeros(buf.shape, bf16)
     sort_rows(bounds, row_ref, x_ref, [0, 1], blocks, moved,
-              lambda n, first: (buf, pl.multiple_of(first + n * cut[0] * TILE, 16)))
+              lambda n, first: (buf, pl.multiple_of(first + n * cut[0], 16)))
+    labels = labels_ref[...]
+    names_ref[...] = stream_names(pos_ref[...], labels, 0, span, cap)
+    ids = labels % span
+    info_ref[...] = jnp.zeros(info_ref.shape, f32)
+    for s in range(span):
+        number = jnp.sum(jnp.sum(jnp.where(ids == s, 1.0, 0.0), axis=1, keepdims=True), axis=0, keepdims=True)
+        info_ref[s : s + 1, :] = jnp.broadcast_to(number, (1, 128))
     for f in fetches:
         f.wait()
     set_weights(HID, direction_v, gain_v, bias_v, codes_v, wp_ref, wpt_ref, w_ref, cb_ref, norm_ref)
-    clear(lambda c: c.wait())
-
-
-def prepare(bounds, row, points, direction, gain, bias, codes, oct_count, cap):
+
+
+def prepare(bounds, row, labels, pos, points, direction, gain, bias, codes, oct_count, cap):
     width = points.shape[1]
     ins, outs = direction.shape
     blocks = row.shape[0]
     return pl.pallas_call(
-        functools.partial(prepare_kernel, oct_count, "oct", cap),
-        in_specs=specs("svvvaaa"),
-        out_specs=specs("aavvvvvvvvv"),
+        functools.partial(prepare_kernel, oct_count, "oct", codes.shape[0], cap),
+        in_specs=specs("svvvvvaaa"),
+        out_specs=specs("vvvvvvvvvvv"),
         out_shape=[
-            pltpu.HBM((oct_count * cap, outs), bf16),
-            pltpu.HBM((cap, outs), bf16),
             pltpu.VMEM((width + 16, outs), f32),
             pltpu.VMEM((2 * cap + BLOCK + WIN, width), bf16),
             pltpu.VMEM((width, outs), bf16),
@@ -360,63 +365,62 @@
             pltpu.VMEM((1, outs), f32),
             pltpu.VMEM((ins, outs), f32),
             pltpu.VMEM((1, outs), f32),
+            pltpu.VMEM(row.shape, i32),
+            pltpu.VMEM((8, 128), f32),
         ],
         scratch_shapes=[
             pltpu.VMEM((blocks * window_rows(2, 64) + WIN, width), bf16),
-            pltpu.VMEM((TILE, outs), bf16),
             pltpu.VMEM((1, outs), f32),
-            pltpu.SemaphoreType.DMA,
             pltpu.SemaphoreType.DMA((3,)),
         ],
         compiler_params=params(14),
         cost_estimate=cost("prepare"),
         name="prepare",
-    )(bounds, row, keep(points), codes, stay(direction), stay(gain[None, :]), stay(bias[None, :]))
+    )(bounds, row, labels, pos, keep(points), codes, stay(direction), stay(gain[None, :]), stay(bias[None, :]))
 
 
 class Rows:
-    def __init__(self, bounds, cut, source, cap, place):
-        self.cut, self.source, self.cap, self.place = cut, source, cap, place
-        self.count = cut[0] + cut[1]
-
-    def split(self, unit, i):
-        t = unit * 2 + i
-        second = (t >= self.cut[0]).astype(i32)
-        return t, second, t - second * self.cut[0]
-
-    def live(self, unit):
-        return unit * 2 < self.count
-
-    def move(self, unit, own, other, other_at, mine, mine_at, sem, out, go):
-        for i in range(2):
-            t, second, slot = self.split(unit, i)
-            here = mine.at[pl.ds(mine_at + i * TILE, TILE), :]
-
-            def one(array, row):
-                there = array.at[pl.ds(pl.multiple_of(row + slot * TILE, TILE), TILE), :]
-                go(pltpu.make_async_copy(here, there, sem) if out else pltpu.make_async_copy(there, here, sem))
-
-            @pl.when((t < self.count) & (second == 0))
-            def _():
-                one(own, self.source * self.cap)
-
-            @pl.when((t < self.count) & (second == 1))
-            def _():
-                one(other, other_at)
-
-    def fetch(self, unit, ct, ctx, mine, at, sem, go):
-        self.move(unit, ct, ctx, self.place * self.cap, mine, at, sem, False, go)
-
-    def store(self, unit, lo, lox, mine, at, sem, go):
-        self.move(unit, lo, lox, self.place * self.cap, mine, at, sem, True, go)
-
-    def names(self, unit, names_ref):
-        rows = []
-        for i in range(2):
-            t, second, slot = self.split(unit, i)
-            row = names_ref[pl.ds(jnp.minimum(second * 8 + slot, names_ref.shape[0] - 1), 1), :]
-            rows.append(jnp.where(t < self.count, row, 0))
-        return jnp.concatenate(rows, axis=1)
+    def __init__(self, cut, source, cap, place):
+        self.cut, self.own_at, self.other_at = cut, source * cap, place * cap
+        self.total = cut[0] + cut[1]
+        self.tiles = (self.total + (TILE - 1)) // TILE
+
+    def move(self, tile, own, other, mine, mine_at, sem, out, go):
+        first = tile * TILE
+        cut, total = self.cut[0], self.total
+
+        def one(at, rows, second):
+            here = mine.at[pl.ds(mine_at + at, rows), :]
+            row = first + at
+            there = other if second else own
+            start = self.other_at + row - cut if second else self.own_at + row
+            there = there.at[pl.ds(pl.multiple_of(start, ALIGN), rows), :]
+            go(pltpu.make_async_copy(here, there, sem) if out else pltpu.make_async_copy(there, here, sem))
+
+        whole = first + TILE <= cut
+        last = (first >= cut) & (first + TILE <= total)
+        pl.when(whole)(lambda: one(0, TILE, False))
+        pl.when(last)(lambda: one(0, TILE, True))
+
+        @pl.when((first < total) & jnp.logical_not(whole | last))
+        def _():
+            for at in range(0, TILE, ALIGN):
+                pl.when(first + at < cut)(lambda: one(at, ALIGN, False))
+                pl.when((first + at >= cut) & (first + at < total))(lambda: one(at, ALIGN, True))
+
+    def fetch(self, tile, ct, ctx, mine, at, sem, go):
+        self.move(tile, ct, ctx, mine, at, sem, False, go)
+
+    def store(self, tile, lo, lox, mine, at, sem, go):
+        self.move(tile, lo, lox, mine, at, sem, True, go)
+
+
+def rows_of(bounds, group, blocks, source, cap, place, row=1):
+    return Rows([filled(bounds, group + r, blocks, row) for r in range(2)], source, cap, place)
+
+
+def names_at(names_ref, tile, number):
+    return jnp.concatenate([names_ref[pl.ds(tile + i, 1), :] for i in range(number)], axis=1)
 
 
 def go_start(copy):
@@ -428,14 +432,28 @@
 
 
 def local_kernel(oct_axis, far, blocks, span, cap, bounds, *refs):
-    names_ref, ct_hbm, ctx_ref, wp_ref, wpt_ref, cb_ref, lo_in, lon_in, gw_in, buf_in, refs = *refs[:10], refs[10:]
+    names_ref, ct_hbm, ctx_ref, wp_ref, wpt_ref, cb_ref, gw_in, buf_in, refs = *refs[:8], refs[8:]
     lo_hbm, lon_hbm, lof_hbm, gw_ref, buf, refs = *refs[:5], refs[5:]
     ct_v, lo_v, zero, ct_sem, lo_sem, zero_sem = refs
     source = lax.axis_index(oct_axis)
-    near = Rows(bounds, [tiles_of(bounds, r, blocks) for r in range(2)], source, cap, 0)
-    count = units(near.count)
+    near = rows_of(bounds, 0, blocks, source, cap, 0)
+    count = (near.tiles + (PART - 1)) // PART
 
     def clear(go):
+        def empty(array, at, t, cut):
+            pl.when(t * TILE >= cut)(lambda: go(pltpu.make_async_copy(zero, array.at[pl.ds(pl.multiple_of(at + t * TILE, TILE), TILE), :], zero_sem)))
+
+            @pl.when((t * TILE < cut) & ((t + 1) * TILE > cut))
+            def _():
+                for q in range(0, TILE, ALIGN):
+                    @pl.when(t * TILE + q >= cut)
+                    def _():
+                        rows = pl.ds(pl.multiple_of(at + t * TILE + q, ALIGN), ALIGN)
+                        go(pltpu.make_async_copy(zero.at[pl.ds(0, ALIGN), :], array.at[rows, :], zero_sem))
+
+        for t in range(cap // TILE):
+            empty(lo_hbm, source * cap, t, near.cut[0])
+            empty(lon_hbm, 0, t, near.cut[1])
         for k in range(1, far + 1):
             for t in range(cap // TILE):
                 at = (source ^ (2 * k)) * cap + t * TILE
@@ -443,9 +461,17 @@
         for t in range(lof_hbm.shape[0] // TILE):
             go(pltpu.make_async_copy(zero, lof_hbm.at[pl.ds(t * TILE, TILE), :], zero_sem))
 
+    def fetch(i, slot, go):
+        for j in range(PART):
+            near.fetch(i * PART + j, ct_hbm, ctx_ref, ct_v.at[slot], j * TILE, ct_sem.at[slot], go)
+
+    def store(i, slot, go):
+        for j in range(PART):
+            near.store(i * PART + j, lo_hbm, lon_hbm, lo_v.at[slot], j * TILE, lo_sem.at[slot], go)
+
     @pl.when(count > 0)
     def _():
-        near.fetch(0, ct_hbm, ctx_ref, ct_v.at[0], 0, ct_sem.at[0], go_start)
+        fetch(0, 0, go_start)
 
     zero[...] = jnp.zeros(zero.shape, bf16)
     clear(go_start)
@@ -455,52 +481,57 @@
 
         @pl.when(i + 1 < count)
         def _():
-            near.fetch(i + 1, ct_hbm, ctx_ref, ct_v.at[1 - slot], 0, ct_sem.at[1 - slot], go_start)
-
-        near.fetch(i, ct_hbm, ctx_ref, ct_v.at[slot], 0, ct_sem.at[slot], go_wait)
+            fetch(i + 1, 1 - slot, go_start)
+
+        fetch(i, slot, go_wait)
 
         @pl.when(i >= 2)
         def _():
-            near.store(i - 2, lo_hbm, lon_hbm, lo_v.at[slot], 0, lo_sem.at[slot], go_wait)
-
-        at = pl.ds(pl.multiple_of(i * UNIT, UNIT), UNIT)
-        lo, gx = layer_tile(buf[at, :], near.names(i, names_ref), ct_v[slot], wp_ref, wpt_ref, cb_ref, gw_ref, span)
-        lo_v[slot] = lo
-        buf[at, :] = gx
-        near.store(i, lo_hbm, lon_hbm, lo_v.at[slot], 0, lo_sem.at[slot], go_start)
+            store(i - 2, slot, go_wait)
+
+        def work(size):
+            at = pl.ds(pl.multiple_of(i * PART * TILE, TILE), size * TILE)
+            ct = ct_v[slot, : size * TILE, :]
+            lo, gx = layer_tile(buf[at, :], names_at(names_ref, i * PART, size), ct, wp_ref, wpt_ref, cb_ref, gw_ref, span)
+            lo_v[slot, : size * TILE, :] = lo
+            buf[at, :] = gx
+
+        more = near.tiles - i * PART > 2
+        pl.when(more)(lambda: work(PART))
+        pl.when(jnp.logical_not(more))(lambda: work(2))
+        store(i, slot, go_start)
         return carry
 
     lax.fori_loop(0, count, step, 0)
     for back in (2, 1):
         @pl.when(count >= back)
         def _():
-            slot = (count - back) % 2
-            near.store(count - back, lo_hbm, lon_hbm, lo_v.at[slot], 0, lo_sem.at[slot], go_wait)
+            store(count - back, (count - back) % 2, go_wait)
 
     clear(go_wait)
 
 
-def local(bounds, names, cotangent, ctx, weights, lo, lon, gw, buf, far, blocks, span, cap):
-    outs = lo.shape[1]
+def local(bounds, names, cotangent, ctx, weights, gw, buf, far, blocks, span, cap):
+    outs = cotangent.shape[1]
     return pl.pallas_call(
         functools.partial(local_kernel, "oct", far, blocks, span, cap),
-        in_specs=specs("svavvvvaavv"),
+        in_specs=specs("svavvvvvv"),
         out_specs=specs("aaavv"),
-        out_shape=[pltpu.HBM(lo.shape, bf16), pltpu.HBM(lon.shape, bf16), pltpu.HBM((far * cap, outs), bf16),
+        out_shape=[pltpu.HBM(cotangent.shape, bf16), pltpu.HBM((cap, outs), bf16), pltpu.HBM((far * cap, outs), bf16),
                    pltpu.VMEM(gw.shape, f32), pltpu.VMEM(buf.shape, bf16)],
-        input_output_aliases={7: 0, 8: 1, 9: 3, 10: 4},
+        input_output_aliases={7: 3, 8: 4},
         scratch_shapes=[
-            pltpu.VMEM((2, UNIT, outs), bf16),
-            pltpu.VMEM((2, UNIT, outs), bf16),
+            pltpu.VMEM((2, PART * TILE, outs), bf16),
+            pltpu.VMEM((2, PART * TILE, outs), bf16),
             pltpu.VMEM((TILE, outs), bf16),
             pltpu.SemaphoreType.DMA((2,)),
             pltpu.SemaphoreType.DMA((2,)),
             pltpu.SemaphoreType.DMA,
         ],
-        compiler_params=params(12),
+        compiler_params=params(24),
         cost_estimate=cost("local"),
         name="local",
-    )(bounds, names, stay(cotangent), keep(ctx), *[keep(w) for w in weights], stay(lo), stay(lon), keep(gw), keep(buf))
+    )(bounds, names, stay(cotangent), keep(ctx), *[keep(w) for w in weights], keep(gw), keep(buf))
 
 
 def unlocal_kernel(oct_axis, cap, bounds, row_ref, gbuf, lon_ref, lo_in, part_ref, lo_hbm, moved, sem):
@@ -510,7 +541,7 @@
     def emit(b, rows):
         part_ref[b * BLOCK : (b + 1) * BLOCK, :] = rows.astype(bf16)
 
-    cut = tiles_of(bounds, 0, blocks) * TILE
+    cut = filled(bounds, 0, blocks)
     unsort_rows(bounds, row_ref, [0, 1], blocks,
                 lambda n, first, rows: gbuf[pl.ds(pl.multiple_of(first + n * cut, 16), rows), :], moved, emit)
     join(cap, [0], oct_axis, lon_ref, lo_hbm, sem, go_wait)
@@ -536,10 +567,7 @@
     blocks = labels.shape[0]
     groups = [2 * kx, 2 * kx + 1]
     pos, _, _, _, last = plan(labels, groups, span)
-    tiles = cap // TILE
-    names_ref[...] = jnp.zeros(names_ref.shape, i32)
-    for n, g in enumerate(groups):
-        names_ref[n * 8 : n * 8 + tiles, :] = squeeze(pos[n * blocks : (n + 1) * blocks], labels, g, span)[:tiles]
+    names_ref[...] = stream_names(pos, labels, groups[0], span, cap)
     count_ref[...] = jnp.zeros(count_ref.shape, i32)
     count_ref[0:1, : 2 * blocks] = last[:1]
     back_ref[...] = jnp.zeros(back_ref.shape, bf16)
@@ -551,7 +579,7 @@
         in_specs=specs("v"),
         out_specs=specs("vvv"),
         out_shape=[
-            jax.ShapeDtypeStruct((16, BLOCK), i32),
+            jax.ShapeDtypeStruct((labels.shape[0], BLOCK), i32),
             jax.ShapeDtypeStruct((8, 128), i32),
             pltpu.VMEM((2 * cap + UNIT, labels.shape[1]), bf16),
         ],
@@ -562,15 +590,16 @@
 
 
 def lead_of(tiles):
-    return jnp.maximum(units(tiles), LEAD)
-
-
-def take_back(place, theirs, blocks, x_ref, at, back):
-    n = place - lead_of(tiles_of(theirs, 0, blocks, 0) + tiles_of(theirs, 1, blocks, 0))
-
-    @pl.when((n >= 0) & (n < back.shape[0] // UNIT - 1))
-    def _():
-        back[pl.ds(pl.multiple_of(n * UNIT, UNIT), UNIT), :] = x_ref[at : at + UNIT, :]
+    return jnp.maximum(tiles, LEAD)
+
+
+def take_back(place, number, theirs, blocks, x_ref, at, back):
+    for i in range(number):
+        n = place + i - lead_of(tiles_of(theirs, 0, blocks, 0))
+
+        @pl.when((n >= 0) & (n < (back.shape[0] - UNIT) // TILE))
+        def _():
+            back[pl.ds(pl.multiple_of(n * TILE, TILE), TILE), :] = x_ref[at + i * TILE : at + (i + 1) * TILE, :]
 
 
 def far_kernel(message, before, after_it, emits, kx, oct_axis, blocks, span, cap, mine, theirs, *refs):
@@ -587,37 +616,42 @@
     ct_sem, new_sem, lo_sem = refs
     first, number = message
     source = lax.axis_index(oct_axis) ^ (2 * kx)
-    rows = Rows(theirs, [tiles_of(theirs, r, blocks, 0) for r in range(2)], source, cap, kx - 1)
-    lead = lead_of(tiles_of(mine, 2 * kx, blocks) + tiles_of(mine, 2 * kx + 1, blocks))
+    rows = rows_of(theirs, 0, blocks, source, cap, kx - 1, 0)
+    lead = lead_of(tiles_of(mine, 2 * kx, blocks))
 
     def fetch(u, go):
         if not before:
-            rows.fetch(first + u, ct_hbm, ctx_ref, ct_v, u * UNIT, ct_sem.at[u], go)
+            rows.fetch(first + u, ct_hbm, ctx_ref, ct_v, u * TILE, ct_sem.at[u], go)
 
     def ahead(go):
         if before:
             for u in range(before[1]):
-                rows.store(before[0] + u, lo_hbm, lof_hbm, lo_old, u * UNIT, lo_sem, go)
+                rows.store(before[0] + u, lo_hbm, lof_hbm, lo_old, u * TILE, lo_sem, go)
         if after_it:
             for u in range(after_it[1]):
-                rows.fetch(after_it[0] + u, ct_hbm, ctx_ref, ct_new, u * UNIT, new_sem, go)
+                rows.fetch(after_it[0] + u, ct_hbm, ctx_ref, ct_new, u * TILE, new_sem, go)
 
     for u in range(number):
         fetch(u, go_start)
     ahead(go_start)
+    take_back(first, number, theirs, blocks, x_ref, 0, back)
     for u in range(number):
-        take_back(first + u, theirs, blocks, x_ref, u * UNIT, back)
         fetch(u, go_wait)
 
-        @pl.when(rows.live(first + u))
-        def _():
-            at = slice(u * UNIT, (u + 1) * UNIT)
-            lo, gx = layer_tile(x_ref[at, :], rows.names(first + u, names_ref), ct_v[at, :], wp_ref, wpt_ref, cb_ref, gw_ref, span)
-            lo_v[at, :] = lo
-            queue[pl.ds(pl.multiple_of((lead + first + u) * UNIT, UNIT), UNIT), :] = gx
+    def work(size):
+        at = slice(0, size * TILE)
+        lo, gx = layer_tile(x_ref[at, :], names_at(names_ref, first, size), ct_v[at, :], wp_ref, wpt_ref, cb_ref, gw_ref, span)
+        lo_v[at, :] = lo
+        queue[pl.ds(pl.multiple_of((lead + first) * TILE, TILE), size * TILE), :] = gx
+
+    if number > 2:
+        pl.when(first + 2 < rows.tiles)(lambda: work(number))
+        pl.when((first < rows.tiles) & (first + 2 >= rows.tiles))(lambda: work(2))
+    else:
+        pl.when(first < rows.tiles)(lambda: work(number))
 
     for payload, (place, count) in zip(payloads, emits):
-        payload[...] = queue[place * UNIT : (place + count) * UNIT, :]
+        payload[...] = queue[place * TILE : (place + count) * TILE, :]
     ahead(go_wait)
 
 
@@ -628,11 +662,11 @@
     last = points_in[-1] == m
     message, before, after_it = messages[m], (messages[m - 1] if m > 0 else None), (None if last else messages[m + 1])
     emits = messages[m + 2 :] if last else [messages[m + 2]]
-    own = (message[1] * UNIT, outs)
+    own = (message[1] * TILE, outs)
     shapes = [pltpu.VMEM(queue.shape, bf16), pltpu.HBM(lo.shape, bf16), pltpu.HBM(lof.shape, bf16), pltpu.VMEM(gw.shape, f32),
-              pltpu.VMEM(back.shape, bf16)] + [pltpu.VMEM((count * UNIT, width), bf16) for _, count in emits]
+              pltpu.VMEM(back.shape, bf16)] + [pltpu.VMEM((count * TILE, width), bf16) for _, count in emits]
     if after_it:
-        shapes.append(pltpu.VMEM((after_it[1] * UNIT, outs), bf16))
+        shapes.append(pltpu.VMEM((after_it[1] * TILE, outs), bf16))
     shapes.append(pltpu.VMEM(own, bf16))
     args = [mine, theirs, names, keep(x), stay(cotangent), keep(ctx), keep(wp), keep(wpt), keep(cb), keep(queue), stay(lo),
             stay(lof), keep(gw), keep(back)] + [keep(a) for a in ahead]
@@ -644,7 +678,7 @@
         input_output_aliases={9 + i: i for i in range(5)},
         scratch_shapes=([] if before else [pltpu.VMEM(own, bf16)])
         + [pltpu.SemaphoreType.DMA((message[1],)), pltpu.SemaphoreType.DMA, pltpu.SemaphoreType.DMA],
-        compiler_params=params(12),
+        compiler_params=params(20),
         cost_estimate=cost("last" if last else "far"),
         name="far",
     )(*args)
@@ -658,9 +692,8 @@
     out_ref, backs, moved = refs[0], refs[1 : 1 + far], refs[-1]
     for k in range(far):
         for j, (first, number) in enumerate(lasts):
-            for u in range(number):
-                take_back(first + u, theirs[k], blocks, parts[k * len(lasts) + j], u * UNIT, backs[k])
-        cut = tiles_of(bounds, 2 + 2 * k, blocks) * TILE
+            take_back(first, number, theirs[k], blocks, parts[k * len(lasts) + j], 0, backs[k])
+        cut = filled(bounds, 2 + 2 * k, blocks)
 
         def pick(n, first, count):
             return backs[k][pl.ds(pl.multiple_of(first + n * cut, 16), count), :]
@@ -698,6 +731,25 @@
         go(pltpu.make_async_copy(lox_ref.at[pl.ds(n * cap, cap), :], lo_hbm.at[at, :], sem.at[n]))
 
 
+def merge_kernel(cap, kxs, oct_axis, lox_ref, lo_in, lo_hbm, sem):
+    for go in (go_start, go_wait):
+        join(cap, kxs, oct_axis, lox_ref, lo_hbm, sem, go)
+
+
+def merge(lox, lo, cap, kxs):
+    return pl.pallas_call(
+        functools.partial(merge_kernel, cap, tuple(kxs), "oct"),
+        in_specs=specs("va"),
+        out_specs=specs("a")[0],
+        out_shape=pltpu.HBM(lo.shape, lo.dtype),
+        input_output_aliases={1: 0},
+        scratch_shapes=[pltpu.SemaphoreType.DMA((len(kxs),))],
+        compiler_params=params(4),
+        cost_estimate=cost("merge"),
+        name="merge",
+    )(keep(lox), stay(lo))
+
+
 def column_block(axes, n):
     a, b = (lax.axis_index(axis) % 2 for axis in axes)
     return (a ^ (n % 2)) * 2 + (b ^ (n // 2))
@@ -711,9 +763,9 @@
 
     def store(go):
         for k in range(extra):
-            rows = Rows(theirs[k], [tiles_of(theirs[k], r, blocks, 0) for r in range(2)], source ^ (2 * k + 2), cap, k)
+            rows = rows_of(theirs[k], 0, blocks, source ^ (2 * k + 2), cap, k, 0)
             for u in range(message[1]):
-                rows.store(message[0] + u, lo_hbm, lof_hbm, olds[k], u * UNIT, sem, go)
+                rows.store(message[0] + u, lo_hbm, lof_hbm, olds[k], u * TILE, sem, go)
 
     store(go_start)
     width = gw_ref.shape[0] - 16
@@ -725,6 +777,13 @@
     for s in range(span):
         ps = ps + jnp.where(iota((shapes, 1), 0) == base + s, gw_ref[width + s : width + s + 1, :], 0.0)
     full[width : width + shapes, :] = ps
+    flag = jnp.int32(0)
+    for k in range(extra):
+        ours = tiles_of(mine, 2 + 2 * k, blocks)
+        other = tiles_of(theirs[k], 0, blocks, 0)
+        most = jnp.maximum(jnp.maximum(ours, LEAD) + other, jnp.maximum(other, LEAD) + ours)
+        flag = flag | ((jnp.maximum(ours, other) > usual) | (most > steps)).astype(i32)
+    flag = flag.astype(f32)
     lane = iota((1, cols - code_width), 1)
     info = jnp.zeros((shapes, cols), f32)
     for s in range(span):
@@ -732,17 +791,10 @@
         high = jnp.floor(number / 1024.0)
         mid = jnp.floor((number - 1024.0 * high) / 32.0)
         low = number - 1024.0 * high - 32.0 * mid
-        digits = jnp.where(lane < 64, low, jnp.where(lane < 128, mid, high))
+        digits = jnp.where(lane < 64, low, jnp.where(lane < 128, mid, jnp.where(lane < 192, high, flag)))
         code = jnp.where(lax.axis_index(oct_axis) == 0, codes_ref[s : s + 1, :].astype(f32), 0.0)
         info = info + jnp.where(iota((shapes, 1), 0) == base + s, jnp.concatenate([code, digits], axis=1), 0.0)
     full[width + shapes : width + 2 * shapes, :] = info
-    flag = jnp.int32(0)
-    for k in range(extra):
-        ours = units(tiles_of(mine, 2 + 2 * k, blocks) + tiles_of(mine, 3 + 2 * k, blocks))
-        other = units(tiles_of(theirs[k], 0, blocks, 0) + tiles_of(theirs[k], 1, blocks, 0))
-        most = jnp.maximum(jnp.maximum(ours, LEAD) + other, jnp.maximum(other, LEAD) + ours)
-        flag = flag | ((jnp.maximum(ours, other) > usual) | (most > steps)).astype(i32)
-    full[width + 2 * shapes :, :] = jnp.zeros((16, cols), f32) + flag.astype(f32)
     for n in range(4):
         at = pl.ds(pl.multiple_of(column_block(axes, n) * 128, 128), 128)
         outs[n][...] = full[:, at].astype(bf16)
@@ -754,17 +806,16 @@
     return high, (x - high.astype(f32)).astype(bf16)
 
 
-def finish_kernel(axes, shape_axis, oct_axis, hid, span, cap, kxs, categories, momentum, *refs):
-    lox_ref, lo_in, parts, refs = *refs[:2], refs[2:6], refs[6:]
+def finish_kernel(axes, shape_axis, hid, span, categories, momentum, *refs):
+    parts, refs = refs[:4], refs[4:]
     direction_ref, gain_ref, norm_ref, w_ref, mean_ref, var_ref, refs = *refs[:6], refs[6:]
-    dg_ref, gg_ref, bg_ref, cg_ref, mean_out, var_out, left_ref, lo_hbm, full, sem = refs
-    join(cap, kxs, oct_axis, lox_ref, lo_hbm, sem, go_start)
+    dg_ref, gg_ref, bg_ref, cg_ref, mean_out, var_out, left_ref, full = refs
     for n in range(4):
         at = pl.ds(pl.multiple_of(column_block(axes, n) * 128, 128), 128)
         full[:, at] = parts[n][...].astype(f32)
     ins, cols = direction_ref.shape
     cats, code_width = mean_ref.shape
-    shapes = (full.shape[0] - 16 - (ins - code_width)) // 2
+    shapes = (full.shape[0] - (ins - code_width)) // 2
     width = ins - code_width
     ps = full[width : width + shapes, :]
     info = full[width + shapes : width + 2 * shapes, :]
@@ -806,16 +857,15 @@
         own = own + jnp.where(iota((8, 1), 0) == s, row, 0.0)
     both = lax.dot_general(jnp.concatenate(halves(own), axis=0), w_ref[...], (((1,), (1,)), ((), ())), preferred_element_type=f32)
     cg_ref[...] = (both[:8] + both[8:])[:span, hid : hid + code_width]
-    left_ref[0] = jnp.max(full[width + 2 * shapes : width + 2 * shapes + 8, :128])
-    join(cap, kxs, oct_axis, lox_ref, lo_hbm, sem, go_wait)
-
-
-def finish(axes, span, cap, kxs, categories, momentum, lox, lo, parts, direction, gain, norms, weight, prev_mean, prev_var):
+    left_ref[0] = jnp.max(info[:, at + 192 :])
+
+
+def finish(axes, span, categories, momentum, parts, direction, gain, norms, weight, prev_mean, prev_var):
     ins, outs = direction.shape
     return pl.pallas_call(
-        functools.partial(finish_kernel, axes, "shape", "oct", HID, span, cap, kxs),
-        in_specs=specs("ssva" + "v" * 10),
-        out_specs=specs("v" * 6 + "sa"),
+        functools.partial(finish_kernel, axes, "shape", HID, span),
+        in_specs=specs("ss" + "v" * 10),
+        out_specs=specs("v" * 6 + "s"),
         out_shape=[
             jax.ShapeDtypeStruct((ins, outs), f32),
             jax.ShapeDtypeStruct((1, outs), f32),
@@ -824,14 +874,12 @@
             jax.ShapeDtypeStruct(prev_mean.shape, f32),
             jax.ShapeDtypeStruct(prev_mean.shape, f32),
             jax.ShapeDtypeStruct((1,), f32),
-            pltpu.HBM(lo.shape, bf16),
         ],
-        input_output_aliases={3: 7},
-        scratch_shapes=[pltpu.VMEM((parts[0].shape[0], outs), f32), pltpu.SemaphoreType.DMA((len(kxs),))],
+        scratch_shapes=[pltpu.VMEM((parts[0].shape[0], outs), f32)],
         compiler_params=params(12),
         cost_estimate=cost("finish"),
         name="finish",
-    )(categories, momentum, keep(lox), stay(lo), *[keep(p) for p in parts], keep(direction), keep(gain), keep(norms), keep(weight), prev_mean, prev_var)
+    )(categories, momentum, *[keep(p) for p in parts], keep(direction), keep(gain), keep(norms), keep(weight), prev_mean, prev_var)
 
 
 def swap(v, axis, k):
@@ -874,7 +922,7 @@
 def collect(mine, theirs, olds, gw, info, codes, lo, lof, shapes, blocks, cap, message, usual, steps):
     span = codes.shape[0]
     far = len(theirs)
-    rows = gw.shape[0] - 16 + 2 * shapes + 16
+    rows = gw.shape[0] - 16 + 2 * shapes
     out = pl.pallas_call(
         functools.partial(collect_kernel, AXES, "shape", "oct", shapes, span, far, blocks, cap, message, usual, steps),
         in_specs=specs("s" + "s" * far + "v" * far + "vvvaa"),
@@ -900,19 +948,19 @@
     messages = plan_messages(usual, steps)
     points_in = [m for m, (first, _) in enumerate(messages) if first < usual]
 
-    (ct_near, ct_far, x_near), heads, queues, rows_far, (row_near, mine, near_names, info) = pack(
+    (ct_near, ct_far, x_near), heads, queues, rows_far, (row_near, mine, labels, pos) = pack(
         octants, shape_ids, point_inputs, cotangent, messages, oct_count, span, cap)
     ctn, ctf = swap(ct_near, "oct", 1), swap(ct_far, "oct", 1)
     got = {(k, m): swap(heads[2 * (k - 1) + m], "oct", 2 * k) for k in far for m in range(2)}
-    lo, lon, gw, buf, wp, wpt, weight, cb, norms, direction_v, gain_v = prepare(
-        mine, row_near, x_near, direction, gain, bias, codes, oct_count, cap)
+    gw, buf, wp, wpt, weight, cb, norms, direction_v, gain_v, near_names, info = prepare(
+        mine, row_near, labels, pos, x_near, direction, gain, bias, codes, oct_count, cap)
     weights = (wp, wpt, cb)
-    lo, lon, lof, gw, buf = local(mine, near_names, cotangent, ctn, weights, lo, lon, gw, buf, len(far), blocks, span, cap)
+    lo, lon, lof, gw, buf = local(mine, near_names, cotangent, ctn, weights, gw, buf, len(far), blocks, span, cap)
 
     queue = {k: queues[k - 1] for k in far}
     named, theirs, back, ahead = {}, {}, {}, {}
     for k in far:
-        named[k], theirs[k], back[k] = make_names(after(got[k, 0], gw)[messages[0][1] * UNIT :], k, span, cap)
+        named[k], theirs[k], back[k] = make_names(after(got[k, 0], gw)[messages[0][1] * TILE :], k, span, cap)
         ahead[k] = ()
     for m in points_in:
         for k in far:
@@ -926,18 +974,19 @@
             gw = after(gw, part)
     their = [theirs[k] for k in far]
     lasts = list(range(len(points_in), len(messages)))
-    order = ((), (0,), (), (1,)) if usual % 2 else ()
+    order = ((), (0,), (), (1,)) if len(lasts) == 2 else ()
     before = [[got[k, lasts[i]] for k in far for i in ii] for ii in order] + [[] for _ in range(20)]
     parts, lo, lof = collect(mine, their, [ahead[k][-1] for k in far], gw, info, codes, lo, lof, shapes, blocks, cap,
                              messages[points_in[-1]], usual, steps)
     lox = swap(lof, "oct", 1)
+    input_grad = unpack(mine, their, rows_far, [messages[m] for m in lasts], [got[k, m] for k in far for m in lasts], part,
+                        [back[k] for k in far])
     for v in total_quarter(parts, before):
         pass
     parts = [v] + quarters_to([v] * 3)
-    input_grad = unpack(mine, their, rows_far, [messages[m] for m in lasts], [got[k, m] for k in far for m in lasts], part,
-                        [back[k] for k in far])
-    direction_grad, gain_grad, bias_grad, code_grad, running_mean, running_var, left, lo = finish(
-        AXES, span, cap, tuple(far), categories, momentum, lox, lo, [after(parts[0], input_grad)] + parts[1:], direction_v, gain_v, norms, weight, prev_mean, prev_var)
+    lo = merge(lox, lo, cap, far)
+    direction_grad, gain_grad, bias_grad, code_grad, running_mean, running_var, left = finish(
+        AXES, span, categories, momentum, [after(parts[0], lo, input_grad)] + parts[1:], direction_v, gain_v, norms, weight, prev_mean, prev_var)
     outputs = (
         lo,
         input_grad,
@@ -953,7 +1002,7 @@
 
 def body(*args):
     points, oct_count = args[0].shape[0], lax.axis_size("oct")
-    most = units(2 * (2 * points // oct_count) // TILE)
+    most = 2 * (2 * points // oct_count) // TILE
     all_steps = max(most, LEAD) + most
     usual, steps = min(USUAL, most), min(STEPS, all_steps)
     outputs, left = run(usual, steps, *args)

time: 85.9 us -> 82.6 us (0.962)
  starting transfers between devices: 31.7 us -> 14.8 us
  Pallas kernels: 35.3 us -> 43.5 us
  waiting for transfers between devices: 17.1 us -> 22.1 us
    ppermute x17, starting transfers between devices: 29.5 us -> 12.3 us  [swap(): return lax.ppermute(v, axis, [(i, i ^ k) for i in range(n)])]
    ppermute x17, waiting for transfers between devices: 14.9 us -> 20 us  [swap(): return lax.ppermute(v, axis, [(i, i ^ k) for i in range(n)])]
    pallas_call x4, Pallas kernels: 9.22 us -> 13.5 us  [far_step(): pl.pallas_call(functools.partial(far_kernel, message, before, after_it, e...]
    pallas_call x1, Pallas kernels: 6.52 us -> 10.8 us  [local(): pl.pallas_call(functools.partial(local_kernel, 'oct', far, blocks, span,...]
    pallas_call x2 -> x3, Pallas kernels: 8.09 us -> 7.46 us  [the longest x1 3.78 us: prepare(): pl.pallas_call(functools.partial(prepare_kernel, oct_count, 'oct', codes....]
  transfers between devices with their start and end apart: 19 -> 19, of which waited for: 10 -> 9; matrix products, arithmetic and copies ran while one was open for 0% -> 0% of each run, Pallas kernels for 33% -> 46%
where the time goes in v3:
time: 82.6 us; the launch traced here: 82.3 us
  Pallas kernels  43.5 us (53%)
  waiting for transfers between devices  22.1 us (27%)
  starting transfers between devices  14.8 us (18%)
  between operations  1.11 us (1%)
    ppermute x17, waiting for transfers between devices, swap(): return lax.ppermute(v, axis, [(i, i ^ k) for i in range(n)])  20 us
    pallas_call x4, Pallas kernels, far_step(): pl.pallas_call(functools.partial(far_kernel, message, before, after_it, e...  13.5 us
    ppermute x17, starting transfers between devices, swap(): return lax.ppermute(v, axis, [(i, i ^ k) for i in range(n)])  12.3 us
    pallas_call x1, Pallas kernels, local(): pl.pallas_call(functools.partial(local_kernel, 'oct', far, blocks, span,...  10.8 us
    pallas_call x1, Pallas kernels, unpack(): pl.pallas_call(functools.partial(unpack_kernel, far, blocks, lasts), in_s...  3.96 us
    pallas_call x1, Pallas kernels, prepare(): pl.pallas_call(functools.partial(prepare_kernel, oct_count, 'oct', codes....  3.78 us
    pallas_call x1, Pallas kernels, pack(): pl.pallas_call(functools.partial(pack_kernel, oct_count, sizes, 'shape',...  3.05 us
    ppermute x2, starting transfers between devices, swap_both(): return lax.ppermute(v, ('shape', 'oct'), [(i, i ^ k) for i in range(n * m)])  2.54 us
  transfers between devices with their start and end apart: 19, of which 9 were waited for; matrix products, arithmetic and copies ran while one was open for 0% of the time, Pallas kernels for 46%

profile of v3, /device:TPU:0, one launch (start us, length us, event | category | flops | bytes accessed | tf_op | source)
XLA Modules:
  0.0 82.3 jit_solution(13818643223930894655)
XLA Ops:
  0.6 0.0 copy-start.6
  0.6 3.0 %pack.3 = (bf16[2048,512]{1,0:T(8,128)(2,1)S(1)}, bf16[2048,512]{1,0:T(8,128)(2,1)S(1)}, bf16[4096,256]{1,0:T(8,128)(2,1)S(1)}, bf16[1040,256]{1,0:T(8,128)(2,1)...) custom-call(s32[32,128]{1,0:T(8,128)} %bitcast.13, ...), custom_call_target="tpu_custom_call" | custom-call | flops 30000001024 | bytes 1 | tf_op jit(solution)/shard_map/pack/pallas_call | solution.py:280
  3.7 0.5 collective-permute-start.22
  4.2 2.6 %collective-permute-start.21 = (bf16[1040,256]{1,0:T(8,128)(2,1)S(1)}, bf16[1040,256]{1,0:T(8,128)(2,1)S(1)}, u32[]{:S(2)}, u32[]{:S(2)}) collective-permute-start(bf16[1040,256]{1,0:T(8,128)(2,1)S(1)} %get-tuple-element.277), channel_id=1, source_target_pairs={{0,2},{1,3},{2,0},{3,1},{4,6},{5,7},{6,4},{7,5},{8,10},{9,11},{10,... | collective-permute-start | bytes 1597448 | tf_op jit(solution)/shard_map/ppermute | solution.py:887
  6.8 0.2 collective-permute-start.24
  7.0 0.3 collective-permute-start.23
  7.2 3.8 %prepare.3 = (f32[272,512]{1,0:T(8,128)S(1)}, bf16[4624,256]{1,0:T(8,128)(2,1)S(1)}, bf16[256,512]{1,0:T(8,128)(2,1)S(1)}, bf16[512,256]{1,0:T(8,128)(2,1)S(1)},...) custom-call(s32[8,128]{1,0:T(8,128)S(1)} %get-tuple-element.276.boun, ...), custom_call_target="tpu_custom_call" | custom-call | flops 30000001024 | bytes 1 | tf_op jit(solution)/shard_map/prepare/pallas_call | solution.py:354
  11.0 10.8 %local.3 = (bf16[8192,512]{1,0:T(8,128)(2,1)}, bf16[2048,512]{1,0:T(8,128)(2,1)}, bf16[2048,512]{1,0:T(8,128)(2,1)}, f32[272,512]{1,0:T(8,128)S(1)}, bf16[4624,256]{1,0:T(8,128)(2,1)S(1)}) custom-call(s32[8,128]{1,0:T(8,128)S(1)} %get-tuple-element.276.bounds.mine.refs_0_, ...), custom_call_target="tpu_custom_call", output_to_operand_aliasing={{3}: (7, {}), {4}: (8, {})} | custom-call | flops 30000001024 | bytes 1 | tf_op jit(solution)/shard_map/local/pallas_call | solution.py:516
  21.8 0.1 collective-permute-start.27
  22.0 0.9 %names.3 = (s32[16,256]{1,0:T(8,128)S(1)}, s32[8,128]{1,0:T(8,128)S(1)}, bf16[4608,256]{1,0:T(8,128)(2,1)S(1)}) custom-call(bf16[16,256]{1,0:T(8,128)(2,1)S(1)} %slice.6.labels_ref), custom_call_target="tpu_custom_call" | custom-call | flops 30000001024 | bytes 1 | tf_op jit(solution)/shard_map/names/pallas_call | solution.py:577
  22.9 4.3 %far.12 = (bf16[8192,256]{1,0:T(8,128)(2,1)S(1)}, bf16[8192,512]{1,0:T(8,128)(2,1)}, bf16[2048,512]{1,0:T(8,128)(2,1)}, f32[272,512]{1,0:T(8,128)S(1)}, bf16[460...) custom-call(s32[8,128]{1,0:T(8,128)S(1)} %get-tuple-element.276.boun, ...), custom_call_target="tpu_custom_call", output_to_operand_aliasing={{0}: (9, {}), {1}: (10, {}), {2}: (11, {}), {3}: (12, {}), ... | custom-call | flops 30000001024 | bytes 1 | tf_op jit(solution)/shard_map/far/pallas_call | solution.py:673
  27.2 0.1 collective-permute-start.26
  27.3 3.7 %collective-permute-done.23.refs_1_ = bf16[1024,256]{1,0:T(8,128)(2,1)S(1)} collective-permute-done((bf16[1024,256]{1,0:T(8,128)(2,1)S(1)}, bf16[1024,256]{1,0:T(8,128)(2,1)S(1)}, u32[]{:S(2)}, u32[]{:S(2)}) %collective-permute-start.23) | collective-permute-done | bytes 524320 | tf_op jit(solution)/shard_map/ppermute | solution.py:887
  31.0 3.4 %far.13 = (bf16[8192,256]{1,0:T(8,128)(2,1)S(1)}, bf16[8192,512]{1,0:T(8,128)(2,1)}, bf16[2048,512]{1,0:T(8,128)(2,1)}, f32[272,512]{1,0:T(8,128)S(1)}, bf16[460...) custom-call(s32[8,128]{1,0:T(8,128)S(1)} %get-tuple-element.276.boun, ...), custom_call_target="tpu_custom_call", output_to_operand_aliasing={{0}: (9, {}), {1}: (10, {}), {2}: (11, {}), {3}: (12, {}), ... | custom-call | flops 30000001024 | bytes 1 | tf_op jit(solution)/shard_map/far/pallas_call | solution.py:673
  34.4 1.0 %collective-permute-start.25 = (bf16[512,256]{1,0:T(8,128)(2,1)S(1)}, bf16[512,256]{1,0:T(8,128)(2,1)S(1)}, u32[]{:S(2)}, u32[]{:S(2)}) collective-permute-start(bf16[512,256]{1,0:T(8,128)(2,1)S(1)} %get-tuple-element.306), channel_id=1, source_target_pairs={{0,2},{1,3},{2,0},{3,1},{4,6},{5,7},{6,4},{7,5},{8,10},{9,11},{10,... | collective-permute-start | bytes 786440 | tf_op jit(solution)/shard_map/ppermute | solution.py:887
  35.4 0.0 collective-permute-done.27.lon_ref
  35.4 2.3 %unlocal.3 = (bf16[4096,256]{1,0:T(8,128)(2,1)S(1)}, bf16[8192,512]{1,0:T(8,128)(2,1)}) custom-call(s32[8,128]{1,0:T(8,128)S(1)} %get-tuple-element.276.bounds.mine.refs_0_, s32[16,256]{1,0:T(8,128)S(1)} %get-tuple-element.278.row_ref, bf16[4624,256]{1,0:T(8,128)(2,1)S(1)} %get-tuple-element.311.gbuf, ...), custom_call_target="tpu_custom_call", output_to_operand_aliasing={{1}: (4, {})} | custom-call | flops 10000000 | bytes 1 | tf_op jit(solution)/shard_map/unlocal/pallas_call | solution.py:552
  37.7 1.7 %collective-permute-done.26.refs_1_ = bf16[768,256]{1,0:T(8,128)(2,1)S(1)} collective-permute-done((bf16[768,256]{1,0:T(8,128)(2,1)S(1)}, bf16[768,256]{1,0:T(8,128)(2,1)S(1)}, u32[]{:S(2)}, u32[]{:S(2)}) %collective-permute-start.26) | collective-permute-done | bytes 393248 | tf_op jit(solution)/shard_map/ppermute | solution.py:887
  39.4 3.5 %far.14 = (bf16[8192,256]{1,0:T(8,128)(2,1)S(1)}, bf16[8192,512]{1,0:T(8,128)(2,1)}, bf16[2048,512]{1,0:T(8,128)(2,1)}, f32[272,512]{1,0:T(8,128)S(1)}, bf16[460...) custom-call(s32[8,128]{1,0:T(8,128)S(1)} %get-tuple-element.276.boun, ...), custom_call_target="tpu_custom_call", output_to_operand_aliasing={{0}: (9, {}), {1}: (10, {}), {2}: (11, {}), {3}: (12, {}), ... | custom-call | flops 30000001024 | bytes 1 | tf_op jit(solution)/shard_map/far/pallas_call | solution.py:673
  42.9 0.2 collective-permute-start.32
  43.2 1.6 %collective-permute-done.25.refs_1_ = bf16[512,256]{1,0:T(8,128)(2,1)S(1)} collective-permute-done((bf16[512,256]{1,0:T(8,128)(2,1)S(1)}, bf16[512,256]{1,0:T(8,128)(2,1)S(1)}, u32[]{:S(2)}, u32[]{:S(2)}) %collective-permute-start.25) | collective-permute-done | bytes 262176 | tf_op jit(solution)/shard_map/ppermute | solution.py:887
  44.8 2.3 %far.15 = (bf16[8192,256]{1,0:T(8,128)(2,1)S(1)}, bf16[8192,512]{1,0:T(8,128)(2,1)}, bf16[2048,512]{1,0:T(8,128)(2,1)}, f32[272,512]{1,0:T(8,128)S(1)}, bf16[460...) custom-call(s32[8,128]{1,0:T(8,128)S(1)} %get-tuple-element.276.boun, ...), custom_call_target="tpu_custom_call", output_to_operand_aliasing={{0}: (9, {}), {1}: (10, {}), {2}: (11, {}), {3}: (12, {}), ... | custom-call | flops 10000000 | bytes 1 | tf_op jit(solution)/shard_map/far/pallas_call | solution.py:673
  47.0 1.5 %collect.3 = (bf16[288,128]{1,0:T(8,128)(2,1)S(1)}, bf16[288,128]{1,0:T(8,128)(2,1)S(1)}, bf16[288,128]{1,0:T(8,128)(2,1)S(1)}, bf16[288,128]{1,0:T(8,128)(2,1)S...) custom-call(s32[8,128]{1,0:T(8,128)S(1)} %get-tuple-element.276.bounds.mi, ...), custom_call_target="tpu_custom_call", output_to_operand_aliasing={{4}: (6, {}), {5}: (7, {})} | custom-call | flops 10000000 | bytes 1 | tf_op jit(solution)/shard_map/collect/pallas_call | solution.py:926
  48.5 1.0 %collective-permute-start.30 = (bf16[288,128]{1,0:T(8,128)(2,1)S(1)}, bf16[288,128]{1,0:T(8,128)(2,1)S(1)}, u32[]{:S(2)}, u32[]{:S(2)}) collective-permute-start(bf16[288,128]{1,0:T(8,128)(2,1)S(1)} %get-tuple-element.336), channel_id=1, source_target_pairs={{0,5},{1,4},{2,7},{3,6},{4,1},{5,0},{6,3},{7,2},{8,13},{9,12},{10,... | collective-permute-start | bytes 221192 | tf_op jit(solution)/shard_map/ppermute | solution.py:892
  49.6 0.9 %collective-permute-start.28 = (bf16[288,128]{1,0:T(8,128)(2,1)S(1)}, bf16[288,128]{1,0:T(8,128)(2,1)S(1)}, u32[]{:S(2)}, u32[]{:S(2)}) collective-permute-start(bf16[288,128]{1,0:T(8,128)(2,1)S(1)} %get-tuple-element.334), channel_id=1, source_target_pairs={{0,1},{1,0},{2,3},{3,2},{4,5},{5,4},{6,7},{7,6},{8,9},{9,8},{10,11... | collective-permute-start | bytes 221192 | tf_op jit(solution)/shard_map/ppermute | solution.py:887
  50.5 0.3 collective-permute-start.29
  50.7 2.1 %collective-permute-done.30 = bf16[288,128]{1,0:T(8,128)(2,1)S(1)} collective-permute-done((bf16[288,128]{1,0:T(8,128)(2,1)S(1)}, bf16[288,128]{1,0:T(8,128)(2,1)S(1)}, u32[]{:S(2)}, u32[]{:S(2)}) %collective-permute-start.30) | collective-permute-done | bytes 73760 | tf_op jit(solution)/shard_map/ppermute | solution.py:892
  52.8 2.0 %collective-permute-done.29 = bf16[288,128]{1,0:T(8,128)(2,1)S(1)} collective-permute-done((bf16[288,128]{1,0:T(8,128)(2,1)S(1)}, bf16[288,128]{1,0:T(8,128)(2,1)S(1)}, u32[]{:S(2)}, u32[]{:S(2)}) %collective-permute-start.29) | collective-permute-done | bytes 73760 | tf_op jit(solution)/shard_map/ppermute | solution.py:887
  54.9 1.6 %collective-permute-start.31 = (bf16[288,128]{1,0:T(8,128)(2,1)S(1)}, bf16[288,128]{1,0:T(8,128)(2,1)S(1)}, u32[]{:S(2)}, u32[]{:S(2)}) collective-permute-start(bf16[288,128]{1,0:T(8,128)(2,1)S(1)} %add_convert_fusion.7), channel_id=1, source_target_pairs={{0,8},{4,12},{8,0},{12,4},{16,24},{20,28},{24,16},{28,20},{1,9},{5... | collective-permute-start | bytes 221192 | tf_op jit(solution)/shard_map/ppermute | solution.py:887
  56.5 0.3 collective-permute-start.35
  56.8 2.5 %collective-permute-done.31 = bf16[288,128]{1,0:T(8,128)(2,1)S(1)} collective-permute-done((bf16[288,128]{1,0:T(8,128)(2,1)S(1)}, bf16[288,128]{1,0:T(8,128)(2,1)S(1)}, u32[]{:S(2)}, u32[]{:S(2)}) %collective-permute-start.31) | collective-permute-done | bytes 73760 | tf_op jit(solution)/shard_map/ppermute | solution.py:887
  59.3 3.7 %collective-permute-start.33 = (bf16[288,128]{1,0:T(8,128)(2,1)S(1)}, bf16[288,128]{1,0:T(8,128)(2,1)S(1)}, u32[]{:S(2)}, u32[]{:S(2)}) collective-permute-start(bf16[288,128]{1,0:T(8,128)(2,1)S(1)} %add_convert_fusion.6), channel_id=1, source_target_pairs={{0,16},{4,20},{8,24},{12,28},{16,0},{20,4},{24,8},{28,12},{1,17},{... | collective-permute-start | bytes 221192 | tf_op jit(solution)/shard_map/ppermute | solution.py:887
  63.0 3.4 %collective-permute-done.33 = bf16[288,128]{1,0:T(8,128)(2,1)S(1)} collective-permute-done((bf16[288,128]{1,0:T(8,128)(2,1)S(1)}, bf16[288,128]{1,0:T(8,128)(2,1)S(1)}, u32[]{:S(2)}, u32[]{:S(2)}) %collective-permute-start.33) | collective-permute-done | bytes 73760 | tf_op jit(solution)/shard_map/ppermute | solution.py:887
  66.4 0.1 collective-permute-start.34
  66.5 0.1 collective-permute-start.36
  66.6 4.3 %collective-permute-done.35.refs_3_ = bf16[1024,256]{1,0:T(8,128)(2,1)S(1)} collective-permute-done((bf16[1024,256]{1,0:T(8,128)(2,1)S(1)}, bf16[1024,256]{1,0:T(8,128)(2,1)S(1)}, u32[]{:S(2)}, u32[]{:S(2)}) %collective-permute-start.35) | collective-permute-done | bytes 524320 | tf_op jit(solution)/shard_map/ppermute | solution.py:887
  70.9 0.8 collective-permute-done.34
  71.7 0.1 collective-permute-start.37
  71.8 0.3 collective-permute-start.38
  72.2 1.5 %collective-permute-start.39 = (bf16[288,128]{1,0:T(8,128)(2,1)S(1)}, bf16[288,128]{1,0:T(8,128)(2,1)S(1)}, u32[]{:S(2)}, u32[]{:S(2)}) collective-permute-start(bf16[288,128]{1,0:T(8,128)(2,1)S(1)} %add_convert_fusion.4.refs_0_), channel_id=1, source_target_pairs={{0,5},{1,4},{2,7},{3,6},{4,1},{5,0},{6,3},{7,2},{8,13},{9,12},{10,... | collective-permute-start | bytes 221192 | tf_op jit(solution)/shard_map/ppermute | solution.py:892
  73.7 4.0 %unpack.3 = (bf16[4096,256]{1,0:T(8,128)(2,1)}, bf16[4608,256]{1,0:T(8,128)(2,1)S(1)}) custom-call(s32[8,128]{1,0:T(8,128)S(1)} %get-tuple-element.276.bounds.mine.refs_0_, s32[8,128]{1,0:T(8,128)S(1)} %get-tuple-element.291.theirs.refs_1_.refs_0_, s32[16,256]{1,0:T(8,128)S(1)} %get-tuple-element.343.refs_1_, ...), custom_call_target="tpu_custom_call", output_to_operand_aliasing={{1}: (6, {})} | custom-call | flops 30000001024 | bytes 1 | tf_op jit(solution)/shard_map/unpack/pallas_call | solution.py:714
  77.6 0.0 copy-start.14
  77.7 0.0 copy-start.16
  77.7 1.3 %merge.3 = bf16[8192,512]{1,0:T(8,128)(2,1)} custom-call(bf16[2048,512]{1,0:T(8,128)(2,1)S(1)} %collective-permute-done.36.lox_ref, bf16[8192,512]{1,0:T(8,128)(2,1)} %get-tuple-element.342.lo_in), custom_call_target="tpu_custom_call", output_to_operand_aliasing={{}: (1, {})} | custom-call | flops 10000000 | bytes 1 | tf_op jit(solution)/shard_map/merge/pallas_call | solution.py:740
  79.0 0.0 collective-permute-done.38.refs_2_
  79.1 0.0 copy-start.8
  79.1 2.3 %finish.3 = (f32[512,512]{1,0:T(8,128)}, f32[1,512]{1,0:T(1,128)}, f32[1,512]{1,0:T(1,128)}, f32[2,256]{1,0:T(2,128)}, f32[5,256]{1,0:T(8,128)}, /*index=5*/f32[5,256]{1,0:T(8,128)}, f32[1]{0:T(128)}) custom-call(s32[16]{0:T(128)S(1)} %copy-done.14, f32[5]{0:T(128)S(1)} %copy-done.16, bf16[288,128]{1,0:T(8,128)(2,1)S(1)} %add_convert_fusion.4.refs_0_, ...), custom_call_target="tpu_custom_call" | custom-call | flops 30000001024 | bytes 1 | tf_op jit(solution)/shard_map/finish/pallas_call | solution.py:865
  81.5 0.7 while.23
  (23 shorter events, 0.2 us)
Async XLA Ops:
  0.6 6.6 %copy-start.6 = (bf16[2,256]{1,0:T(2,128)(2,1)S(1)}, bf16[2,256]{1,0:T(2,128)(2,1)}, u32[]{:S(2)}) copy-start(bf16[2,256]{1,0:T(2,128)(2,1)} %refs_5_.1) | copy-start | bytes 3076
  3.7 7.3 %collective-permute-start.22 = (bf16[2048,512]{1,0:T(8,128)(2,1)S(1)}, bf16[2048,512]{1,0:T(8,128)(2,1)S(1)}, u32[]{:S(2)}, u32[]{:S(2)}) collective-permute-start(bf16[2048,512]{1,0:T(8,128)(2,1)S(1)} %get-tuple-element.283), channel_id=1, source_target_pairs={{0,1},{1,0},{2,3},{3,2},{4,5},{5,4},{6,7},{7,6},{8,9},{9,8},{10,11... | collective-permute-start | bytes 6291464 | tf_op jit(solution)/shard_map/ppermute | solution.py:887
  4.2 17.6 %collective-permute-start.21 = (bf16[1040,256]{1,0:T(8,128)(2,1)S(1)}, bf16[1040,256]{1,0:T(8,128)(2,1)S(1)}, u32[]{:S(2)}, u32[]{:S(2)}) collective-permute-start(bf16[1040,256]{1,0:T(8,128)(2,1)S(1)} %get-tuple-element.277), channel_id=1, source_target_pairs={{0,2},{1,3},{2,0},{3,1},{4,6},{5,7},{6,4},{7,5},{8,10},{9,11},{10,... | collective-permute-start | bytes 1597448 | tf_op jit(solution)/shard_map/ppermute | solution.py:887
  6.8 16.1 %collective-permute-start.24 = (bf16[2048,512]{1,0:T(8,128)(2,1)S(1)}, bf16[2048,512]{1,0:T(8,128)(2,1)S(1)}, u32[]{:S(2)}, u32[]{:S(2)}) collective-permute-start(bf16[2048,512]{1,0:T(8,128)(2,1)S(1)} %get-tuple-element.294), channel_id=1, source_target_pairs={{0,1},{1,0},{2,3},{3,2},{4,5},{5,4},{6,7},{7,6},{8,9},{9,8},{10,11... | collective-permute-start | bytes 6291464 | tf_op jit(solution)/shard_map/ppermute | solution.py:887
  7.0 24.0 %collective-permute-start.23 = (bf16[1024,256]{1,0:T(8,128)(2,1)S(1)}, bf16[1024,256]{1,0:T(8,128)(2,1)S(1)}, u32[]{:S(2)}, u32[]{:S(2)}) collective-permute-start(bf16[1024,256]{1,0:T(8,128)(2,1)S(1)} %get-tuple-element.293), channel_id=1, source_target_pairs={{0,2},{1,3},{2,0},{3,1},{4,6},{5,7},{6,4},{7,5},{8,10},{9,11},{10,... | collective-permute-start | bytes 1572872 | tf_op jit(solution)/shard_map/ppermute | solution.py:887
  21.8 13.6 %collective-permute-start.27 = (bf16[2048,512]{1,0:T(8,128)(2,1)}, bf16[2048,512]{1,0:T(8,128)(2,1)S(1)}, u32[]{:S(2)}, u32[]{:S(2)}) collective-permute-start(bf16[2048,512]{1,0:T(8,128)(2,1)} %get-tuple-element.312), channel_id=1, source_target_pairs={{0,1},{1,0},{2,3},{3,2},{4,5},{5,4},{6,7},{7,6},{8,9},{9,8},{10,11... | collective-permute-start | bytes 6291464 | tf_op jit(solution)/shard_map/ppermute | solution.py:887
  27.2 12.2 %collective-permute-start.26 = (bf16[768,256]{1,0:T(8,128)(2,1)S(1)}, bf16[768,256]{1,0:T(8,128)(2,1)S(1)}, u32[]{:S(2)}, u32[]{:S(2)}) collective-permute-start(bf16[768,256]{1,0:T(8,128)(2,1)S(1)} %get-tuple-element.307), channel_id=1, source_target_pairs={{0,2},{1,3},{2,0},{3,1},{4,6},{5,7},{6,4},{7,5},{8,10},{9,11},{10,... | collective-permute-start | bytes 1179656 | tf_op jit(solution)/shard_map/ppermute | solution.py:887
  34.4 10.3 %collective-permute-start.25 = (bf16[512,256]{1,0:T(8,128)(2,1)S(1)}, bf16[512,256]{1,0:T(8,128)(2,1)S(1)}, u32[]{:S(2)}, u32[]{:S(2)}) collective-permute-start(bf16[512,256]{1,0:T(8,128)(2,1)S(1)} %get-tuple-element.306), channel_id=1, source_target_pairs={{0,2},{1,3},{2,0},{3,1},{4,6},{5,7},{6,4},{7,5},{8,10},{9,11},{10,... | collective-permute-start | bytes 786440 | tf_op jit(solution)/shard_map/ppermute | solution.py:887
  42.9 16.4 %collective-permute-start.32 = (bf16[1024,256]{1,0:T(8,128)(2,1)S(1)}, bf16[1024,256]{1,0:T(8,128)(2,1)S(1)}, u32[]{:S(2)}, u32[]{:S(2)}) collective-permute-start(bf16[1024,256]{1,0:T(8,128)(2,1)S(1)} %get-tuple-element.337), channel_id=1, source_target_pairs={{0,2},{1,3},{2,0},{3,1},{4,6},{5,7},{6,4},{7,5},{8,10},{9,11},{10,... | collective-permute-start | bytes 1572872 | tf_op jit(solution)/shard_map/ppermute | solution.py:887
  44.8 2.3 %copy-start.7 = (bf16[2,256]{1,0:T(2,128)(2,1)S(1)}, bf16[2,256]{1,0:T(2,128)(2,1)}, u32[]{:S(2)}) copy-start(bf16[2,256]{1,0:T(2,128)(2,1)} %refs_5_.1) | copy-start | bytes 3076
  48.5 4.3 %collective-permute-start.30 = (bf16[288,128]{1,0:T(8,128)(2,1)S(1)}, bf16[288,128]{1,0:T(8,128)(2,1)S(1)}, u32[]{:S(2)}, u32[]{:S(2)}) collective-permute-start(bf16[288,128]{1,0:T(8,128)(2,1)S(1)} %get-tuple-element.336), channel_id=1, source_target_pairs={{0,5},{1,4},{2,7},{3,6},{4,1},{5,0},{6,3},{7,2},{8,13},{9,12},{10,... | collective-permute-start | bytes 221192 | tf_op jit(solution)/shard_map/ppermute | solution.py:892
  49.6 3.3 %collective-permute-start.28 = (bf16[288,128]{1,0:T(8,128)(2,1)S(1)}, bf16[288,128]{1,0:T(8,128)(2,1)S(1)}, u32[]{:S(2)}, u32[]{:S(2)}) collective-permute-start(bf16[288,128]{1,0:T(8,128)(2,1)S(1)} %get-tuple-element.334), channel_id=1, source_target_pairs={{0,1},{1,0},{2,3},{3,2},{4,5},{5,4},{6,7},{7,6},{8,9},{9,8},{10,11... | collective-permute-start | bytes 221192 | tf_op jit(solution)/shard_map/ppermute | solution.py:887
  50.5 4.4 %collective-permute-start.29 = (bf16[288,128]{1,0:T(8,128)(2,1)S(1)}, bf16[288,128]{1,0:T(8,128)(2,1)S(1)}, u32[]{:S(2)}, u32[]{:S(2)}) collective-permute-start(bf16[288,128]{1,0:T(8,128)(2,1)S(1)} %get-tuple-element.335), channel_id=1, source_target_pairs={{0,4},{4,0},{8,12},{12,8},{16,20},{20,16},{24,28},{28,24},{1,5},{5... | collective-permute-start | bytes 221192 | tf_op jit(solution)/shard_map/ppermute | solution.py:887
  54.9 4.4 %collective-permute-start.31 = (bf16[288,128]{1,0:T(8,128)(2,1)S(1)}, bf16[288,128]{1,0:T(8,128)(2,1)S(1)}, u32[]{:S(2)}, u32[]{:S(2)}) collective-permute-start(bf16[288,128]{1,0:T(8,128)(2,1)S(1)} %add_convert_fusion.7), channel_id=1, source_target_pairs={{0,8},{4,12},{8,0},{12,4},{16,24},{20,28},{24,16},{28,20},{1,9},{5... | collective-permute-start | bytes 221192 | tf_op jit(solution)/shard_map/ppermute | solution.py:887
  56.5 14.4 %collective-permute-start.35 = (bf16[1024,256]{1,0:T(8,128)(2,1)S(1)}, bf16[1024,256]{1,0:T(8,128)(2,1)S(1)}, u32[]{:S(2)}, u32[]{:S(2)}) collective-permute-start(bf16[1024,256]{1,0:T(8,128)(2,1)S(1)} %get-tuple-element.339), channel_id=1, source_target_pairs={{0,2},{1,3},{2,0},{3,1},{4,6},{5,7},{6,4},{7,5},{8,10},{9,11},{10,... | collective-permute-start | bytes 1572872 | tf_op jit(solution)/shard_map/ppermute | solution.py:887
  59.3 7.1 %collective-permute-start.33 = (bf16[288,128]{1,0:T(8,128)(2,1)S(1)}, bf16[288,128]{1,0:T(8,128)(2,1)S(1)}, u32[]{:S(2)}, u32[]{:S(2)}) collective-permute-start(bf16[288,128]{1,0:T(8,128)(2,1)S(1)} %add_convert_fusion.6), channel_id=1, source_target_pairs={{0,16},{4,20},{8,24},{12,28},{16,0},{20,4},{24,8},{28,12},{1,17},{... | collective-permute-start | bytes 221192 | tf_op jit(solution)/shard_map/ppermute | solution.py:887
  66.4 5.3 %collective-permute-start.34 = (bf16[288,128]{1,0:T(8,128)(2,1)S(1)}, bf16[288,128]{1,0:T(8,128)(2,1)S(1)}, u32[]{:S(2)}, u32[]{:S(2)}) collective-permute-start(bf16[288,128]{1,0:T(8,128)(2,1)S(1)} %add_convert_fusion.5), channel_id=1, source_target_pairs={{0,2},{1,3},{2,0},{3,1},{4,6},{5,7},{6,4},{7,5},{8,10},{9,11},{10,... | collective-permute-start | bytes 221192 | tf_op jit(solution)/shard_map/ppermute | solution.py:887
  66.5 11.1 %collective-permute-start.36 = (bf16[2048,512]{1,0:T(8,128)(2,1)}, bf16[2048,512]{1,0:T(8,128)(2,1)S(1)}, u32[]{:S(2)}, u32[]{:S(2)}) collective-permute-start(bf16[2048,512]{1,0:T(8,128)(2,1)} %get-tuple-element.341), channel_id=1, source_target_pairs={{0,1},{1,0},{2,3},{3,2},{4,5},{5,4},{6,7},{7,6},{8,9},{9,8},{10,11... | collective-permute-start | bytes 6291464 | tf_op jit(solution)/shard_map/ppermute | solution.py:887
  71.7 7.3 %collective-permute-start.37 = (bf16[288,128]{1,0:T(8,128)(2,1)S(1)}, bf16[288,128]{1,0:T(8,128)(2,1)S(1)}, u32[]{:S(2)}, u32[]{:S(2)}) collective-permute-start(bf16[288,128]{1,0:T(8,128)(2,1)S(1)} %add_convert_fusion.4.refs_0_), channel_id=1, source_target_pairs={{0,1},{1,0},{2,3},{3,2},{4,5},{5,4},{6,7},{7,6},{8,9},{9,8},{10,11... | collective-permute-start | bytes 221192 | tf_op jit(solution)/shard_map/ppermute | solution.py:887
  71.8 7.2 %collective-permute-start.38 = (bf16[288,128]{1,0:T(8,128)(2,1)S(1)}, bf16[288,128]{1,0:T(8,128)(2,1)S(1)}, u32[]{:S(2)}, u32[]{:S(2)}) collective-permute-start(bf16[288,128]{1,0:T(8,128)(2,1)S(1)} %add_convert_fusion.4.refs_0_), channel_id=1, source_target_pairs={{0,4},{4,0},{8,12},{12,8},{16,20},{20,16},{24,28},{28,24},{1,5},{5... | collective-permute-start | bytes 221192 | tf_op jit(solution)/shard_map/ppermute | solution.py:887
  72.2 6.9 %collective-permute-start.39 = (bf16[288,128]{1,0:T(8,128)(2,1)S(1)}, bf16[288,128]{1,0:T(8,128)(2,1)S(1)}, u32[]{:S(2)}, u32[]{:S(2)}) collective-permute-start(bf16[288,128]{1,0:T(8,128)(2,1)S(1)} %add_convert_fusion.4.refs_0_), channel_id=1, source_target_pairs={{0,5},{1,4},{2,7},{3,6},{4,1},{5,0},{6,3},{7,2},{8,13},{9,12},{10,... | collective-permute-start | bytes 221192 | tf_op jit(solution)/shard_map/ppermute | solution.py:892
  77.6 1.4 %copy-start.10 = (f32[5,256]{1,0:T(8,128)S(1)}, f32[5,256]{1,0:T(8,128)}, u32[]{:S(2)}) copy-start(f32[5,256]{1,0:T(8,128)} %refs_8_.1) | copy-start | bytes 15364
  77.6 1.4 %copy-start.12 = (f32[5,256]{1,0:T(8,128)S(1)}, f32[5,256]{1,0:T(8,128)}, u32[]{:S(2)}) copy-start(f32[5,256]{1,0:T(8,128)} %refs_9_.1) | copy-start | bytes 15364
  77.6 1.4 %copy-start.14 = (s32[16]{0:T(128)S(1)}, s32[16]{0:T(128)}, u32[]{:S(2)}) copy-start(s32[16]{0:T(128)} %categories.1) | copy-start | bytes 196
  77.7 1.4 %copy-start.16 = (f32[5]{0:T(128)S(1)}, f32[5]{0:T(128)}, u32[]{:S(2)}) copy-start(f32[5]{0:T(128)} %momentum.1) | copy-start | bytes 64
  79.1 2.4 %copy-start.8 = (bf16[2,256]{1,0:T(2,128)(2,1)S(1)}, bf16[2,256]{1,0:T(2,128)(2,1)}, u32[]{:S(2)}) copy-start(bf16[2,256]{1,0:T(2,128)(2,1)} %refs_5_.1) | copy-start | bytes 3076

commit v4 on v3

--- a/solution.py
+++ b/solution.py
@@ -689,7 +689,13 @@
     theirs, rows_far, refs = refs[:far], refs[far : 2 * far], refs[2 * far :]
     parts, refs = refs[: far * len(lasts)], refs[far * len(lasts) :]
     part_ref, refs = refs[0], refs[1 + far :]
-    out_ref, backs, moved = refs[0], refs[1 : 1 + far], refs[-1]
+    out_hbm, backs, (moved, out_ref, sem) = refs[0], refs[1 : 1 + far], refs[-3:]
+    group = max(1, blocks // 4)
+
+    def send(n):
+        rows = pl.ds(n * group * BLOCK, group * BLOCK)
+        return pltpu.make_async_copy(out_ref.at[rows, :], out_hbm.at[rows, :], sem.at[n])
+
     for k in range(far):
         for j, (first, number) in enumerate(lasts):
             take_back(first, number, theirs[k], blocks, parts[k * len(lasts) + j], 0, backs[k])
@@ -702,8 +708,12 @@
             at = slice(b * BLOCK, (b + 1) * BLOCK)
             before = part_ref if k == 0 else out_ref
             out_ref[at, :] = (value + before[at, :].astype(f32)).astype(bf16)
+            if k == far - 1 and (b + 1) % group == 0:
+                send(b // group).start()
 
         unsort_rows(bounds, rows_far[k], [2 + 2 * k, 3 + 2 * k], blocks, pick, moved, emit)
+    for n in range(blocks // group):
+        send(n).wait()
 
 
 def unpack(bounds, theirs, rows_far, lasts, parts, part, backs):
@@ -714,10 +724,14 @@
     return pl.pallas_call(
         functools.partial(unpack_kernel, far, blocks, lasts),
         in_specs=specs("s" + "s" * far + "v" * (2 * far + extra + 1)),
-        out_specs=specs("v" * (1 + far)),
-        out_shape=[jax.ShapeDtypeStruct(part.shape, bf16)] + [pltpu.VMEM(b.shape, bf16) for b in backs],
+        out_specs=specs("a" + "v" * far),
+        out_shape=[pltpu.HBM(part.shape, bf16)] + [pltpu.VMEM(b.shape, bf16) for b in backs],
         input_output_aliases={2 * far + extra + 2 + k: 1 + k for k in range(far)},
-        scratch_shapes=[pltpu.VMEM((blocks * window_rows(2, 128) + WIN, width), bf16)],
+        scratch_shapes=[
+            pltpu.VMEM((blocks * window_rows(2, 128) + WIN, width), bf16),
+            pltpu.VMEM(part.shape, bf16),
+            pltpu.SemaphoreType.DMA((4,)),
+        ],
         compiler_params=params(20),
         cost_estimate=cost("unpack"),
         name="unpack",

time: 82.6 us -> 81.6 us (0.988); the launches traced: 82.3 us -> 80.5 us
  waiting for transfers between devices: 22.1 us -> 19.4 us
  starting transfers between devices: 14.8 us -> 16.2 us
    ppermute x17, starting transfers between devices: 12.3 us -> 15.8 us  [swap(): return lax.ppermute(v, axis, [(i, i ^ k) for i in range(n)])]
    ppermute x17, waiting for transfers between devices: 20 us -> 17.3 us  [swap(): return lax.ppermute(v, axis, [(i, i ^ k) for i in range(n)])]
    ppermute x2, starting transfers between devices: 2.54 us -> 0.43 us  [swap_both(): return lax.ppermute(v, ('shape', 'oct'), [(i, i ^ k) for i in range(n * m)])]
    pallas_call x1, Pallas kernels: 10.8 us -> 12 us  [local(): pl.pallas_call(functools.partial(local_kernel, 'oct', far, blocks, span,...]
  transfers between devices with their start and end apart: 19 -> 19, of which waited for: 9 -> 9; matrix products, arithmetic and copies ran while one was open for 0% -> 0% of each run, Pallas kernels for 46% -> 47%
where the time goes in v4:
time: 81.6 us; the launch traced here: 80.5 us
  Pallas kernels  42.9 us (53%)
  waiting for transfers between devices  19.4 us (24%)
  starting transfers between devices  16.2 us (20%)
  between operations  1.15 us (1%)
    ppermute x17, waiting for transfers between devices, swap(): return lax.ppermute(v, axis, [(i, i ^ k) for i in range(n)])  17.3 us
    ppermute x17, starting transfers between devices, swap(): return lax.ppermute(v, axis, [(i, i ^ k) for i in range(n)])  15.8 us
    pallas_call x4, Pallas kernels, far_step(): pl.pallas_call(functools.partial(far_kernel, message, before, after_it, e...  12.8 us
    pallas_call x1, Pallas kernels, local(): pl.pallas_call(functools.partial(local_kernel, 'oct', far, blocks, span,...  12 us
    pallas_call x1, Pallas kernels, prepare(): pl.pallas_call(functools.partial(prepare_kernel, oct_count, 'oct', codes....  3.75 us
    pallas_call x1, Pallas kernels, unpack(): pl.pallas_call(functools.partial(unpack_kernel, far, blocks, lasts), in_s...  3.47 us
    pallas_call x1, Pallas kernels, pack(): pl.pallas_call(functools.partial(pack_kernel, oct_count, sizes, 'shape',...  3.05 us
    pallas_call x1, Pallas kernels, finish(): pl.pallas_call(functools.partial(finish_kernel, axes, 'shape', HID, span)...  2.34 us
  transfers between devices with their start and end apart: 19, of which 9 were waited for; matrix products, arithmetic and copies ran while one was open for 0% of the time, Pallas kernels for 47%

profile of v4, /device:TPU:0, one launch (start us, length us, event | category | flops | bytes accessed | tf_op | source)
XLA Modules:
  0.0 80.5 jit_solution(9654050760103649211)
XLA Ops:
  0.6 0.0 copy-start.6
  0.6 3.0 %pack.3 = (bf16[2048,512]{1,0:T(8,128)(2,1)S(1)}, bf16[2048,512]{1,0:T(8,128)(2,1)S(1)}, bf16[4096,256]{1,0:T(8,128)(2,1)S(1)}, bf16[1040,256]{1,0:T(8,128)(2,1)...) custom-call(s32[32,128]{1,0:T(8,128)} %bitcast.13, ...), custom_call_target="tpu_custom_call" | custom-call | flops 30000001024 | bytes 1 | tf_op jit(solution)/shard_map/pack/pallas_call | solution.py:280
  3.7 0.5 collective-permute-start.22
  4.2 2.6 %collective-permute-start.21 = (bf16[1040,256]{1,0:T(8,128)(2,1)S(1)}, bf16[1040,256]{1,0:T(8,128)(2,1)S(1)}, u32[]{:S(2)}, u32[]{:S(2)}) collective-permute-start(bf16[1040,256]{1,0:T(8,128)(2,1)S(1)} %get-tuple-element.277), channel_id=1, source_target_pairs={{0,2},{1,3},{2,0},{3,1},{4,6},{5,7},{6,4},{7,5},{8,10},{9,11},{10,... | collective-permute-start | bytes 1597448 | tf_op jit(solution)/shard_map/ppermute | solution.py:901
  6.8 0.2 collective-permute-start.24
  7.0 0.3 collective-permute-start.23
  7.2 3.7 %prepare.3 = (f32[272,512]{1,0:T(8,128)S(1)}, bf16[4624,256]{1,0:T(8,128)(2,1)S(1)}, bf16[256,512]{1,0:T(8,128)(2,1)S(1)}, bf16[512,256]{1,0:T(8,128)(2,1)S(1)},...) custom-call(s32[8,128]{1,0:T(8,128)S(1)} %get-tuple-element.276.boun, ...), custom_call_target="tpu_custom_call" | custom-call | flops 30000001024 | bytes 1 | tf_op jit(solution)/shard_map/prepare/pallas_call | solution.py:354
  11.0 12.0 %local.3 = (bf16[8192,512]{1,0:T(8,128)(2,1)}, bf16[2048,512]{1,0:T(8,128)(2,1)}, bf16[2048,512]{1,0:T(8,128)(2,1)}, f32[272,512]{1,0:T(8,128)S(1)}, bf16[4624,256]{1,0:T(8,128)(2,1)S(1)}) custom-call(s32[8,128]{1,0:T(8,128)S(1)} %get-tuple-element.276.bounds.mine.refs_0_, ...), custom_call_target="tpu_custom_call", output_to_operand_aliasing={{3}: (7, {}), {4}: (8, {})} | custom-call | flops 30000001024 | bytes 1 | tf_op jit(solution)/shard_map/local/pallas_call | solution.py:516
  23.0 0.1 collective-permute-start.27
  23.1 0.9 %names.3 = (s32[16,256]{1,0:T(8,128)S(1)}, s32[8,128]{1,0:T(8,128)S(1)}, bf16[4608,256]{1,0:T(8,128)(2,1)S(1)}) custom-call(bf16[16,256]{1,0:T(8,128)(2,1)S(1)} %slice.6.labels_ref), custom_call_target="tpu_custom_call" | custom-call | flops 30000001024 | bytes 1 | tf_op jit(solution)/shard_map/names/pallas_call | solution.py:577
  24.1 4.3 %far.12 = (bf16[8192,256]{1,0:T(8,128)(2,1)S(1)}, bf16[8192,512]{1,0:T(8,128)(2,1)}, bf16[2048,512]{1,0:T(8,128)(2,1)}, f32[272,512]{1,0:T(8,128)S(1)}, bf16[460...) custom-call(s32[8,128]{1,0:T(8,128)S(1)} %get-tuple-element.276.boun, ...), custom_call_target="tpu_custom_call", output_to_operand_aliasing={{0}: (9, {}), {1}: (10, {}), {2}: (11, {}), {3}: (12, {}), ... | custom-call | flops 30000001024 | bytes 1 | tf_op jit(solution)/shard_map/far/pallas_call | solution.py:673
  28.4 0.1 collective-permute-start.26
  28.4 2.3 %collective-permute-done.23.refs_1_ = bf16[1024,256]{1,0:T(8,128)(2,1)S(1)} collective-permute-done((bf16[1024,256]{1,0:T(8,128)(2,1)S(1)}, bf16[1024,256]{1,0:T(8,128)(2,1)S(1)}, u32[]{:S(2)}, u32[]{:S(2)}) %collective-permute-start.23) | collective-permute-done | bytes 524320 | tf_op jit(solution)/shard_map/ppermute | solution.py:901
  30.7 3.4 %far.13 = (bf16[8192,256]{1,0:T(8,128)(2,1)S(1)}, bf16[8192,512]{1,0:T(8,128)(2,1)}, bf16[2048,512]{1,0:T(8,128)(2,1)}, f32[272,512]{1,0:T(8,128)S(1)}, bf16[460...) custom-call(s32[8,128]{1,0:T(8,128)S(1)} %get-tuple-element.276.boun, ...), custom_call_target="tpu_custom_call", output_to_operand_aliasing={{0}: (9, {}), {1}: (10, {}), {2}: (11, {}), {3}: (12, {}), ... | custom-call | flops 30000001024 | bytes 1 | tf_op jit(solution)/shard_map/far/pallas_call | solution.py:673
  34.2 1.3 %collective-permute-start.25 = (bf16[512,256]{1,0:T(8,128)(2,1)S(1)}, bf16[512,256]{1,0:T(8,128)(2,1)S(1)}, u32[]{:S(2)}, u32[]{:S(2)}) collective-permute-start(bf16[512,256]{1,0:T(8,128)(2,1)S(1)} %get-tuple-element.306), channel_id=1, source_target_pairs={{0,2},{1,3},{2,0},{3,1},{4,6},{5,7},{6,4},{7,5},{8,10},{9,11},{10,... | collective-permute-start | bytes 786440 | tf_op jit(solution)/shard_map/ppermute | solution.py:901
  35.4 2.3 %unlocal.3 = (bf16[4096,256]{1,0:T(8,128)(2,1)S(1)}, bf16[8192,512]{1,0:T(8,128)(2,1)}) custom-call(s32[8,128]{1,0:T(8,128)S(1)} %get-tuple-element.276.bounds.mine.refs_0_, s32[16,256]{1,0:T(8,128)S(1)} %get-tuple-element.278.row_ref, bf16[4624,256]{1,0:T(8,128)(2,1)S(1)} %get-tuple-element.311.gbuf, ...), custom_call_target="tpu_custom_call", output_to_operand_aliasing={{1}: (4, {})} | custom-call | flops 10000000 | bytes 1 | tf_op jit(solution)/shard_map/unlocal/pallas_call | solution.py:552
  37.7 2.6 %collective-permute-done.26.refs_1_ = bf16[768,256]{1,0:T(8,128)(2,1)S(1)} collective-permute-done((bf16[768,256]{1,0:T(8,128)(2,1)S(1)}, bf16[768,256]{1,0:T(8,128)(2,1)S(1)}, u32[]{:S(2)}, u32[]{:S(2)}) %collective-permute-start.26) | collective-permute-done | bytes 393248 | tf_op jit(solution)/shard_map/ppermute | solution.py:901
  40.4 3.4 %far.14 = (bf16[8192,256]{1,0:T(8,128)(2,1)S(1)}, bf16[8192,512]{1,0:T(8,128)(2,1)}, bf16[2048,512]{1,0:T(8,128)(2,1)}, f32[272,512]{1,0:T(8,128)S(1)}, bf16[460...) custom-call(s32[8,128]{1,0:T(8,128)S(1)} %get-tuple-element.276.boun, ...), custom_call_target="tpu_custom_call", output_to_operand_aliasing={{0}: (9, {}), {1}: (10, {}), {2}: (11, {}), {3}: (12, {}), ... | custom-call | flops 30000001024 | bytes 1 | tf_op jit(solution)/shard_map/far/pallas_call | solution.py:673
  43.8 0.1 collective-permute-start.32
  43.9 1.6 %collective-permute-done.25.refs_1_ = bf16[512,256]{1,0:T(8,128)(2,1)S(1)} collective-permute-done((bf16[512,256]{1,0:T(8,128)(2,1)S(1)}, bf16[512,256]{1,0:T(8,128)(2,1)S(1)}, u32[]{:S(2)}, u32[]{:S(2)}) %collective-permute-start.25) | collective-permute-done | bytes 262176 | tf_op jit(solution)/shard_map/ppermute | solution.py:901
  45.4 1.7 %far.15 = (bf16[8192,256]{1,0:T(8,128)(2,1)S(1)}, bf16[8192,512]{1,0:T(8,128)(2,1)}, bf16[2048,512]{1,0:T(8,128)(2,1)}, f32[272,512]{1,0:T(8,128)S(1)}, bf16[460...) custom-call(s32[8,128]{1,0:T(8,128)S(1)} %get-tuple-element.276.boun, ...), custom_call_target="tpu_custom_call", output_to_operand_aliasing={{0}: (9, {}), {1}: (10, {}), {2}: (11, {}), {3}: (12, {}), ... | custom-call | flops 10000000 | bytes 1 | tf_op jit(solution)/shard_map/far/pallas_call | solution.py:673
  47.1 0.9 %collect.3 = (bf16[288,128]{1,0:T(8,128)(2,1)S(1)}, bf16[288,128]{1,0:T(8,128)(2,1)S(1)}, bf16[288,128]{1,0:T(8,128)(2,1)S(1)}, bf16[288,128]{1,0:T(8,128)(2,1)S...) custom-call(s32[8,128]{1,0:T(8,128)S(1)} %get-tuple-element.276.bounds.mi, ...), custom_call_target="tpu_custom_call", output_to_operand_aliasing={{4}: (6, {}), {5}: (7, {})} | custom-call | flops 10000000 | bytes 1 | tf_op jit(solution)/shard_map/collect/pallas_call | solution.py:940
  48.0 0.4 collective-permute-start.30
  48.4 0.8 collective-permute-start.28
  49.1 1.1 %collective-permute-start.29 = (bf16[288,128]{1,0:T(8,128)(2,1)S(1)}, bf16[288,128]{1,0:T(8,128)(2,1)S(1)}, u32[]{:S(2)}, u32[]{:S(2)}) collective-permute-start(bf16[288,128]{1,0:T(8,128)(2,1)S(1)} %get-tuple-element.335), channel_id=1, source_target_pairs={{0,4},{4,0},{8,12},{12,8},{16,20},{20,16},{24,28},{28,24},{1,5},{5... | collective-permute-start | bytes 221192 | tf_op jit(solution)/shard_map/ppermute | solution.py:901
  50.2 2.1 %collective-permute-done.30 = bf16[288,128]{1,0:T(8,128)(2,1)S(1)} collective-permute-done((bf16[288,128]{1,0:T(8,128)(2,1)S(1)}, bf16[288,128]{1,0:T(8,128)(2,1)S(1)}, u32[]{:S(2)}, u32[]{:S(2)}) %collective-permute-start.30) | collective-permute-done | bytes 73760 | tf_op jit(solution)/shard_map/ppermute | solution.py:906
  52.3 1.6 %collective-permute-done.29 = bf16[288,128]{1,0:T(8,128)(2,1)S(1)} collective-permute-done((bf16[288,128]{1,0:T(8,128)(2,1)S(1)}, bf16[288,128]{1,0:T(8,128)(2,1)S(1)}, u32[]{:S(2)}, u32[]{:S(2)}) %collective-permute-start.29) | collective-permute-done | bytes 73760 | tf_op jit(solution)/shard_map/ppermute | solution.py:901
  53.9 1.4 %collective-permute-start.31 = (bf16[288,128]{1,0:T(8,128)(2,1)S(1)}, bf16[288,128]{1,0:T(8,128)(2,1)S(1)}, u32[]{:S(2)}, u32[]{:S(2)}) collective-permute-start(bf16[288,128]{1,0:T(8,128)(2,1)S(1)} %add_convert_fusion.7), channel_id=1, source_target_pairs={{0,8},{4,12},{8,0},{12,4},{16,24},{20,28},{24,16},{28,20},{1,9},{5... | collective-permute-start | bytes 221192 | tf_op jit(solution)/shard_map/ppermute | solution.py:901
  55.3 1.5 %collective-permute-start.35 = (bf16[1024,256]{1,0:T(8,128)(2,1)S(1)}, bf16[1024,256]{1,0:T(8,128)(2,1)S(1)}, u32[]{:S(2)}, u32[]{:S(2)}) collective-permute-start(bf16[1024,256]{1,0:T(8,128)(2,1)S(1)} %get-tuple-element.339), channel_id=1, source_target_pairs={{0,2},{1,3},{2,0},{3,1},{4,6},{5,7},{6,4},{7,5},{8,10},{9,11},{10,... | collective-permute-start | bytes 1572872 | tf_op jit(solution)/shard_map/ppermute | solution.py:901
  56.8 1.5 %collective-permute-done.31 = bf16[288,128]{1,0:T(8,128)(2,1)S(1)} collective-permute-done((bf16[288,128]{1,0:T(8,128)(2,1)S(1)}, bf16[288,128]{1,0:T(8,128)(2,1)S(1)}, u32[]{:S(2)}, u32[]{:S(2)}) %collective-permute-start.31) | collective-permute-done | bytes 73760 | tf_op jit(solution)/shard_map/ppermute | solution.py:901
  58.3 3.5 %collective-permute-start.33 = (bf16[288,128]{1,0:T(8,128)(2,1)S(1)}, bf16[288,128]{1,0:T(8,128)(2,1)S(1)}, u32[]{:S(2)}, u32[]{:S(2)}) collective-permute-start(bf16[288,128]{1,0:T(8,128)(2,1)S(1)} %add_convert_fusion.6), channel_id=1, source_target_pairs={{0,16},{4,20},{8,24},{12,28},{16,0},{20,4},{24,8},{28,12},{1,17},{... | collective-permute-start | bytes 221192 | tf_op jit(solution)/shard_map/ppermute | solution.py:901
  61.9 3.1 %collective-permute-done.33 = bf16[288,128]{1,0:T(8,128)(2,1)S(1)} collective-permute-done((bf16[288,128]{1,0:T(8,128)(2,1)S(1)}, bf16[288,128]{1,0:T(8,128)(2,1)S(1)}, u32[]{:S(2)}, u32[]{:S(2)}) %collective-permute-start.33) | collective-permute-done | bytes 73760 | tf_op jit(solution)/shard_map/ppermute | solution.py:901
  65.0 0.1 collective-permute-start.34
  65.1 0.1 collective-permute-start.36
  65.2 3.8 %collective-permute-done.35.refs_3_ = bf16[1024,256]{1,0:T(8,128)(2,1)S(1)} collective-permute-done((bf16[1024,256]{1,0:T(8,128)(2,1)S(1)}, bf16[1024,256]{1,0:T(8,128)(2,1)S(1)}, u32[]{:S(2)}, u32[]{:S(2)}) %collective-permute-start.35) | collective-permute-done | bytes 524320 | tf_op jit(solution)/shard_map/ppermute | solution.py:901
  69.0 0.8 collective-permute-done.34
  69.8 0.1 collective-permute-start.37
  69.9 2.3 %collective-permute-start.38 = (bf16[288,128]{1,0:T(8,128)(2,1)S(1)}, bf16[288,128]{1,0:T(8,128)(2,1)S(1)}, u32[]{:S(2)}, u32[]{:S(2)}) collective-permute-start(bf16[288,128]{1,0:T(8,128)(2,1)S(1)} %add_convert_fusion.4.refs_0_), channel_id=1, source_target_pairs={{0,4},{4,0},{8,12},{12,8},{16,20},{20,16},{24,28},{28,24},{1,5},{5... | collective-permute-start | bytes 221192 | tf_op jit(solution)/shard_map/ppermute | solution.py:901
  72.2 0.1 collective-permute-start.39
  72.3 3.5 %unpack.3 = (bf16[4096,256]{1,0:T(8,128)(2,1)}, bf16[4608,256]{1,0:T(8,128)(2,1)S(1)}) custom-call(s32[8,128]{1,0:T(8,128)S(1)} %get-tuple-element.276.bounds.mine.refs_0_, s32[8,128]{1,0:T(8,128)S(1)} %get-tuple-element.291.theirs.refs_1_.refs_0_, s32[16,256]{1,0:T(8,128)S(1)} %get-tuple-element.343.refs_1_, ...), custom_call_target="tpu_custom_call", output_to_operand_aliasing={{1}: (6, {})} | custom-call | flops 30000001024 | bytes 1 | tf_op jit(solution)/shard_map/unpack/pallas_call | solution.py:724
  75.7 0.0 copy-start.10
  75.8 0.0 copy-start.12
  75.8 0.0 copy-start.14
  75.8 0.0 copy-start.16
  75.8 1.3 %merge.3 = bf16[8192,512]{1,0:T(8,128)(2,1)} custom-call(bf16[2048,512]{1,0:T(8,128)(2,1)S(1)} %collective-permute-done.36.lox_ref, bf16[8192,512]{1,0:T(8,128)(2,1)} %get-tuple-element.342.lo_in), custom_call_target="tpu_custom_call", output_to_operand_aliasing={{}: (1, {})} | custom-call | flops 10000000 | bytes 1 | tf_op jit(solution)/shard_map/merge/pallas_call | solution.py:754
  77.2 0.0 copy-start.8
  77.2 2.3 %finish.3 = (f32[512,512]{1,0:T(8,128)}, f32[1,512]{1,0:T(1,128)}, f32[1,512]{1,0:T(1,128)}, f32[2,256]{1,0:T(2,128)}, f32[5,256]{1,0:T(8,128)}, /*index=5*/f32[5,256]{1,0:T(8,128)}, f32[1]{0:T(128)}) custom-call(s32[16]{0:T(128)S(1)} %copy-done.14, f32[5]{0:T(128)S(1)} %copy-done.16, bf16[288,128]{1,0:T(8,128)(2,1)S(1)} %add_convert_fusion.4.refs_0_, ...), custom_call_target="tpu_custom_call" | custom-call | flops 30000001024 | bytes 1 | tf_op jit(solution)/shard_map/finish/pallas_call | solution.py:879
  79.6 0.7 while.23
  (23 shorter events, 0.2 us)
Async XLA Ops:
  0.6 6.6 %copy-start.6 = (bf16[2,256]{1,0:T(2,128)(2,1)S(1)}, bf16[2,256]{1,0:T(2,128)(2,1)}, u32[]{:S(2)}) copy-start(bf16[2,256]{1,0:T(2,128)(2,1)} %refs_5_.1) | copy-start | bytes 3076
  3.7 7.3 %collective-permute-start.22 = (bf16[2048,512]{1,0:T(8,128)(2,1)S(1)}, bf16[2048,512]{1,0:T(8,128)(2,1)S(1)}, u32[]{:S(2)}, u32[]{:S(2)}) collective-permute-start(bf16[2048,512]{1,0:T(8,128)(2,1)S(1)} %get-tuple-element.283), channel_id=1, source_target_pairs={{0,1},{1,0},{2,3},{3,2},{4,5},{5,4},{6,7},{7,6},{8,9},{9,8},{10,11... | collective-permute-start | bytes 6291464 | tf_op jit(solution)/shard_map/ppermute | solution.py:901
  4.2 18.8 %collective-permute-start.21 = (bf16[1040,256]{1,0:T(8,128)(2,1)S(1)}, bf16[1040,256]{1,0:T(8,128)(2,1)S(1)}, u32[]{:S(2)}, u32[]{:S(2)}) collective-permute-start(bf16[1040,256]{1,0:T(8,128)(2,1)S(1)} %get-tuple-element.277), channel_id=1, source_target_pairs={{0,2},{1,3},{2,0},{3,1},{4,6},{5,7},{6,4},{7,5},{8,10},{9,11},{10,... | collective-permute-start | bytes 1597448 | tf_op jit(solution)/shard_map/ppermute | solution.py:901
  6.8 17.3 %collective-permute-start.24 = (bf16[2048,512]{1,0:T(8,128)(2,1)S(1)}, bf16[2048,512]{1,0:T(8,128)(2,1)S(1)}, u32[]{:S(2)}, u32[]{:S(2)}) collective-permute-start(bf16[2048,512]{1,0:T(8,128)(2,1)S(1)} %get-tuple-element.294), channel_id=1, source_target_pairs={{0,1},{1,0},{2,3},{3,2},{4,5},{5,4},{6,7},{7,6},{8,9},{9,8},{10,11... | collective-permute-start | bytes 6291464 | tf_op jit(solution)/shard_map/ppermute | solution.py:901
  7.0 23.8 %collective-permute-start.23 = (bf16[1024,256]{1,0:T(8,128)(2,1)S(1)}, bf16[1024,256]{1,0:T(8,128)(2,1)S(1)}, u32[]{:S(2)}, u32[]{:S(2)}) collective-permute-start(bf16[1024,256]{1,0:T(8,128)(2,1)S(1)} %get-tuple-element.293), channel_id=1, source_target_pairs={{0,2},{1,3},{2,0},{3,1},{4,6},{5,7},{6,4},{7,5},{8,10},{9,11},{10,... | collective-permute-start | bytes 1572872 | tf_op jit(solution)/shard_map/ppermute | solution.py:901
  23.0 12.4 %collective-permute-start.27 = (bf16[2048,512]{1,0:T(8,128)(2,1)}, bf16[2048,512]{1,0:T(8,128)(2,1)S(1)}, u32[]{:S(2)}, u32[]{:S(2)}) collective-permute-start(bf16[2048,512]{1,0:T(8,128)(2,1)} %get-tuple-element.312), channel_id=1, source_target_pairs={{0,1},{1,0},{2,3},{3,2},{4,5},{5,4},{6,7},{7,6},{8,9},{9,8},{10,11... | collective-permute-start | bytes 6291464 | tf_op jit(solution)/shard_map/ppermute | solution.py:901
  28.4 12.0 %collective-permute-start.26 = (bf16[768,256]{1,0:T(8,128)(2,1)S(1)}, bf16[768,256]{1,0:T(8,128)(2,1)S(1)}, u32[]{:S(2)}, u32[]{:S(2)}) collective-permute-start(bf16[768,256]{1,0:T(8,128)(2,1)S(1)} %get-tuple-element.307), channel_id=1, source_target_pairs={{0,2},{1,3},{2,0},{3,1},{4,6},{5,7},{6,4},{7,5},{8,10},{9,11},{10,... | collective-permute-start | bytes 1179656 | tf_op jit(solution)/shard_map/ppermute | solution.py:901
  34.2 11.3 %collective-permute-start.25 = (bf16[512,256]{1,0:T(8,128)(2,1)S(1)}, bf16[512,256]{1,0:T(8,128)(2,1)S(1)}, u32[]{:S(2)}, u32[]{:S(2)}) collective-permute-start(bf16[512,256]{1,0:T(8,128)(2,1)S(1)} %get-tuple-element.306), channel_id=1, source_target_pairs={{0,2},{1,3},{2,0},{3,1},{4,6},{5,7},{6,4},{7,5},{8,10},{9,11},{10,... | collective-permute-start | bytes 786440 | tf_op jit(solution)/shard_map/ppermute | solution.py:901
  43.8 14.5 %collective-permute-start.32 = (bf16[1024,256]{1,0:T(8,128)(2,1)S(1)}, bf16[1024,256]{1,0:T(8,128)(2,1)S(1)}, u32[]{:S(2)}, u32[]{:S(2)}) collective-permute-start(bf16[1024,256]{1,0:T(8,128)(2,1)S(1)} %get-tuple-element.337), channel_id=1, source_target_pairs={{0,2},{1,3},{2,0},{3,1},{4,6},{5,7},{6,4},{7,5},{8,10},{9,11},{10,... | collective-permute-start | bytes 1572872 | tf_op jit(solution)/shard_map/ppermute | solution.py:901
  45.4 1.7 %copy-start.7 = (bf16[2,256]{1,0:T(2,128)(2,1)S(1)}, bf16[2,256]{1,0:T(2,128)(2,1)}, u32[]{:S(2)}) copy-start(bf16[2,256]{1,0:T(2,128)(2,1)} %refs_5_.1) | copy-start | bytes 3076
  48.0 4.3 %collective-permute-start.30 = (bf16[288,128]{1,0:T(8,128)(2,1)S(1)}, bf16[288,128]{1,0:T(8,128)(2,1)S(1)}, u32[]{:S(2)}, u32[]{:S(2)}) collective-permute-start(bf16[288,128]{1,0:T(8,128)(2,1)S(1)} %get-tuple-element.336), channel_id=1, source_target_pairs={{0,5},{1,4},{2,7},{3,6},{4,1},{5,0},{6,3},{7,2},{8,13},{9,12},{10,... | collective-permute-start | bytes 221192 | tf_op jit(solution)/shard_map/ppermute | solution.py:906
  48.4 3.9 %collective-permute-start.28 = (bf16[288,128]{1,0:T(8,128)(2,1)S(1)}, bf16[288,128]{1,0:T(8,128)(2,1)S(1)}, u32[]{:S(2)}, u32[]{:S(2)}) collective-permute-start(bf16[288,128]{1,0:T(8,128)(2,1)S(1)} %get-tuple-element.334), channel_id=1, source_target_pairs={{0,1},{1,0},{2,3},{3,2},{4,5},{5,4},{6,7},{7,6},{8,9},{9,8},{10,11... | collective-permute-start | bytes 221192 | tf_op jit(solution)/shard_map/ppermute | solution.py:901
  49.1 4.7 %collective-permute-start.29 = (bf16[288,128]{1,0:T(8,128)(2,1)S(1)}, bf16[288,128]{1,0:T(8,128)(2,1)S(1)}, u32[]{:S(2)}, u32[]{:S(2)}) collective-permute-start(bf16[288,128]{1,0:T(8,128)(2,1)S(1)} %get-tuple-element.335), channel_id=1, source_target_pairs={{0,4},{4,0},{8,12},{12,8},{16,20},{20,16},{24,28},{28,24},{1,5},{5... | collective-permute-start | bytes 221192 | tf_op jit(solution)/shard_map/ppermute | solution.py:901
  53.9 4.4 %collective-permute-start.31 = (bf16[288,128]{1,0:T(8,128)(2,1)S(1)}, bf16[288,128]{1,0:T(8,128)(2,1)S(1)}, u32[]{:S(2)}, u32[]{:S(2)}) collective-permute-start(bf16[288,128]{1,0:T(8,128)(2,1)S(1)} %add_convert_fusion.7), channel_id=1, source_target_pairs={{0,8},{4,12},{8,0},{12,4},{16,24},{20,28},{24,16},{28,20},{1,9},{5... | collective-permute-start | bytes 221192 | tf_op jit(solution)/shard_map/ppermute | solution.py:901
  55.3 13.7 %collective-permute-start.35 = (bf16[1024,256]{1,0:T(8,128)(2,1)S(1)}, bf16[1024,256]{1,0:T(8,128)(2,1)S(1)}, u32[]{:S(2)}, u32[]{:S(2)}) collective-permute-start(bf16[1024,256]{1,0:T(8,128)(2,1)S(1)} %get-tuple-element.339), channel_id=1, source_target_pairs={{0,2},{1,3},{2,0},{3,1},{4,6},{5,7},{6,4},{7,5},{8,10},{9,11},{10,... | collective-permute-start | bytes 1572872 | tf_op jit(solution)/shard_map/ppermute | solution.py:901
  58.3 6.7 %collective-permute-start.33 = (bf16[288,128]{1,0:T(8,128)(2,1)S(1)}, bf16[288,128]{1,0:T(8,128)(2,1)S(1)}, u32[]{:S(2)}, u32[]{:S(2)}) collective-permute-start(bf16[288,128]{1,0:T(8,128)(2,1)S(1)} %add_convert_fusion.6), channel_id=1, source_target_pairs={{0,16},{4,20},{8,24},{12,28},{16,0},{20,4},{24,8},{28,12},{1,17},{... | collective-permute-start | bytes 221192 | tf_op jit(solution)/shard_map/ppermute | solution.py:901
  65.0 4.8 %collective-permute-start.34 = (bf16[288,128]{1,0:T(8,128)(2,1)S(1)}, bf16[288,128]{1,0:T(8,128)(2,1)S(1)}, u32[]{:S(2)}, u32[]{:S(2)}) collective-permute-start(bf16[288,128]{1,0:T(8,128)(2,1)S(1)} %add_convert_fusion.5), channel_id=1, source_target_pairs={{0,2},{1,3},{2,0},{3,1},{4,6},{5,7},{6,4},{7,5},{8,10},{9,11},{10,... | collective-permute-start | bytes 221192 | tf_op jit(solution)/shard_map/ppermute | solution.py:901
  65.1 10.6 %collective-permute-start.36 = (bf16[2048,512]{1,0:T(8,128)(2,1)}, bf16[2048,512]{1,0:T(8,128)(2,1)S(1)}, u32[]{:S(2)}, u32[]{:S(2)}) collective-permute-start(bf16[2048,512]{1,0:T(8,128)(2,1)} %get-tuple-element.341), channel_id=1, source_target_pairs={{0,1},{1,0},{2,3},{3,2},{4,5},{5,4},{6,7},{7,6},{8,9},{9,8},{10,11... | collective-permute-start | bytes 6291464 | tf_op jit(solution)/shard_map/ppermute | solution.py:901
  69.8 7.3 %collective-permute-start.37 = (bf16[288,128]{1,0:T(8,128)(2,1)S(1)}, bf16[288,128]{1,0:T(8,128)(2,1)S(1)}, u32[]{:S(2)}, u32[]{:S(2)}) collective-permute-start(bf16[288,128]{1,0:T(8,128)(2,1)S(1)} %add_convert_fusion.4.refs_0_), channel_id=1, source_target_pairs={{0,1},{1,0},{2,3},{3,2},{4,5},{5,4},{6,7},{7,6},{8,9},{9,8},{10,11... | collective-permute-start | bytes 221192 | tf_op jit(solution)/shard_map/ppermute | solution.py:901
  69.9 7.3 %collective-permute-start.38 = (bf16[288,128]{1,0:T(8,128)(2,1)S(1)}, bf16[288,128]{1,0:T(8,128)(2,1)S(1)}, u32[]{:S(2)}, u32[]{:S(2)}) collective-permute-start(bf16[288,128]{1,0:T(8,128)(2,1)S(1)} %add_convert_fusion.4.refs_0_), channel_id=1, source_target_pairs={{0,4},{4,0},{8,12},{12,8},{16,20},{20,16},{24,28},{28,24},{1,5},{5... | collective-permute-start | bytes 221192 | tf_op jit(solution)/shard_map/ppermute | solution.py:901
  72.2 5.0 %collective-permute-start.39 = (bf16[288,128]{1,0:T(8,128)(2,1)S(1)}, bf16[288,128]{1,0:T(8,128)(2,1)S(1)}, u32[]{:S(2)}, u32[]{:S(2)}) collective-permute-start(bf16[288,128]{1,0:T(8,128)(2,1)S(1)} %add_convert_fusion.4.refs_0_), channel_id=1, source_target_pairs={{0,5},{1,4},{2,7},{3,6},{4,1},{5,0},{6,3},{7,2},{8,13},{9,12},{10,... | collective-permute-start | bytes 221192 | tf_op jit(solution)/shard_map/ppermute | solution.py:906
  75.7 1.4 %copy-start.10 = (f32[5,256]{1,0:T(8,128)S(1)}, f32[5,256]{1,0:T(8,128)}, u32[]{:S(2)}) copy-start(f32[5,256]{1,0:T(8,128)} %refs_8_.1) | copy-start | bytes 15364
  75.8 1.4 %copy-start.12 = (f32[5,256]{1,0:T(8,128)S(1)}, f32[5,256]{1,0:T(8,128)}, u32[]{:S(2)}) copy-start(f32[5,256]{1,0:T(8,128)} %refs_9_.1) | copy-start | bytes 15364
  75.8 1.4 %copy-start.14 = (s32[16]{0:T(128)S(1)}, s32[16]{0:T(128)}, u32[]{:S(2)}) copy-start(s32[16]{0:T(128)} %categories.1) | copy-start | bytes 196
  75.8 1.4 %copy-start.16 = (f32[5]{0:T(128)S(1)}, f32[5]{0:T(128)}, u32[]{:S(2)}) copy-start(f32[5]{0:T(128)} %momentum.1) | copy-start | bytes 64
  77.2 2.4 %copy-start.8 = (bf16[2,256]{1,0:T(2,128)(2,1)S(1)}, bf16[2,256]{1,0:T(2,128)(2,1)}, u32[]{:S(2)}) copy-start(bf16[2,256]{1,0:T(2,128)(2,1)} %refs_5_.1) | copy-start | bytes 3076

commit v5 on v4

--- a/solution.py
+++ b/solution.py
@@ -172,6 +172,10 @@
             dst[pl.ds(start, 16), :] = jnp.where(iota((16, 1), 0) < over, old, new)
             rest = pl.ds(pl.multiple_of(start + 16, 16), BLOCK)
             dst[rest, :] = moved[pl.ds(pl.multiple_of(at + 16, 16), BLOCK), :]
+        end = bounds[1, (groups[n] + 1) * blocks - 1]
+        dst, start = put(n, (end + 15) // 16 * 16)
+        size = ALIGN if n + 1 < len(groups) else PART * TILE
+        dst[pl.ds(start, size), :] = jnp.zeros((size, dst.shape[1]), bf16)
 
 
 def unsort_rows(bounds, row_ref, groups, blocks, pick, moved, emit):
@@ -332,7 +336,6 @@
         f.start()
 
     gw_ref[...] = jnp.zeros(gw_ref.shape, f32)
-    buf[...] = jnp.zeros(buf.shape, bf16)
     sort_rows(bounds, row_ref, x_ref, [0, 1], blocks, moved,
               lambda n, first: (buf, pl.multiple_of(first + n * cut[0], 16)))
     labels = labels_ref[...]
@@ -357,7 +360,7 @@
         out_specs=specs("vvvvvvvvvvv"),
         out_shape=[
             pltpu.VMEM((width + 16, outs), f32),
-            pltpu.VMEM((2 * cap + BLOCK + WIN, width), bf16),
+            pltpu.VMEM((2 * cap + PART * TILE, width), bf16),
             pltpu.VMEM((width, outs), bf16),
             pltpu.VMEM((outs, width), bf16),
             pltpu.VMEM((ins, outs), bf16),

time: 81.6 us -> 82 us (level); the launches traced: 80.5 us -> 82.4 us
  starting transfers between devices: 16.2 us -> 28.9 us
  Pallas kernels: 42.9 us -> 33.5 us
  waiting for transfers between devices: 19.4 us -> 18.1 us
    ppermute x17, starting transfers between devices: 15.8 us -> 26.4 us  [swap(): return lax.ppermute(v, axis, [(i, i ^ k) for i in range(n)])]
    pallas_call x1, Pallas kernels: 12 us -> 6.23 us  [local(): pl.pallas_call(functools.partial(local_kernel, 'oct', far, blocks, span,...]
    pallas_call x4, Pallas kernels: 12.8 us -> 9.3 us  [far_step(): pl.pallas_call(functools.partial(far_kernel, message, before, after_it, e...]
    ppermute x2, starting transfers between devices: 0.43 us -> 2.56 us  [swap_both(): return lax.ppermute(v, ('shape', 'oct'), [(i, i ^ k) for i in range(n * m)])]
  transfers between devices with their start and end apart: 19 -> 19, of which waited for: 9 -> 8; matrix products, arithmetic and copies ran while one was open for 0% -> 0% of each run, Pallas kernels for 47% -> 34%
where the time goes in v5:
time: 82 us; the launch traced here: 82.4 us
  Pallas kernels  33.5 us (41%)
  starting transfers between devices  28.9 us (35%)
  waiting for transfers between devices  18.1 us (22%)
  between operations  1.11 us (1%)
    ppermute x17, starting transfers between devices, swap(): return lax.ppermute(v, axis, [(i, i ^ k) for i in range(n)])  26.4 us
    ppermute x17, waiting for transfers between devices, swap(): return lax.ppermute(v, axis, [(i, i ^ k) for i in range(n)])  16.7 us
    pallas_call x4, Pallas kernels, far_step(): pl.pallas_call(functools.partial(far_kernel, message, before, after_it, e...  9.3 us
    pallas_call x1, Pallas kernels, local(): pl.pallas_call(functools.partial(local_kernel, 'oct', far, blocks, span,...  6.23 us
    pallas_call x1, Pallas kernels, prepare(): pl.pallas_call(functools.partial(prepare_kernel, oct_count, 'oct', codes....  3.59 us
    pallas_call x1, Pallas kernels, unpack(): pl.pallas_call(functools.partial(unpack_kernel, far, blocks, lasts), in_s...  3.46 us
    pallas_call x1, Pallas kernels, pack(): pl.pallas_call(functools.partial(pack_kernel, oct_count, sizes, 'shape',...  3.09 us
    ppermute x2, starting transfers between devices, swap_both(): return lax.ppermute(v, ('shape', 'oct'), [(i, i ^ k) for i in range(n * m)])  2.56 us
  transfers between devices with their start and end apart: 19, of which 8 were waited for; matrix products, arithmetic and copies ran while one was open for 0% of the time, Pallas kernels for 34%

profile of v5, /device:TPU:0, one launch (start us, length us, event | category | flops | bytes accessed | tf_op | source)
XLA Modules:
  0.0 82.4 jit_solution(9395118649380939902)
XLA Ops:
  0.6 0.0 copy-start.6
  0.6 3.1 %pack.3 = (bf16[2048,512]{1,0:T(8,128)(2,1)S(1)}, bf16[2048,512]{1,0:T(8,128)(2,1)S(1)}, bf16[4096,256]{1,0:T(8,128)(2,1)S(1)}, bf16[1040,256]{1,0:T(8,128)(2,1)...) custom-call(s32[32,128]{1,0:T(8,128)} %bitcast.13, ...), custom_call_target="tpu_custom_call" | custom-call | flops 30000001024 | bytes 1 | tf_op jit(solution)/shard_map/pack/pallas_call | solution.py:284
  3.7 0.5 collective-permute-start.22
  4.3 2.6 %collective-permute-start.21 = (bf16[1040,256]{1,0:T(8,128)(2,1)S(1)}, bf16[1040,256]{1,0:T(8,128)(2,1)S(1)}, u32[]{:S(2)}, u32[]{:S(2)}) collective-permute-start(bf16[1040,256]{1,0:T(8,128)(2,1)S(1)} %get-tuple-element.277), channel_id=1, source_target_pairs={{0,2},{1,3},{2,0},{3,1},{4,6},{5,7},{6,4},{7,5},{8,10},{9,11},{10,... | collective-permute-start | bytes 1597448 | tf_op jit(solution)/shard_map/ppermute | solution.py:904
  6.8 0.2 collective-permute-start.24
  7.0 0.3 collective-permute-start.23
  7.3 3.6 %prepare.3 = (f32[272,512]{1,0:T(8,128)S(1)}, bf16[5120,256]{1,0:T(8,128)(2,1)S(1)}, bf16[256,512]{1,0:T(8,128)(2,1)S(1)}, bf16[512,256]{1,0:T(8,128)(2,1)S(1)},...) custom-call(s32[8,128]{1,0:T(8,128)S(1)} %get-tuple-element.276.boun, ...), custom_call_target="tpu_custom_call" | custom-call | flops 30000001024 | bytes 1 | tf_op jit(solution)/shard_map/prepare/pallas_call | solution.py:357
  10.9 0.0 collective-permute-done.22.refs_2_
  10.9 6.2 %local.3 = (bf16[8192,512]{1,0:T(8,128)(2,1)}, bf16[2048,512]{1,0:T(8,128)(2,1)}, bf16[2048,512]{1,0:T(8,128)(2,1)}, f32[272,512]{1,0:T(8,128)S(1)}, bf16[5120,256]{1,0:T(8,128)(2,1)S(1)}) custom-call(s32[8,128]{1,0:T(8,128)S(1)} %get-tuple-element.276.bounds.mine.refs_0_, ...), custom_call_target="tpu_custom_call", output_to_operand_aliasing={{3}: (7, {}), {4}: (8, {})} | custom-call | flops 30000001024 | bytes 1 | tf_op jit(solution)/shard_map/local/pallas_call | solution.py:519
  17.1 2.7 %collective-permute-done.21.refs_1_ = bf16[1040,256]{1,0:T(8,128)(2,1)S(1)} collective-permute-done((bf16[1040,256]{1,0:T(8,128)(2,1)S(1)}, bf16[1040,256]{1,0:T(8,128)(2,1)S(1)}, u32[]{:S(2)}, u32[]{:S(2)}) %collective-permute-start.21) | collective-permute-done | bytes 532512 | tf_op jit(solution)/shard_map/ppermute | solution.py:904
  19.8 0.0 collective-permute-start.27
  19.8 0.9 %names.3 = (s32[16,256]{1,0:T(8,128)S(1)}, s32[8,128]{1,0:T(8,128)S(1)}, bf16[4608,256]{1,0:T(8,128)(2,1)S(1)}) custom-call(bf16[16,256]{1,0:T(8,128)(2,1)S(1)} %slice.6.labels_ref), custom_call_target="tpu_custom_call" | custom-call | flops 30000001024 | bytes 1 | tf_op jit(solution)/shard_map/names/pallas_call | solution.py:580
  20.7 0.0 collective-permute-done.24.refs_3_
  20.7 4.1 %far.12 = (bf16[8192,256]{1,0:T(8,128)(2,1)S(1)}, bf16[8192,512]{1,0:T(8,128)(2,1)}, bf16[2048,512]{1,0:T(8,128)(2,1)}, f32[272,512]{1,0:T(8,128)S(1)}, bf16[460...) custom-call(s32[8,128]{1,0:T(8,128)S(1)} %get-tuple-element.276.boun, ...), custom_call_target="tpu_custom_call", output_to_operand_aliasing={{0}: (9, {}), {1}: (10, {}), {2}: (11, {}), {3}: (12, {}), ... | custom-call | flops 30000001024 | bytes 1 | tf_op jit(solution)/shard_map/far/pallas_call | solution.py:676
  24.9 4.0 %collective-permute-start.26 = (bf16[768,256]{1,0:T(8,128)(2,1)S(1)}, bf16[768,256]{1,0:T(8,128)(2,1)S(1)}, u32[]{:S(2)}, u32[]{:S(2)}) collective-permute-start(bf16[768,256]{1,0:T(8,128)(2,1)S(1)} %get-tuple-element.307), channel_id=1, source_target_pairs={{0,2},{1,3},{2,0},{3,1},{4,6},{5,7},{6,4},{7,5},{8,10},{9,11},{10,... | collective-permute-start | bytes 1179656 | tf_op jit(solution)/shard_map/ppermute | solution.py:904
  28.9 2.1 %collective-permute-done.23.refs_1_ = bf16[1024,256]{1,0:T(8,128)(2,1)S(1)} collective-permute-done((bf16[1024,256]{1,0:T(8,128)(2,1)S(1)}, bf16[1024,256]{1,0:T(8,128)(2,1)S(1)}, u32[]{:S(2)}, u32[]{:S(2)}) %collective-permute-start.23) | collective-permute-done | bytes 524320 | tf_op jit(solution)/shard_map/ppermute | solution.py:904
  31.0 2.4 %far.13 = (bf16[8192,256]{1,0:T(8,128)(2,1)S(1)}, bf16[8192,512]{1,0:T(8,128)(2,1)}, bf16[2048,512]{1,0:T(8,128)(2,1)}, f32[272,512]{1,0:T(8,128)S(1)}, bf16[460...) custom-call(s32[8,128]{1,0:T(8,128)S(1)} %get-tuple-element.276.boun, ...), custom_call_target="tpu_custom_call", output_to_operand_aliasing={{0}: (9, {}), {1}: (10, {}), {2}: (11, {}), {3}: (12, {}), ... | custom-call | flops 30000001024 | bytes 1 | tf_op jit(solution)/shard_map/far/pallas_call | solution.py:676
  33.4 3.0 %collective-permute-start.25 = (bf16[512,256]{1,0:T(8,128)(2,1)S(1)}, bf16[512,256]{1,0:T(8,128)(2,1)S(1)}, u32[]{:S(2)}, u32[]{:S(2)}) collective-permute-start(bf16[512,256]{1,0:T(8,128)(2,1)S(1)} %get-tuple-element.306), channel_id=1, source_target_pairs={{0,2},{1,3},{2,0},{3,1},{4,6},{5,7},{6,4},{7,5},{8,10},{9,11},{10,... | collective-permute-start | bytes 786440 | tf_op jit(solution)/shard_map/ppermute | solution.py:904
  36.4 2.3 %unlocal.3 = (bf16[4096,256]{1,0:T(8,128)(2,1)S(1)}, bf16[8192,512]{1,0:T(8,128)(2,1)}) custom-call(s32[8,128]{1,0:T(8,128)S(1)} %get-tuple-element.276.bounds.mine.refs_0_, s32[16,256]{1,0:T(8,128)S(1)} %get-tuple-element.278.row_ref, bf16[5120,256]{1,0:T(8,128)(2,1)S(1)} %get-tuple-element.311.gbuf, ...), custom_call_target="tpu_custom_call", output_to_operand_aliasing={{1}: (4, {})} | custom-call | flops 10000000 | bytes 1 | tf_op jit(solution)/shard_map/unlocal/pallas_call | solution.py:555
  38.7 0.7 collective-permute-done.26.refs_1_
  39.4 1.7 %far.14 = (bf16[8192,256]{1,0:T(8,128)(2,1)S(1)}, bf16[8192,512]{1,0:T(8,128)(2,1)}, bf16[2048,512]{1,0:T(8,128)(2,1)}, f32[272,512]{1,0:T(8,128)S(1)}, bf16[460...) custom-call(s32[8,128]{1,0:T(8,128)S(1)} %get-tuple-element.276.boun, ...), custom_call_target="tpu_custom_call", output_to_operand_aliasing={{0}: (9, {}), {1}: (10, {}), {2}: (11, {}), {3}: (12, {}), ... | custom-call | flops 30000001024 | bytes 1 | tf_op jit(solution)/shard_map/far/pallas_call | solution.py:676
  41.2 3.8 %collective-permute-start.32 = (bf16[1024,256]{1,0:T(8,128)(2,1)S(1)}, bf16[1024,256]{1,0:T(8,128)(2,1)S(1)}, u32[]{:S(2)}, u32[]{:S(2)}) collective-permute-start(bf16[1024,256]{1,0:T(8,128)(2,1)S(1)} %get-tuple-element.337), channel_id=1, source_target_pairs={{0,2},{1,3},{2,0},{3,1},{4,6},{5,7},{6,4},{7,5},{8,10},{9,11},{10,... | collective-permute-start | bytes 1572872 | tf_op jit(solution)/shard_map/ppermute | solution.py:904
  45.0 1.0 %far.15 = (bf16[8192,256]{1,0:T(8,128)(2,1)S(1)}, bf16[8192,512]{1,0:T(8,128)(2,1)}, bf16[2048,512]{1,0:T(8,128)(2,1)}, f32[272,512]{1,0:T(8,128)S(1)}, bf16[460...) custom-call(s32[8,128]{1,0:T(8,128)S(1)} %get-tuple-element.276.boun, ...), custom_call_target="tpu_custom_call", output_to_operand_aliasing={{0}: (9, {}), {1}: (10, {}), {2}: (11, {}), {3}: (12, {}), ... | custom-call | flops 10000000 | bytes 1 | tf_op jit(solution)/shard_map/far/pallas_call | solution.py:676
  46.0 0.9 %collect.3 = (bf16[288,128]{1,0:T(8,128)(2,1)S(1)}, bf16[288,128]{1,0:T(8,128)(2,1)S(1)}, bf16[288,128]{1,0:T(8,128)(2,1)S(1)}, bf16[288,128]{1,0:T(8,128)(2,1)S...) custom-call(s32[8,128]{1,0:T(8,128)S(1)} %get-tuple-element.276.bounds.mi, ...), custom_call_target="tpu_custom_call", output_to_operand_aliasing={{4}: (6, {}), {5}: (7, {})} | custom-call | flops 10000000 | bytes 1 | tf_op jit(solution)/shard_map/collect/pallas_call | solution.py:943
  46.9 0.8 collective-permute-start.30
  47.7 1.7 %collective-permute-start.28 = (bf16[288,128]{1,0:T(8,128)(2,1)S(1)}, bf16[288,128]{1,0:T(8,128)(2,1)S(1)}, u32[]{:S(2)}, u32[]{:S(2)}) collective-permute-start(bf16[288,128]{1,0:T(8,128)(2,1)S(1)} %get-tuple-element.334), channel_id=1, source_target_pairs={{0,1},{1,0},{2,3},{3,2},{4,5},{5,4},{6,7},{7,6},{8,9},{9,8},{10,11... | collective-permute-start | bytes 221192 | tf_op jit(solution)/shard_map/ppermute | solution.py:904
  49.3 0.0 collective-permute-start.29
  49.4 1.4 %collective-permute-done.30 = bf16[288,128]{1,0:T(8,128)(2,1)S(1)} collective-permute-done((bf16[288,128]{1,0:T(8,128)(2,1)S(1)}, bf16[288,128]{1,0:T(8,128)(2,1)S(1)}, u32[]{:S(2)}, u32[]{:S(2)}) %collective-permute-start.30) | collective-permute-done | bytes 73760 | tf_op jit(solution)/shard_map/ppermute | solution.py:909
  50.7 3.0 %collective-permute-done.29 = bf16[288,128]{1,0:T(8,128)(2,1)S(1)} collective-permute-done((bf16[288,128]{1,0:T(8,128)(2,1)S(1)}, bf16[288,128]{1,0:T(8,128)(2,1)S(1)}, u32[]{:S(2)}, u32[]{:S(2)}) %collective-permute-start.29) | collective-permute-done | bytes 73760 | tf_op jit(solution)/shard_map/ppermute | solution.py:904
  53.7 1.7 %collective-permute-start.31 = (bf16[288,128]{1,0:T(8,128)(2,1)S(1)}, bf16[288,128]{1,0:T(8,128)(2,1)S(1)}, u32[]{:S(2)}, u32[]{:S(2)}) collective-permute-start(bf16[288,128]{1,0:T(8,128)(2,1)S(1)} %add_convert_fusion.7), channel_id=1, source_target_pairs={{0,8},{4,12},{8,0},{12,4},{16,24},{20,28},{24,16},{28,20},{1,9},{5... | collective-permute-start | bytes 221192 | tf_op jit(solution)/shard_map/ppermute | solution.py:904
  55.4 3.1 %collective-permute-start.35 = (bf16[1024,256]{1,0:T(8,128)(2,1)S(1)}, bf16[1024,256]{1,0:T(8,128)(2,1)S(1)}, u32[]{:S(2)}, u32[]{:S(2)}) collective-permute-start(bf16[1024,256]{1,0:T(8,128)(2,1)S(1)} %get-tuple-element.339), channel_id=1, source_target_pairs={{0,2},{1,3},{2,0},{3,1},{4,6},{5,7},{6,4},{7,5},{8,10},{9,11},{10,... | collective-permute-start | bytes 1572872 | tf_op jit(solution)/shard_map/ppermute | solution.py:904
  58.6 2.4 %collective-permute-start.33 = (bf16[288,128]{1,0:T(8,128)(2,1)S(1)}, bf16[288,128]{1,0:T(8,128)(2,1)S(1)}, u32[]{:S(2)}, u32[]{:S(2)}) collective-permute-start(bf16[288,128]{1,0:T(8,128)(2,1)S(1)} %add_convert_fusion.6), channel_id=1, source_target_pairs={{0,16},{4,20},{8,24},{12,28},{16,0},{20,4},{24,8},{28,12},{1,17},{... | collective-permute-start | bytes 221192 | tf_op jit(solution)/shard_map/ppermute | solution.py:904
  61.0 4.0 %collective-permute-done.33 = bf16[288,128]{1,0:T(8,128)(2,1)S(1)} collective-permute-done((bf16[288,128]{1,0:T(8,128)(2,1)S(1)}, bf16[288,128]{1,0:T(8,128)(2,1)S(1)}, u32[]{:S(2)}, u32[]{:S(2)}) %collective-permute-start.33) | collective-permute-done | bytes 73760 | tf_op jit(solution)/shard_map/ppermute | solution.py:904
  65.1 3.0 %collective-permute-start.34 = (bf16[288,128]{1,0:T(8,128)(2,1)S(1)}, bf16[288,128]{1,0:T(8,128)(2,1)S(1)}, u32[]{:S(2)}, u32[]{:S(2)}) collective-permute-start(bf16[288,128]{1,0:T(8,128)(2,1)S(1)} %add_convert_fusion.5), channel_id=1, source_target_pairs={{0,2},{1,3},{2,0},{3,1},{4,6},{5,7},{6,4},{7,5},{8,10},{9,11},{10,... | collective-permute-start | bytes 221192 | tf_op jit(solution)/shard_map/ppermute | solution.py:904
  68.0 3.2 %collective-permute-done.35.refs_3_ = bf16[1024,256]{1,0:T(8,128)(2,1)S(1)} collective-permute-done((bf16[1024,256]{1,0:T(8,128)(2,1)S(1)}, bf16[1024,256]{1,0:T(8,128)(2,1)S(1)}, u32[]{:S(2)}, u32[]{:S(2)}) %collective-permute-start.35) | collective-permute-done | bytes 524320 | tf_op jit(solution)/shard_map/ppermute | solution.py:904
  71.3 1.0 %collective-permute-done.34 = bf16[288,128]{1,0:T(8,128)(2,1)S(1)} collective-permute-done((bf16[288,128]{1,0:T(8,128)(2,1)S(1)}, bf16[288,128]{1,0:T(8,128)(2,1)S(1)}, u32[]{:S(2)}, u32[]{:S(2)}) %collective-permute-start.34) | collective-permute-done | bytes 73760 | tf_op jit(solution)/shard_map/ppermute | solution.py:904
  72.3 0.1 collective-permute-start.37
  72.4 0.1 collective-permute-start.38
  72.4 1.8 %collective-permute-start.39 = (bf16[288,128]{1,0:T(8,128)(2,1)S(1)}, bf16[288,128]{1,0:T(8,128)(2,1)S(1)}, u32[]{:S(2)}, u32[]{:S(2)}) collective-permute-start(bf16[288,128]{1,0:T(8,128)(2,1)S(1)} %add_convert_fusion.4.refs_0_), channel_id=1, source_target_pairs={{0,5},{1,4},{2,7},{3,6},{4,1},{5,0},{6,3},{7,2},{8,13},{9,12},{10,... | collective-permute-start | bytes 221192 | tf_op jit(solution)/shard_map/ppermute | solution.py:909
  74.2 3.5 %unpack.3 = (bf16[4096,256]{1,0:T(8,128)(2,1)}, bf16[4608,256]{1,0:T(8,128)(2,1)S(1)}) custom-call(s32[8,128]{1,0:T(8,128)S(1)} %get-tuple-element.276.bounds.mine.refs_0_, s32[8,128]{1,0:T(8,128)S(1)} %get-tuple-element.291.theirs.refs_1_.refs_0_, s32[16,256]{1,0:T(8,128)S(1)} %get-tuple-element.343.refs_1_, ...), custom_call_target="tpu_custom_call", output_to_operand_aliasing={{1}: (6, {})} | custom-call | flops 30000001024 | bytes 1 | tf_op jit(solution)/shard_map/unpack/pallas_call | solution.py:727
  77.7 0.0 copy-start.10
  77.7 0.0 copy-start.12
  77.7 0.0 copy-start.14
  77.7 0.0 copy-start.16
  77.8 1.3 %merge.3 = bf16[8192,512]{1,0:T(8,128)(2,1)} custom-call(bf16[2048,512]{1,0:T(8,128)(2,1)S(1)} %collective-permute-done.36.lox_ref, bf16[8192,512]{1,0:T(8,128)(2,1)} %get-tuple-element.342.lo_in), custom_call_target="tpu_custom_call", output_to_operand_aliasing={{}: (1, {})} | custom-call | flops 10000000 | bytes 1 | tf_op jit(solution)/shard_map/merge/pallas_call | solution.py:757
  79.2 0.0 copy-start.8
  79.2 2.3 %finish.3 = (f32[512,512]{1,0:T(8,128)}, f32[1,512]{1,0:T(1,128)}, f32[1,512]{1,0:T(1,128)}, f32[2,256]{1,0:T(2,128)}, f32[5,256]{1,0:T(8,128)}, /*index=5*/f32[5,256]{1,0:T(8,128)}, f32[1]{0:T(128)}) custom-call(s32[16]{0:T(128)S(1)} %copy-done.14, f32[5]{0:T(128)S(1)} %copy-done.16, bf16[288,128]{1,0:T(8,128)(2,1)S(1)} %add_convert_fusion.4.refs_0_, ...), custom_call_target="tpu_custom_call" | custom-call | flops 30000001024 | bytes 1 | tf_op jit(solution)/shard_map/finish/pallas_call | solution.py:882
  81.5 0.7 while.23
  (23 shorter events, 0.2 us)
Async XLA Ops:
  0.6 6.6 %copy-start.6 = (bf16[2,256]{1,0:T(2,128)(2,1)S(1)}, bf16[2,256]{1,0:T(2,128)(2,1)}, u32[]{:S(2)}) copy-start(bf16[2,256]{1,0:T(2,128)(2,1)} %refs_5_.1) | copy-start | bytes 3076
  3.7 7.1 %collective-permute-start.22 = (bf16[2048,512]{1,0:T(8,128)(2,1)S(1)}, bf16[2048,512]{1,0:T(8,128)(2,1)S(1)}, u32[]{:S(2)}, u32[]{:S(2)}) collective-permute-start(bf16[2048,512]{1,0:T(8,128)(2,1)S(1)} %get-tuple-element.283), channel_id=1, source_target_pairs={{0,1},{1,0},{2,3},{3,2},{4,5},{5,4},{6,7},{7,6},{8,9},{9,8},{10,11... | collective-permute-start | bytes 6291464 | tf_op jit(solution)/shard_map/ppermute | solution.py:904
  4.3 15.5 %collective-permute-start.21 = (bf16[1040,256]{1,0:T(8,128)(2,1)S(1)}, bf16[1040,256]{1,0:T(8,128)(2,1)S(1)}, u32[]{:S(2)}, u32[]{:S(2)}) collective-permute-start(bf16[1040,256]{1,0:T(8,128)(2,1)S(1)} %get-tuple-element.277), channel_id=1, source_target_pairs={{0,2},{1,3},{2,0},{3,1},{4,6},{5,7},{6,4},{7,5},{8,10},{9,11},{10,... | collective-permute-start | bytes 1597448 | tf_op jit(solution)/shard_map/ppermute | solution.py:904
  6.8 13.9 %collective-permute-start.24 = (bf16[2048,512]{1,0:T(8,128)(2,1)S(1)}, bf16[2048,512]{1,0:T(8,128)(2,1)S(1)}, u32[]{:S(2)}, u32[]{:S(2)}) collective-permute-start(bf16[2048,512]{1,0:T(8,128)(2,1)S(1)} %get-tuple-element.294), channel_id=1, source_target_pairs={{0,1},{1,0},{2,3},{3,2},{4,5},{5,4},{6,7},{7,6},{8,9},{9,8},{10,11... | collective-permute-start | bytes 6291464 | tf_op jit(solution)/shard_map/ppermute | solution.py:904
  7.0 24.0 %collective-permute-start.23 = (bf16[1024,256]{1,0:T(8,128)(2,1)S(1)}, bf16[1024,256]{1,0:T(8,128)(2,1)S(1)}, u32[]{:S(2)}, u32[]{:S(2)}) collective-permute-start(bf16[1024,256]{1,0:T(8,128)(2,1)S(1)} %get-tuple-element.293), channel_id=1, source_target_pairs={{0,2},{1,3},{2,0},{3,1},{4,6},{5,7},{6,4},{7,5},{8,10},{9,11},{10,... | collective-permute-start | bytes 1572872 | tf_op jit(solution)/shard_map/ppermute | solution.py:904
  19.8 16.7 %collective-permute-start.27 = (bf16[2048,512]{1,0:T(8,128)(2,1)}, bf16[2048,512]{1,0:T(8,128)(2,1)S(1)}, u32[]{:S(2)}, u32[]{:S(2)}) collective-permute-start(bf16[2048,512]{1,0:T(8,128)(2,1)} %get-tuple-element.312), channel_id=1, source_target_pairs={{0,1},{1,0},{2,3},{3,2},{4,5},{5,4},{6,7},{7,6},{8,9},{9,8},{10,11... | collective-permute-start | bytes 6291464 | tf_op jit(solution)/shard_map/ppermute | solution.py:904
  24.9 14.6 %collective-permute-start.26 = (bf16[768,256]{1,0:T(8,128)(2,1)S(1)}, bf16[768,256]{1,0:T(8,128)(2,1)S(1)}, u32[]{:S(2)}, u32[]{:S(2)}) collective-permute-start(bf16[768,256]{1,0:T(8,128)(2,1)S(1)} %get-tuple-element.307), channel_id=1, source_target_pairs={{0,2},{1,3},{2,0},{3,1},{4,6},{5,7},{6,4},{7,5},{8,10},{9,11},{10,... | collective-permute-start | bytes 1179656 | tf_op jit(solution)/shard_map/ppermute | solution.py:904
  33.4 11.5 %collective-permute-start.25 = (bf16[512,256]{1,0:T(8,128)(2,1)S(1)}, bf16[512,256]{1,0:T(8,128)(2,1)S(1)}, u32[]{:S(2)}, u32[]{:S(2)}) collective-permute-start(bf16[512,256]{1,0:T(8,128)(2,1)S(1)} %get-tuple-element.306), channel_id=1, source_target_pairs={{0,2},{1,3},{2,0},{3,1},{4,6},{5,7},{6,4},{7,5},{8,10},{9,11},{10,... | collective-permute-start | bytes 786440 | tf_op jit(solution)/shard_map/ppermute | solution.py:904
  41.2 17.4 %collective-permute-start.32 = (bf16[1024,256]{1,0:T(8,128)(2,1)S(1)}, bf16[1024,256]{1,0:T(8,128)(2,1)S(1)}, u32[]{:S(2)}, u32[]{:S(2)}) collective-permute-start(bf16[1024,256]{1,0:T(8,128)(2,1)S(1)} %get-tuple-element.337), channel_id=1, source_target_pairs={{0,2},{1,3},{2,0},{3,1},{4,6},{5,7},{6,4},{7,5},{8,10},{9,11},{10,... | collective-permute-start | bytes 1572872 | tf_op jit(solution)/shard_map/ppermute | solution.py:904
  45.0 1.0 %copy-start.7 = (bf16[2,256]{1,0:T(2,128)(2,1)S(1)}, bf16[2,256]{1,0:T(2,128)(2,1)}, u32[]{:S(2)}) copy-start(bf16[2,256]{1,0:T(2,128)(2,1)} %refs_5_.1) | copy-start | bytes 3076
  46.9 3.8 %collective-permute-start.30 = (bf16[288,128]{1,0:T(8,128)(2,1)S(1)}, bf16[288,128]{1,0:T(8,128)(2,1)S(1)}, u32[]{:S(2)}, u32[]{:S(2)}) collective-permute-start(bf16[288,128]{1,0:T(8,128)(2,1)S(1)} %get-tuple-element.336), channel_id=1, source_target_pairs={{0,5},{1,4},{2,7},{3,6},{4,1},{5,0},{6,3},{7,2},{8,13},{9,12},{10,... | collective-permute-start | bytes 221192 | tf_op jit(solution)/shard_map/ppermute | solution.py:909
  47.7 3.1 %collective-permute-start.28 = (bf16[288,128]{1,0:T(8,128)(2,1)S(1)}, bf16[288,128]{1,0:T(8,128)(2,1)S(1)}, u32[]{:S(2)}, u32[]{:S(2)}) collective-permute-start(bf16[288,128]{1,0:T(8,128)(2,1)S(1)} %get-tuple-element.334), channel_id=1, source_target_pairs={{0,1},{1,0},{2,3},{3,2},{4,5},{5,4},{6,7},{7,6},{8,9},{9,8},{10,11... | collective-permute-start | bytes 221192 | tf_op jit(solution)/shard_map/ppermute | solution.py:904
  49.3 4.4 %collective-permute-start.29 = (bf16[288,128]{1,0:T(8,128)(2,1)S(1)}, bf16[288,128]{1,0:T(8,128)(2,1)S(1)}, u32[]{:S(2)}, u32[]{:S(2)}) collective-permute-start(bf16[288,128]{1,0:T(8,128)(2,1)S(1)} %get-tuple-element.335), channel_id=1, source_target_pairs={{0,4},{4,0},{8,12},{12,8},{16,20},{20,16},{24,28},{28,24},{1,5},{5... | collective-permute-start | bytes 221192 | tf_op jit(solution)/shard_map/ppermute | solution.py:904
  53.7 4.8 %collective-permute-start.31 = (bf16[288,128]{1,0:T(8,128)(2,1)S(1)}, bf16[288,128]{1,0:T(8,128)(2,1)S(1)}, u32[]{:S(2)}, u32[]{:S(2)}) collective-permute-start(bf16[288,128]{1,0:T(8,128)(2,1)S(1)} %add_convert_fusion.7), channel_id=1, source_target_pairs={{0,8},{4,12},{8,0},{12,4},{16,24},{20,28},{24,16},{28,20},{1,9},{5... | collective-permute-start | bytes 221192 | tf_op jit(solution)/shard_map/ppermute | solution.py:904
  55.4 15.9 %collective-permute-start.35 = (bf16[1024,256]{1,0:T(8,128)(2,1)S(1)}, bf16[1024,256]{1,0:T(8,128)(2,1)S(1)}, u32[]{:S(2)}, u32[]{:S(2)}) collective-permute-start(bf16[1024,256]{1,0:T(8,128)(2,1)S(1)} %get-tuple-element.339), channel_id=1, source_target_pairs={{0,2},{1,3},{2,0},{3,1},{4,6},{5,7},{6,4},{7,5},{8,10},{9,11},{10,... | collective-permute-start | bytes 1572872 | tf_op jit(solution)/shard_map/ppermute | solution.py:904
  58.6 6.4 %collective-permute-start.33 = (bf16[288,128]{1,0:T(8,128)(2,1)S(1)}, bf16[288,128]{1,0:T(8,128)(2,1)S(1)}, u32[]{:S(2)}, u32[]{:S(2)}) collective-permute-start(bf16[288,128]{1,0:T(8,128)(2,1)S(1)} %add_convert_fusion.6), channel_id=1, source_target_pairs={{0,16},{4,20},{8,24},{12,28},{16,0},{20,4},{24,8},{28,12},{1,17},{... | collective-permute-start | bytes 221192 | tf_op jit(solution)/shard_map/ppermute | solution.py:904
  65.1 7.2 %collective-permute-start.34 = (bf16[288,128]{1,0:T(8,128)(2,1)S(1)}, bf16[288,128]{1,0:T(8,128)(2,1)S(1)}, u32[]{:S(2)}, u32[]{:S(2)}) collective-permute-start(bf16[288,128]{1,0:T(8,128)(2,1)S(1)} %add_convert_fusion.5), channel_id=1, source_target_pairs={{0,2},{1,3},{2,0},{3,1},{4,6},{5,7},{6,4},{7,5},{8,10},{9,11},{10,... | collective-permute-start | bytes 221192 | tf_op jit(solution)/shard_map/ppermute | solution.py:904
  68.0 9.7 %collective-permute-start.36 = (bf16[2048,512]{1,0:T(8,128)(2,1)}, bf16[2048,512]{1,0:T(8,128)(2,1)S(1)}, u32[]{:S(2)}, u32[]{:S(2)}) collective-permute-start(bf16[2048,512]{1,0:T(8,128)(2,1)} %get-tuple-element.341), channel_id=1, source_target_pairs={{0,1},{1,0},{2,3},{3,2},{4,5},{5,4},{6,7},{7,6},{8,9},{9,8},{10,11... | collective-permute-start | bytes 6291464 | tf_op jit(solution)/shard_map/ppermute | solution.py:904
  72.3 6.8 %collective-permute-start.37 = (bf16[288,128]{1,0:T(8,128)(2,1)S(1)}, bf16[288,128]{1,0:T(8,128)(2,1)S(1)}, u32[]{:S(2)}, u32[]{:S(2)}) collective-permute-start(bf16[288,128]{1,0:T(8,128)(2,1)S(1)} %add_convert_fusion.4.refs_0_), channel_id=1, source_target_pairs={{0,1},{1,0},{2,3},{3,2},{4,5},{5,4},{6,7},{7,6},{8,9},{9,8},{10,11... | collective-permute-start | bytes 221192 | tf_op jit(solution)/shard_map/ppermute | solution.py:904
  72.4 6.8 %collective-permute-start.38 = (bf16[288,128]{1,0:T(8,128)(2,1)S(1)}, bf16[288,128]{1,0:T(8,128)(2,1)S(1)}, u32[]{:S(2)}, u32[]{:S(2)}) collective-permute-start(bf16[288,128]{1,0:T(8,128)(2,1)S(1)} %add_convert_fusion.4.refs_0_), channel_id=1, source_target_pairs={{0,4},{4,0},{8,12},{12,8},{16,20},{20,16},{24,28},{28,24},{1,5},{5... | collective-permute-start | bytes 221192 | tf_op jit(solution)/shard_map/ppermute | solution.py:904
  72.4 6.7 %collective-permute-start.39 = (bf16[288,128]{1,0:T(8,128)(2,1)S(1)}, bf16[288,128]{1,0:T(8,128)(2,1)S(1)}, u32[]{:S(2)}, u32[]{:S(2)}) collective-permute-start(bf16[288,128]{1,0:T(8,128)(2,1)S(1)} %add_convert_fusion.4.refs_0_), channel_id=1, source_target_pairs={{0,5},{1,4},{2,7},{3,6},{4,1},{5,0},{6,3},{7,2},{8,13},{9,12},{10,... | collective-permute-start | bytes 221192 | tf_op jit(solution)/shard_map/ppermute | solution.py:909
  77.7 1.4 %copy-start.10 = (f32[5,256]{1,0:T(8,128)S(1)}, f32[5,256]{1,0:T(8,128)}, u32[]{:S(2)}) copy-start(f32[5,256]{1,0:T(8,128)} %refs_8_.1) | copy-start | bytes 15364
  77.7 1.4 %copy-start.12 = (f32[5,256]{1,0:T(8,128)S(1)}, f32[5,256]{1,0:T(8,128)}, u32[]{:S(2)}) copy-start(f32[5,256]{1,0:T(8,128)} %refs_9_.1) | copy-start | bytes 15364
  77.7 1.4 %copy-start.14 = (s32[16]{0:T(128)S(1)}, s32[16]{0:T(128)}, u32[]{:S(2)}) copy-start(s32[16]{0:T(128)} %categories.1) | copy-start | bytes 196
  77.7 1.4 %copy-start.16 = (f32[5]{0:T(128)S(1)}, f32[5]{0:T(128)}, u32[]{:S(2)}) copy-start(f32[5]{0:T(128)} %momentum.1) | copy-start | bytes 64
  79.2 2.4 %copy-start.8 = (bf16[2,256]{1,0:T(2,128)(2,1)S(1)}, bf16[2,256]{1,0:T(2,128)(2,1)}, u32[]{:S(2)}) copy-start(bf16[2,256]{1,0:T(2,128)(2,1)} %refs_5_.1) | copy-start | bytes 3076
